TPU v7x, 512 devices: a whole 4x4x16 slice. The times are simulated.
512 devices in a mesh: slab: 64 (over z, x_lo, core), mode: 8 (over x_hi, y).
Axes of the slice: x: 4 (x_hi: 2, x_lo: 2; x = x_hi * 2 + x_lo), y: 4, z: 16, core: 2. Of those that a mesh axis runs over, the one named last changes fastest.
Arguments:
- initial_block: bfloat16 [96, 64, 64, 128], P('mode', 'slab'), may hold values from -180 to 180
- labels: int32 [64, 64, 128], P('slab'), may hold values from 0 to 3
- filter_low: float32 [], replicated, may hold values from 1 to 3
- filter_high: float32 [], replicated, may hold values from 22 to 24
Outputs:
- modes_out: bfloat16 [96, 64, 64, 128], P('mode', 'slab')
- projected: float32 [96, 96], replicated
Inputs may be any that keep to these rules, and one draw needn't show every extreme that they name: `labels`: 0 marks a voxel outside the brain; 1, 2 and 3 are tissue classes.
All inputs are finite; a program needn't handle non-finite values.
Results may differ from a plain program's by a relative error of at most 0.0015.
The roundings to bfloat16 on the way count: a program that leaves them out, or rounds other values in their place, can miss the bound.
Values may be sent and summed in bfloat16 or wider, within the bound.
No kernel may reach another device: no remote copies, remote signals or barrier semaphores. Data moves between devices by JAX's collectives and lax.ppermute only.
A program may use at most 64 MiB of HBM per device.

v0:
```python
import math

import jax
import jax.numpy as jnp
from jax import lax
from jax.sharding import PartitionSpec as P

DEGREE = 4


ROOTS = (0.0, 0.7745967, 1.0, 1.3416408)


def padded_2(shard, sides, width):
    for axis, dim in sides:
        peers, length = (lax.axis_size(axis), shard.shape[dim])
        up = [(i, (i + 1) % peers) for i in range(peers - 1)]
        down = [(j, i) for i, j in up]
        last = lax.slice_in_dim(shard, length - width, length, axis=dim)
        first = lax.slice_in_dim(shard, 0, width, axis=dim)
        before = lax.ppermute(last, axis, up)
        after = lax.ppermute(first, axis, down)
        shard = jnp.concatenate([before, shard, after], axis=dim)
    return shard


def strength_of(labels):
    total = jnp.zeros(labels.shape, jnp.float32)
    for level in range(1, 4):
        total = total + jnp.where(labels == level, ROOTS[level], 0.0)
    return total


def face_weights(strong, padded):
    return (
        strong * padded[:-2, 1:-1, 1:-1],
        strong * padded[2:, 1:-1, 1:-1],
        strong * padded[1:-1, :-2, 1:-1],
        strong * padded[1:-1, 2:, 1:-1],
        strong * padded[1:-1, 1:-1, :-2],
        strong * padded[1:-1, 1:-1, 2:],
    )


def combine_faces(field, padded, weights):
    beside_all = (
        padded[:, :-2, 1:-1, 1:-1],
        padded[:, 2:, 1:-1, 1:-1],
        padded[:, 1:-1, :-2, 1:-1],
        padded[:, 1:-1, 2:, 1:-1],
        padded[:, 1:-1, 1:-1, :-2],
        padded[:, 1:-1, 1:-1, 2:],
    )
    total = weights[0] * (field - beside_all[0])
    for weight, other in zip(weights[1:], beside_all[1:]):
        total = total + weight * (field - other)
    return total


def chebyshev(block, apply_fn, low, high):
    centre = 0.5 * (high + low)
    half = 0.5 * (high - low)
    prev = block
    cur = (apply_fn(block) - centre * block) / half
    for step in range(DEGREE - 1):
        nxt = 2.0 * (apply_fn(cur) - centre * cur) / half - prev
        prev, cur = (cur, nxt)
    return cur


def factor(gram, cross):
    lower = jnp.linalg.cholesky(gram)
    inverse = jax.scipy.linalg.solve_triangular(
        lower, jnp.eye(gram.shape[0], dtype=jnp.float32), lower=True
    )
    projected = jnp.dot(
        jnp.dot(inverse, cross, precision=lax.Precision.HIGHEST),
        inverse.T,
        precision=lax.Precision.HIGHEST,
    )
    return (projected, inverse.T.astype(jnp.bfloat16))


def per_device(initial_block, labels, filter_low, filter_high):
    local = initial_block.shape[0]
    modes = local * lax.axis_size("mode")
    depth, height, width = labels.shape
    scale = math.sqrt(depth * height * width * lax.axis_size("slab"))
    strong = strength_of(labels)
    mask = (labels > 0).astype(jnp.float32)
    rim = padded_2(strong, (("slab", 0),), 1)
    weights = face_weights(strong, jnp.pad(rim, ((0, 0), (1, 1), (1, 1))))

    def apply_fn(field):
        padded = padded_2(field, (("slab", 1),), 1)
        return combine_faces(field, jnp.pad(padded, ((0, 0), (0, 0), (1, 1), (1, 1))), weights)

    block = initial_block.astype(jnp.float32) * mask[None]
    cur = chebyshev(block, apply_fn, filter_low, filter_high)
    filtered = cur.astype(jnp.bfloat16)
    applied = apply_fn(cur).astype(jnp.bfloat16)
    everything = lax.all_gather(filtered, "mode", axis=0, tiled=True)
    whole = everything.reshape(modes, -1)
    own = filtered.reshape(local, -1)
    own_applied = applied.reshape(local, -1)
    gram_block = jnp.einsum("mc,nc->mn", whole, own, preferred_element_type=jnp.float32)
    cross_block = jnp.einsum("mc,nc->mn", whole, own_applied, preferred_element_type=jnp.float32)
    gram_sum, cross_sum = lax.psum((gram_block, cross_block), "slab")
    gram, cross = (
        lax.all_gather(gram_sum, "mode", axis=1, tiled=True),
        lax.all_gather(cross_sum, "mode", axis=1, tiled=True),
    )
    projected, rotation = factor(gram, cross)
    columns = lax.dynamic_slice_in_dim(rotation, lax.axis_index("mode") * local, local, 1)
    turned = jnp.einsum("mj,mc->jc", columns, whole, preferred_element_type=jnp.float32)
    modes_out = (turned * scale).astype(jnp.bfloat16).reshape(local, depth, height, width)
    return (modes_out, projected)


def solution(mesh):
    placed = (P("mode", "slab", None, None), P("slab", None, None), P(), P())
    return jax.shard_map(
        per_device,
        mesh=mesh,
        in_specs=placed,
        out_specs=(P("mode", "slab", None, None), P()),
        check_vma=False,
    )
```

profile of v0, /device:TPU:4, one launch (start us, length us, event | category | flops | bytes accessed | tf_op | source)
XLA Modules:
  0.0 454.6 jit_solution(9304281027527931800)
XLA Ops:
  7.2 0.8 convert_bitcast_fusion
  8.0 1.0 convert_multiply_fusion
  9.0 1.8 collective-permute-start.1
  10.8 1.3 collective-permute-start.3
  12.1 0.8 select_add_fusion
  12.9 4.0 collective-permute-start
  16.9 1.3 collective-permute-start.2
  19.5 1.7 collective-permute-done.2
  21.2 0.1 select_maximum_fusion.10
  21.3 0.9 multiply_bitcast_fusion.1
  22.2 0.8 select_maximum_fusion.8
  23.0 0.5 fusion.66
  23.5 4.6 %collective-permute-start.4 = (f32[12,1,64,128]{3,2,1,0:T(8,128)S(1)}, f32[12,1,64,128]{3,2,1,0:T(8,128)S(1)}, u32[]{:S(2)}, u32[]{:S(2)}) collective-permute-start(f32[12,1,64,128]{3,2,1,0:T(8,128)S(1)} %fusion.66), channel_id=1, source_target_pairs={{0,8},{8,16},{16,24},{24,32},{32,40},{40,48},{48,56},{56,64},{64,7... | collective-permute-start | bytes 1179656 | tf_op jit(solution)/shard_map/ppermute | solution.py:21
  28.1 1.3 collective-permute-start.5
  29.4 3.0 collective-permute-done.5
  32.4 0.8 select_maximum_fusion.6
  33.2 0.5 fusion.56
  33.7 9.0 %collective-permute-start.6 = (f32[12,1,64,128]{3,2,1,0:T(8,128)S(1)}, f32[12,1,64,128]{3,2,1,0:T(8,128)S(1)}, u32[]{:S(2)}, u32[]{:S(2)}) collective-permute-start(f32[12,1,64,128]{3,2,1,0:T(8,128)S(1)} %fusion.56), channel_id=1, source_target_pairs={{0,8},{8,16},{16,24},{24,32},{32,40},{40,48},{48,56},{56,64},{64,7... | collective-permute-start | bytes 1179656 | tf_op jit(solution)/shard_map/ppermute | solution.py:21
  42.7 1.3 collective-permute-start.7
  44.0 2.3 collective-permute-done.7
  46.3 0.8 select_maximum_fusion.4
  47.1 0.5 fusion.44
  47.6 8.3 %collective-permute-start.8 = (f32[12,1,64,128]{3,2,1,0:T(8,128)S(1)}, f32[12,1,64,128]{3,2,1,0:T(8,128)S(1)}, u32[]{:S(2)}, u32[]{:S(2)}) collective-permute-start(f32[12,1,64,128]{3,2,1,0:T(8,128)S(1)} %fusion.44), channel_id=1, source_target_pairs={{0,8},{8,16},{16,24},{24,32},{32,40},{40,48},{48,56},{56,64},{64,7... | collective-permute-start | bytes 1179656 | tf_op jit(solution)/shard_map/ppermute | solution.py:21
  55.9 1.3 collective-permute-start.9
  57.2 2.3 collective-permute-done.9
  59.5 0.8 select_maximum_fusion.2
  60.3 1.2 fusion.88
  61.5 8.3 %collective-permute-start.10 = (f32[12,1,64,128]{3,2,1,0:T(8,128)S(1)}, f32[12,1,64,128]{3,2,1,0:T(8,128)S(1)}, u32[]{:S(2)}, u32[]{:S(2)}) collective-permute-start(f32[12,1,64,128]{3,2,1,0:T(8,128)S(1)} %get-tuple-element.11), channel_id=1, source_target_pairs={{0,8},{8,16},{16,24},{24,32},{32,40},{40,48},{48,56},{56,64},{64,7... | collective-permute-start | bytes 1179656 | tf_op jit(solution)/shard_map/ppermute | solution.py:21
  69.8 1.3 collective-permute-start.11
  71.1 2.3 collective-permute-done.11
  73.4 0.8 select_maximum_fusion
  74.2 0.5 fusion.78
  74.7 67.0 %all-gather.4.cloned.1.call-done = bf16[96,1,64,128]{3,2,1,0:T(8,128)(2,1)} async-done(((bf16[12,1,64,128]{3,2,1,0:T(8,128)(2,1)}), bf16[96,1,64,128]{3,2,1,0:T(8,128)(2,1)}) %all-gather.4.cloned.1.call-update) | async-done | bytes 1572880 | tf_op jit(solution)/shard_map/all_gather | solution.py:102
  141.7 2.6 fusion.15
  144.3 2.4 fusion.12
  146.7 212.0 %all-reduce.6 = (f32[96,12]{0,1:T(8,128)S(1)}, f32[96,12]{0,1:T(8,128)S(1)}) all-reduce(f32[96,12]{0,1:T(8,128)S(1)} %fusion.12, f32[96,12]{0,1:T(8,128)S(1)} %fusion.15), channel_id=1, replica_groups=mesh['slab'=64,'mode'=8] {'slab'}, use_global_device_ids=true, to_apply=%region_0.1 | all-reduce | flops 2304 | bytes 18432 | tf_op jit(solution)/shard_map/psum | solution.py:108
  358.7 34.3 %all-gather = f32[8,12,96]{2,1,0:T(8,128)S(1)} all-gather(f32[1,12,96]{2,1,0:T(8,128)S(1)} %bitcast.67), channel_id=1, replica_groups=mesh['slab'=64,'mode'=8] {'mode'}, dimensions={0}, use_global_device_ids=true | all-gather | bytes 41472 | tf_op jit(solution)/shard_map/all_gather | solution.py:110
  393.0 0.1 copy.15
  393.1 8.8 %cholesky.17 = f32[96,96]{1,0:T(8,128)S(1)} custom-call(f32[96,96]{1,0:T(8,128)S(1)} %fusion.82), custom_call_target="Cholesky" | custom-call | tf_op jit(solution)/shard_map/jit(cholesky)/cholesky | solution.py:72
  401.9 0.6 compare_reduce_fusion
  402.6 0.7 fusion.79
  403.2 7.4 %custom-call.7 = f32[1,96,96]{1,2,0:T(8,128)S(1)} custom-call(f32[1,96,96]{2,1,0:T(8,128)S(1)} %fusion.79), custom_call_target="InvertDiagBlocksLowerTriangular" | custom-call | tf_op jit(solution)/shard_map/jit(_solve_triangular)/triangular_solve | solution.py:73
  410.6 0.2 fusion.80
  410.8 34.2 %all-gather.1 = f32[8,12,96]{2,1,0:T(8,128)S(1)} all-gather(f32[1,12,96]{2,1,0:T(8,128)S(1)} %bitcast.66), channel_id=1, replica_groups=mesh['slab'=64,'mode'=8] {'mode'}, dimensions={0}, use_global_device_ids=true | all-gather | bytes 41472 | tf_op jit(solution)/shard_map/all_gather | solution.py:111
  445.0 0.2 fusion.90
  445.2 0.8 fusion.91
  446.1 1.0 fusion
  447.1 0.7 bitcast_bitcast_fusion
  (20 shorter events, 0.2 us)
Async XLA Ops:
  7.2 134.5 %all-gather.4.cloned.1.call-start = ((), (), s32[]{:S(2)}) async-start(), calls=%async_computation | async-start | bytes 1769472 | tf_op jit(solution)/shard_map/all_gather | solution.py:102
  8.0 15.0 %copy-start = (bf16[12,1,64,128]{3,2,1,0:T(8,128)(2,1)S(1)}, bf16[12,1,64,128]{3,2,1,0:T(8,128)(2,1)}, u32[]{:S(2)}) copy-start(bf16[12,1,64,128]{3,2,1,0:T(8,128)(2,1)} %param.4) | copy-start | bytes 589828
  9.0 13.2 %collective-permute-start.1 = (f32[12,1,64,128]{3,2,1,0:T(8,128)S(1)}, f32[12,1,64,128]{3,2,1,0:T(8,128)S(1)}, u32[]{:S(2)}, u32[]{:S(2)}) collective-permute-start(f32[12,1,64,128]{3,2,1,0:T(8,128)S(1)} %convert_multiply_fusion), channel_id=1, source_target_pairs={{0,8},{8,16},{16,24},{24,32},{32,40},{40,48},{48,56},{56,64},{64,7... | collective-permute-start | bytes 1179656 | tf_op jit(solution)/shard_map/ppermute | solution.py:21
  10.8 11.4 %collective-permute-start.3 = (f32[12,1,64,128]{3,2,1,0:T(8,128)S(1)}, f32[12,1,64,128]{3,2,1,0:T(8,128)S(1)}, u32[]{:S(2)}, u32[]{:S(2)}) collective-permute-start(f32[12,1,64,128]{3,2,1,0:T(8,128)S(1)} %convert_multiply_fusion), channel_id=1, source_target_pairs={{8,0},{16,8},{24,16},{32,24},{40,32},{48,40},{56,48},{64,56},{72,6... | collective-permute-start | bytes 1179656 | tf_op jit(solution)/shard_map/ppermute | solution.py:22
  12.9 6.6 %collective-permute-start = (f32[1,64,128]{2,1,0:T(8,128)S(1)}, f32[1,64,128]{2,1,0:T(8,128)S(1)}, u32[]{:S(2)}, u32[]{:S(2)}) collective-permute-start(f32[1,64,128]{2,1,0:T(8,128)S(1)} %select_add_fusion), channel_id=1, source_target_pairs={{0,8},{8,16},{16,24},{24,32},{32,40},{40,48},{48,56},{56,64},{64,7... | collective-permute-start | bytes 98312 | tf_op jit(solution)/shard_map/ppermute | solution.py:21
  16.9 4.3 collective-permute-start.2
  23.5 5.9 %collective-permute-start.4 = (f32[12,1,64,128]{3,2,1,0:T(8,128)S(1)}, f32[12,1,64,128]{3,2,1,0:T(8,128)S(1)}, u32[]{:S(2)}, u32[]{:S(2)}) collective-permute-start(f32[12,1,64,128]{3,2,1,0:T(8,128)S(1)} %fusion.66), channel_id=1, source_target_pairs={{0,8},{8,16},{16,24},{24,32},{32,40},{40,48},{48,56},{56,64},{64,7... | collective-permute-start | bytes 1179656 | tf_op jit(solution)/shard_map/ppermute | solution.py:21
  28.1 4.3 collective-permute-start.5
  33.7 10.3 %collective-permute-start.6 = (f32[12,1,64,128]{3,2,1,0:T(8,128)S(1)}, f32[12,1,64,128]{3,2,1,0:T(8,128)S(1)}, u32[]{:S(2)}, u32[]{:S(2)}) collective-permute-start(f32[12,1,64,128]{3,2,1,0:T(8,128)S(1)} %fusion.56), channel_id=1, source_target_pairs={{0,8},{8,16},{16,24},{24,32},{32,40},{40,48},{48,56},{56,64},{64,7... | collective-permute-start | bytes 1179656 | tf_op jit(solution)/shard_map/ppermute | solution.py:21
  42.7 3.6 collective-permute-start.7
  47.6 9.6 %collective-permute-start.8 = (f32[12,1,64,128]{3,2,1,0:T(8,128)S(1)}, f32[12,1,64,128]{3,2,1,0:T(8,128)S(1)}, u32[]{:S(2)}, u32[]{:S(2)}) collective-permute-start(f32[12,1,64,128]{3,2,1,0:T(8,128)S(1)} %fusion.44), channel_id=1, source_target_pairs={{0,8},{8,16},{16,24},{24,32},{32,40},{40,48},{48,56},{56,64},{64,7... | collective-permute-start | bytes 1179656 | tf_op jit(solution)/shard_map/ppermute | solution.py:21
  55.9 3.6 collective-permute-start.9
  61.5 9.6 %collective-permute-start.10 = (f32[12,1,64,128]{3,2,1,0:T(8,128)S(1)}, f32[12,1,64,128]{3,2,1,0:T(8,128)S(1)}, u32[]{:S(2)}, u32[]{:S(2)}) collective-permute-start(f32[12,1,64,128]{3,2,1,0:T(8,128)S(1)} %get-tuple-element.11), channel_id=1, source_target_pairs={{0,8},{8,16},{16,24},{24,32},{32,40},{40,48},{48,56},{56,64},{64,7... | collective-permute-start | bytes 1179656 | tf_op jit(solution)/shard_map/ppermute | solution.py:21
  69.8 3.6 collective-permute-start.11
  74.2 70.1 %copy-start.2 = (bf16[12,1,64,128]{3,2,1,0:T(8,128)(2,1)S(1)}, bf16[12,1,64,128]{3,2,1,0:T(8,128)(2,1)}, u32[]{:S(2)}) copy-start(bf16[12,1,64,128]{3,2,1,0:T(8,128)(2,1)} %get-tuple-element.10) | copy-start | bytes 589828
  141.7 304.4 %copy-start.1 = (bf16[96,1,64,128]{3,2,1,0:T(8,128)(2,1)S(1)}, bf16[96,1,64,128]{3,2,1,0:T(8,128)(2,1)}, u32[]{:S(2)}) copy-start(bf16[96,1,64,128]{3,2,1,0:T(8,128)(2,1)} %all-gather.4.cloned.1.call-done) | copy-start | bytes 4718596
Sparse Core Ops, SparseCore 0:
  61.6 80.0 all-gather.3
where the time goes:
time: 455 us
  blocking collectives  280 us (62%)
  waiting for transfers between devices  78.8 us (17%)
  starting transfers between devices  43.7 us (10%)
  other arithmetic  28 us (6%)
  between operations  15.6 us (3%)
  matrix products  7.25 us (2%)
    psum x1, blocking collectives, per_device(): gram_sum, cross_sum = lax.psum((gram_block, cross_block), 'slab')  212 us
    all_gather x1, waiting for transfers between devices, per_device(): everything = lax.all_gather(filtered, 'mode', axis=0, tiled=True)  67 us
    ppermute x6, starting transfers between devices, padded_2(): before = lax.ppermute(last, axis, up)  35.9 us
    all_gather x1, blocking collectives, per_device(): lax.all_gather(gram_sum, 'mode', axis=1, tiled=True)  34.3 us
    all_gather x1, blocking collectives, per_device(): lax.all_gather(cross_sum, 'mode', axis=1, tiled=True)  34.2 us
    ppermute x6, waiting for transfers between devices, padded_2(): after = lax.ppermute(first, axis, down)  11.7 us
    another operation x3, other arithmetic, factor(): lower = jnp.linalg.cholesky(gram)  9.45 us
  transfers between devices with their start and end apart: 13, of which 6 were waited for; matrix products, arithmetic and copies ran while one was open for 1% of the time, Pallas kernels for 0%

commit v1 on v0

v1 whole, which is shorter than its diff:
```python
import functools
import math

import jax
import jax.numpy as jnp
from jax import lax
from jax.experimental import pallas as pl
from jax.experimental.pallas import tpu as pltpu
from jax.sharding import Mesh, PartitionSpec as P

DEGREE = 4
ROOTS = (0.0, 0.7745967, 1.0, 1.3416408)
REACH = DEGREE + 1

AXES = ("z", "xl", "core", "xh", "y")
GROUP = ("xl", "core")
MODE = ("xh", "y")
LAYER = ("xh", "y", "xl", "core")


def filter_kernel(bounds, far_lo, lo, own, hi, far_hi, out, even, odd, weak_even, weak_odd, strong, degree):
    planes, height, width = strong.shape
    local = even.shape[1]
    rows = out.shape[3]
    low, high = bounds[0], bounds[1]
    centre = 0.5 * (high + low)
    scale = 1.0 / (0.5 * (high - low))
    row = lax.broadcasted_iota(jnp.int32, (height, width), 0)
    lane = lax.broadcasted_iota(jnp.int32, (height, width), 1)

    def beside(value):
        up = jnp.where(row == 0, 0.0, pltpu.roll(value, 1, 0))
        down = jnp.where(row == height - 1, 0.0, pltpu.roll(value, height - 1, 0))
        left = jnp.where(lane == 0, 0.0, pltpu.roll(value, 1, 1))
        right = jnp.where(lane == width - 1, 0.0, pltpu.roll(value, width - 1, 1))
        return (up + down) + (left + right)

    start = 0
    for source in (far_lo, lo, own, hi, far_hi):
        count = source.shape[0]

        def load(index, carry, source=source, start=start):
            label = source[index, local].astype(jnp.float32)
            root = jnp.where(label == 1.0, ROOTS[1], 0.0)
            root = jnp.where(label == 2.0, ROOTS[2], root)
            root = jnp.where(label == 3.0, ROOTS[3], root)
            strong[start + index] = root
            for mode in range(local):
                value = jnp.where(label > 0.0, source[index, mode].astype(jnp.float32), 0.0)
                even[start + index, mode] = value
                weak_even[start + index, mode] = root * value
            return carry

        lax.fori_loop(0, count, load, 0)
        start += count

    def weigh(plane, carry):
        root = strong[plane]
        degree[plane] = root * (strong[plane - 1] + strong[plane + 1] + beside(root))
        return carry

    lax.fori_loop(1, planes - 1, weigh, 0)

    cur, prev, weak, weak_next = even, odd, weak_even, weak_odd
    for step in range(DEGREE):
        factor = scale if step == 0 else 2.0 * scale

        def advance(plane, carry, cur=cur, prev=prev, weak=weak, weak_next=weak_next, factor=factor, step=step):
            root = strong[plane]
            here = (degree[plane] - centre) * factor
            there = root * factor
            for mode in range(local):
                around = weak[plane - 1, mode] + weak[plane + 1, mode] + beside(weak[plane, mode])
                value = here * cur[plane, mode] - there * around
                if step > 0:
                    value = value - prev[plane, mode]
                prev[plane, mode] = value
                weak_next[plane, mode] = root * value
            return carry

        lax.fori_loop(step + 1, planes - step - 1, advance, 0)
        cur, prev = prev, cur
        weak, weak_next = weak_next, weak

    def finish(index, carry):
        plane = REACH + index
        root, heavy = strong[plane], degree[plane]
        for mode in range(local):
            value = cur[plane, mode]
            around = weak[plane - 1, mode] + weak[plane + 1, mode] + beside(weak[plane, mode])
            image = heavy * value - root * around
            out[:, index, mode] = value.reshape(-1, rows, width).astype(out.dtype)
            out[:, index, local + mode] = image.reshape(-1, rows, width).astype(out.dtype)
        return carry

    lax.fori_loop(0, own.shape[0], finish, 0)


def filtered_and_applied(bounds, far_lo, lo, own, hi, far_hi, blocks):
    depth, fields, height, width = own.shape
    local = fields - 1
    planes = depth + 2 * REACH
    field = pltpu.VMEM((planes, local, height, width), jnp.float32)
    plane = pltpu.VMEM((planes, height, width), jnp.float32)
    vmem = pl.BlockSpec(memory_space=pltpu.VMEM)
    return pl.pallas_call(
        filter_kernel,
        out_shape=jax.ShapeDtypeStruct((blocks, depth, 2 * local, height // blocks, width), jnp.bfloat16),
        in_specs=[pl.BlockSpec(memory_space=pltpu.SMEM)] + [vmem] * 5,
        out_specs=vmem,
        scratch_shapes=[field, field, field, field, plane, plane],
        compiler_params=pltpu.CompilerParams(vmem_limit_bytes=40 * 1024 * 1024),
        name="chebyshev_filter",
    )(bounds, far_lo, lo, own, hi, far_hi)


def shifted(value, axis, step):
    size = lax.axis_size(axis)
    pairs = [(i, i + step) for i in range(size) if 0 <= i + step < size]
    return lax.ppermute(value, axis, pairs)


def exchanged(value, axis, mask):
    size = lax.axis_size(axis)
    return lax.ppermute(value, axis, [(i, i ^ mask) for i in range(size)])


def summed_over_z(value):
    for base in (1, 4):
        one = exchanged(value, "z", base)
        two = exchanged(value, "z", 2 * base)
        three = exchanged(value, "z", 3 * base)
        value = (value + one) + (two + three)
    return value


def total_over_all(partial):
    rows, columns = partial.shape
    peers = lax.axis_size(LAYER)
    chunk = 8
    padded = jnp.pad(partial, ((0, peers * chunk - rows), (0, 0))).reshape(peers, chunk, columns)
    terms = lax.all_to_all(padded, LAYER, 0, 0, tiled=True)
    mine = summed_over_z(jnp.sum(terms, axis=0))
    whole = lax.all_to_all(jnp.broadcast_to(mine, (peers, chunk, columns)), LAYER, 0, 0, tiled=True)
    return whole.reshape(peers * chunk, columns)[:rows]


def factor(gram, cross):
    lower = jnp.linalg.cholesky(gram)
    inverse = jax.scipy.linalg.solve_triangular(
        lower, jnp.eye(gram.shape[0], dtype=jnp.float32), lower=True
    )
    projected = jnp.dot(
        jnp.dot(inverse, cross, precision=lax.Precision.HIGHEST),
        inverse.T,
        precision=lax.Precision.HIGHEST,
    )
    return (projected, inverse.astype(jnp.bfloat16))


def per_device(initial_block, labels, filter_low, filter_high):
    share, _, height, width = initial_block.shape
    group, blocks = lax.axis_size(GROUP), lax.axis_size(MODE)
    local = share // group
    modes = share * blocks
    rows = height // blocks
    scale = math.sqrt(height * width * group * lax.axis_size("z"))

    fields = initial_block.reshape(group, local, height, width)
    tags = jnp.broadcast_to(labels.astype(jnp.bfloat16)[None], (group, 1, height, width))
    own = lax.all_to_all(jnp.concatenate([fields, tags], axis=1), GROUP, 0, 0, tiled=True)
    extra = REACH - group
    lo, hi = shifted(own, "z", 1), shifted(own, "z", -1)
    far_lo, far_hi = shifted(own[group - extra :], "z", 2), shifted(own[:extra], "z", -2)

    bounds = jnp.stack([filter_low, filter_high])
    pair = filtered_and_applied(bounds, far_lo, lo, own, hi, far_hi, blocks)
    pair = pair.reshape(blocks * group, 2 * local, rows, width)

    pair = lax.all_to_all(pair, LAYER, 0, 0, tiled=True)
    filtered = pair[:, :local].reshape(modes, rows * width)
    applied = pair[:, local:].reshape(modes, rows * width)
    both = jnp.concatenate([filtered, applied], axis=0)
    partial = jnp.einsum("mc,nc->mn", both, filtered, preferred_element_type=jnp.float32)
    total = total_over_all(partial)
    gram, cross = total[:modes], total[modes:].T
    projected, rotation = factor(gram, cross)
    turned = jnp.einsum("jm,mc->jc", rotation, filtered, preferred_element_type=jnp.float32)
    turned = (turned * scale).astype(jnp.bfloat16).reshape(blocks, share, rows, width)
    turned = lax.all_to_all(turned, MODE, 0, 0, tiled=True)
    modes_out = jnp.transpose(turned, (1, 0, 2, 3)).reshape(share, 1, height, width)
    return (modes_out, projected)


def solution(mesh):
    devices = mesh.devices
    slabs, modes = devices.shape
    fine = Mesh(devices.reshape(slabs // 4, 2, 2, 2, modes // 2), AXES)
    placed = (P(MODE, ("z",) + GROUP, None, None), P(("z",) + GROUP, None, None), P(), P())
    return jax.shard_map(
        per_device,
        mesh=fine,
        in_specs=placed,
        out_specs=(P(MODE, ("z",) + GROUP, None, None), P()),
        check_vma=False,
    )
```

time: 455 us -> 151 us (0.33)
  the two profiles are of different devices: /device:TPU:4 before, /device:TPU:1 now
where the time goes in v1:
time: 151 us; the launch traced here: 150 us
  starting transfers between devices  58.6 us (39%)
  blocking collectives  41.5 us (27%)
  other arithmetic  20 us (13%)
  waiting for transfers between devices  17.5 us (12%)
  Pallas kernels  6.99 us (5%)
  between operations  2.15 us (1%)
  matrix products  1.75 us (1%)
  local copies, waits for them, and re-layouts  1.66 us (1%)
    ppermute x6, starting transfers between devices, exchanged(): return lax.ppermute(value, axis, [(i, i ^ mask) for i in range(size)])  33.5 us
    all_to_all x1, blocking collectives, per_device(): pair = lax.all_to_all(pair, LAYER, 0, 0, tiled=True)  15.2 us
    all_to_all x1, blocking collectives, total_over_all(): lax.all_to_all(jnp.broadcast_to(mine, (peers, chunk, columns)), LAYER, 0,...  14.6 us
    all_to_all x1, blocking collectives, total_over_all(): terms = lax.all_to_all(padded, LAYER, 0, 0, tiled=True)  11.8 us
    ppermute x4, starting transfers between devices, shifted(): return lax.ppermute(value, axis, pairs)  11.5 us
    all_to_all x1, starting transfers between devices, per_device(): lax.all_to_all(jnp.concatenate([fields, tags], axis=1), GROUP, 0, 0, tile...  10.2 us
    another operation x3, other arithmetic, factor(): lower = jnp.linalg.cholesky(gram)  9.45 us
    another operation x2, other arithmetic, factor(): jax.scipy.linalg.solve_triangular(lower, jnp.eye(gram.shape[0], dtype=jnp...  8.01 us
  transfers between devices with their start and end apart: 12, of which 7 were waited for; matrix products, arithmetic and copies ran while one was open for 1% of the time, Pallas kernels for 0%

profile of v1, /device:TPU:1, one launch (start us, length us, event | category | flops | bytes accessed | tf_op | source)
XLA Modules:
  0.0 150.1 jit_solution(115674970497498745)
XLA Ops:
  0.6 0.8 convert_bitcast_fusion
  1.4 1.7 %pad_maximum_fusion = bf16[4,4,64,128]{3,2,1,0:T(8,128)(2,1)} fusion(bf16[4,1,64,128]{3,2,1,0:T(8,128)(2,1)S(1)} %broadcast_in_dim.14, bf16[4,3,64,128]{3,2,1,0:T(8,128)(2,1)} %bitcast.52), kind=kLoop, calls=%fused_computation.7 | loop fusion | flops 131072 | bytes 524288 | tf_op jit(solution)/shard_map/concatenate | solution.py:171
  3.1 10.2 %all-to-all-start = ((bf16[4,4,64,128]{3,2,1,0:T(8,128)(2,1)}), bf16[4,4,64,128]{3,2,1,0:T(8,128)(2,1)S(1)}, u32[]{:S(2)}, u32[]{:S(2)}) async-start(bf16[4,4,64,128]{3,2,1,0:T(8,128)(2,1)} %pad_maximum_fusion), calls=%async_computation | async-start | bytes 524288 | tf_op jit(solution)/shard_map/all_to_all | solution.py:171
  14.6 3.9 %all-to-all-done.own = bf16[4,4,64,128]{3,2,1,0:T(8,128)(2,1)S(1)} async-done(((bf16[4,4,64,128]{3,2,1,0:T(8,128)(2,1)}), bf16[4,4,64,128]{3,2,1,0:T(8,128)(2,1)S(1)}, u32[]{:S(2)}, u32[]{:S(2)}) %all-to-all-start) | async-done | bytes 262176 | tf_op jit(solution)/shard_map/all_to_all | solution.py:171
  18.5 1.3 collective-permute-start.2
  19.8 4.0 %collective-permute-start.1 = (bf16[4,4,64,128]{3,2,1,0:T(8,128)(2,1)S(1)}, bf16[4,4,64,128]{3,2,1,0:T(8,128)(2,1)S(1)}, u32[]{:S(2)}, u32[]{:S(2)}) collective-permute-start(bf16[4,4,64,128]{3,2,1,0:T(8,128)(2,1)S(1)} %all-to-all-done.own), channel_id=1, source_target_pairs={{0,32},{32,64},{64,96},{96,128},{128,160},{160,192},{192,224},{224... | collective-permute-start | bytes 786440 | tf_op jit(solution)/shard_map/ppermute | solution.py:120
  23.8 1.3 collective-permute-start.3
  25.1 4.9 %collective-permute-start = (bf16[1,4,64,128]{3,2,1,0:T(8,128)(2,1)S(1)}, bf16[1,4,64,128]{3,2,1,0:T(8,128)(2,1)S(1)}, u32[]{:S(2)}, u32[]{:S(2)}) collective-permute-start(bf16[1,4,64,128]{3,2,1,0:T(8,128)(2,1)S(1)} %get-tuple-element.5), channel_id=1, source_target_pairs={{0,64},{32,96},{64,128},{96,160},{128,192},{160,224},{192,256},{22... | collective-permute-start | bytes 196616 | tf_op jit(solution)/shard_map/ppermute | solution.py:120
  30.0 0.1 pad_maximum_fusion.1.bounds
  30.1 0.3 collective-permute-done.3.far_hi
  30.4 0.9 collective-permute-done.far_lo
  31.3 0.0 collective-permute-done.2.hi
  31.3 0.0 collective-permute-done.1.lo
  31.3 7.0 %chebyshev_filter.1 = bf16[8,4,6,8,128]{4,3,2,1,0:T(8,128)(2,1)S(1)} custom-call(f32[2]{0:T(128)S(1)} %pad_maximum_fusion.1.bounds, bf16[1,4,64,128]{3,2,1,0:T(8,128)(2,1)S(1)} %collective-permute-done.far_lo, bf16[4,4,64,128]{3,2,1,0:T(8,128)(2,1)S(1)} %collective-permute-done.1.lo, bf16[4,4,64,128]{3,2,1,0:T(8,128)(2,1)S(1)} %all-to-all-done.own, ...), custom_call_target="tpu_custom_call" | custom-call | tf_op jit(solution)/shard_map/chebyshev_filter/pallas_call | solution.py:106
  38.3 15.2 %all_to_all.25 = bf16[32,6,8,128]{3,2,1,0:T(8,128)(2,1)S(1)} all-to-all(bf16[32,6,8,128]{3,2,1,0:T(8,128)(2,1)S(1)} %bitcast.48), channel_id=1, replica_groups=mesh['z'=16,'xl'=2,'core'=2,'xh'=2,'y'=4] {'xh','y','xl','core'}, dimensions={0} | all-to-all | bytes 786432 | tf_op jit(solution)/shard_map/all_to_all | solution.py:180
  53.5 0.1 copy_bitcast_fusion
  53.6 0.3 fusion.2
  53.9 11.8 %all_to_all.26 = f32[32,8,96]{2,1,0:T(8,128)S(1)} all-to-all(f32[32,8,96]{2,1,0:T(8,128)S(1)} %pad_bitcast_fusion), channel_id=1, replica_groups=mesh['z'=16,'xl'=2,'core'=2,'xh'=2,'y'=4] {'xh','y','xl','core'}, dimensions={0} | all-to-all | bytes 196608 | tf_op jit(solution)/shard_map/all_to_all | solution.py:142
  65.7 7.4 %collective-permute-start.6 = (f32[8,96]{1,0:T(8,128)S(1)}, f32[8,96]{1,0:T(8,128)S(1)}, u32[]{:S(2)}, u32[]{:S(2)}) collective-permute-start(f32[8,96]{1,0:T(8,128)S(1)} %reduce_sum.9), channel_id=1, source_target_pairs={{0,96},{32,64},{64,32},{96,0},{128,224},{160,192},{192,160},{224,1... | collective-permute-start | bytes 9224 | tf_op jit(solution)/shard_map/ppermute | solution.py:125
  73.1 1.9 %collective-permute-start.5 = (f32[8,96]{1,0:T(8,128)S(1)}, f32[8,96]{1,0:T(8,128)S(1)}, u32[]{:S(2)}, u32[]{:S(2)}) collective-permute-start(f32[8,96]{1,0:T(8,128)S(1)} %reduce_sum.9), channel_id=1, source_target_pairs={{0,64},{32,96},{64,0},{96,32},{128,192},{160,224},{192,128},{224,1... | collective-permute-start | bytes 9224 | tf_op jit(solution)/shard_map/ppermute | solution.py:125
  75.0 2.2 %collective-permute-start.4 = (f32[8,96]{1,0:T(8,128)S(1)}, f32[8,96]{1,0:T(8,128)S(1)}, u32[]{:S(2)}, u32[]{:S(2)}) collective-permute-start(f32[8,96]{1,0:T(8,128)S(1)} %reduce_sum.9), channel_id=1, source_target_pairs={{0,32},{32,0},{64,96},{96,64},{128,160},{160,128},{192,224},{224,1... | collective-permute-start | bytes 9224 | tf_op jit(solution)/shard_map/ppermute | solution.py:125
  77.2 0.0 collective-permute-done.6
  77.2 1.1 collective-permute-done.5
  78.3 1.0 collective-permute-done.4
  79.4 13.0 %collective-permute-start.9 = (f32[8,96]{1,0:T(8,128)S(1)}, f32[8,96]{1,0:T(8,128)S(1)}, u32[]{:S(2)}, u32[]{:S(2)}) collective-permute-start(f32[8,96]{1,0:T(8,128)S(1)} %add_add_fusion.1), channel_id=1, source_target_pairs={{0,384},{32,416},{64,448},{96,480},{128,256},{160,288},{192,320},{... | collective-permute-start | bytes 9224 | tf_op jit(solution)/shard_map/ppermute | solution.py:125
  92.4 2.8 %collective-permute-start.8 = (f32[8,96]{1,0:T(8,128)S(1)}, f32[8,96]{1,0:T(8,128)S(1)}, u32[]{:S(2)}, u32[]{:S(2)}) collective-permute-start(f32[8,96]{1,0:T(8,128)S(1)} %add_add_fusion.1), channel_id=1, source_target_pairs={{0,256},{32,288},{64,320},{96,352},{128,384},{160,416},{192,448},{... | collective-permute-start | bytes 9224 | tf_op jit(solution)/shard_map/ppermute | solution.py:125
  95.2 6.1 %collective-permute-start.7 = (f32[8,96]{1,0:T(8,128)S(1)}, f32[8,96]{1,0:T(8,128)S(1)}, u32[]{:S(2)}, u32[]{:S(2)}) collective-permute-start(f32[8,96]{1,0:T(8,128)S(1)} %add_add_fusion.1), channel_id=1, source_target_pairs={{0,128},{32,160},{64,192},{96,224},{128,0},{160,32},{192,64},{224,... | collective-permute-start | bytes 9224 | tf_op jit(solution)/shard_map/ppermute | solution.py:125
  101.3 0.0 collective-permute-done.9
  101.3 4.1 %collective-permute-done.8 = f32[8,96]{1,0:T(8,128)S(1)} collective-permute-done((f32[8,96]{1,0:T(8,128)S(1)}, f32[8,96]{1,0:T(8,128)S(1)}, u32[]{:S(2)}, u32[]{:S(2)}) %collective-permute-start.8) | collective-permute-done | bytes 3104 | tf_op jit(solution)/shard_map/ppermute | solution.py:125
  105.5 0.0 collective-permute-done.7
  105.5 14.6 %all_to_all.27 = f32[32,8,96]{2,1,0:T(8,128)S(1)} all-to-all(f32[32,8,96]{2,1,0:T(8,128)S(1)} %broadcast_in_dim.15), channel_id=1, replica_groups=mesh['z'=16,'xl'=2,'core'=2,'xh'=2,'y'=4] {'xh','y','xl','core'}, dimensions={0} | all-to-all | bytes 196608 | tf_op jit(solution)/shard_map/all_to_all | solution.py:144
  120.1 0.1 copy.9
  120.2 8.8 %cholesky.17 = f32[96,96]{1,0:T(8,128)S(1)} custom-call(f32[96,96]{1,0:T(8,128)S(1)} %fusion.10), custom_call_target="Cholesky" | custom-call | tf_op jit(solution)/shard_map/jit(cholesky)/cholesky | solution.py:149
  129.0 0.6 compare_reduce_fusion
  129.6 0.7 fusion.6
  130.3 7.4 %custom-call.7 = f32[1,96,96]{1,2,0:T(8,128)S(1)} custom-call(f32[1,96,96]{2,1,0:T(8,128)S(1)} %fusion.6), custom_call_target="InvertDiagBlocksLowerTriangular" | custom-call | tf_op jit(solution)/shard_map/jit(_solve_triangular)/triangular_solve | solution.py:150
  137.6 0.2 fusion.8
  137.9 0.2 fusion.1
  138.1 0.7 copy.14
  138.8 3.4 %all-to-all-start.4 = ((bf16[8,12,8,128]{3,2,1,0:T(8,128)(2,1)}), bf16[8,12,8,128]{3,2,1,0:T(8,128)(2,1)S(1)}, u32[]{:S(2)}, u32[]{:S(2)}) async-start(bf16[8,12,8,128]{3,2,1,0:T(8,128)(2,1)} %bitcast.21), calls=%async_computation.4 | async-start | bytes 393216 | tf_op jit(solution)/shard_map/all_to_all | solution.py:190
  142.2 0.2 fusion.7
  142.4 0.8 fusion.15
  143.3 6.1 %all-to-all-done.4 = bf16[8,12,8,128]{3,2,1,0:T(8,128)(2,1)S(1)} async-done(((bf16[8,12,8,128]{3,2,1,0:T(8,128)(2,1)}), bf16[8,12,8,128]{3,2,1,0:T(8,128)(2,1)S(1)}, u32[]{:S(2)}, u32[]{:S(2)}) %all-to-all-start.4) | async-done | bytes 196640 | tf_op jit(solution)/shard_map/all_to_all | solution.py:190
  149.4 0.7 copy_bitcast_fusion.2
  (11 shorter events, 0.2 us)
Async XLA Ops:
  3.1 15.4 %all-to-all-start = ((bf16[4,4,64,128]{3,2,1,0:T(8,128)(2,1)}), bf16[4,4,64,128]{3,2,1,0:T(8,128)(2,1)S(1)}, u32[]{:S(2)}, u32[]{:S(2)}) async-start(bf16[4,4,64,128]{3,2,1,0:T(8,128)(2,1)} %pad_maximum_fusion), calls=%async_computation | async-start | bytes 524288 | tf_op jit(solution)/shard_map/all_to_all | solution.py:171
  18.5 12.8 %collective-permute-start.2 = (bf16[4,4,64,128]{3,2,1,0:T(8,128)(2,1)S(1)}, bf16[4,4,64,128]{3,2,1,0:T(8,128)(2,1)S(1)}, u32[]{:S(2)}, u32[]{:S(2)}) collective-permute-start(bf16[4,4,64,128]{3,2,1,0:T(8,128)(2,1)S(1)} %all-to-all-done.own), channel_id=1, source_target_pairs={{32,0},{64,32},{96,64},{128,96},{160,128},{192,160},{224,192},{256... | collective-permute-start | bytes 786440 | tf_op jit(solution)/shard_map/ppermute | solution.py:120
  19.8 11.5 %collective-permute-start.1 = (bf16[4,4,64,128]{3,2,1,0:T(8,128)(2,1)S(1)}, bf16[4,4,64,128]{3,2,1,0:T(8,128)(2,1)S(1)}, u32[]{:S(2)}, u32[]{:S(2)}) collective-permute-start(bf16[4,4,64,128]{3,2,1,0:T(8,128)(2,1)S(1)} %all-to-all-done.own), channel_id=1, source_target_pairs={{0,32},{32,64},{64,96},{96,128},{128,160},{160,192},{192,224},{224... | collective-permute-start | bytes 786440 | tf_op jit(solution)/shard_map/ppermute | solution.py:120
  23.8 6.6 %collective-permute-start.3 = (bf16[1,4,64,128]{3,2,1,0:T(8,128)(2,1)S(1)}, bf16[1,4,64,128]{3,2,1,0:T(8,128)(2,1)S(1)}, u32[]{:S(2)}, u32[]{:S(2)}) collective-permute-start(bf16[1,4,64,128]{3,2,1,0:T(8,128)(2,1)S(1)} %get-tuple-element.4), channel_id=1, source_target_pairs={{64,0},{96,32},{128,64},{160,96},{192,128},{224,160},{256,192},{28... | collective-permute-start | bytes 196616 | tf_op jit(solution)/shard_map/ppermute | solution.py:120
  25.1 6.2 %collective-permute-start = (bf16[1,4,64,128]{3,2,1,0:T(8,128)(2,1)S(1)}, bf16[1,4,64,128]{3,2,1,0:T(8,128)(2,1)S(1)}, u32[]{:S(2)}, u32[]{:S(2)}) collective-permute-start(bf16[1,4,64,128]{3,2,1,0:T(8,128)(2,1)S(1)} %get-tuple-element.5), channel_id=1, source_target_pairs={{0,64},{32,96},{64,128},{96,160},{128,192},{160,224},{192,256},{22... | collective-permute-start | bytes 196616 | tf_op jit(solution)/shard_map/ppermute | solution.py:120
  65.7 11.6 %collective-permute-start.6 = (f32[8,96]{1,0:T(8,128)S(1)}, f32[8,96]{1,0:T(8,128)S(1)}, u32[]{:S(2)}, u32[]{:S(2)}) collective-permute-start(f32[8,96]{1,0:T(8,128)S(1)} %reduce_sum.9), channel_id=1, source_target_pairs={{0,96},{32,64},{64,32},{96,0},{128,224},{160,192},{192,160},{224,1... | collective-permute-start | bytes 9224 | tf_op jit(solution)/shard_map/ppermute | solution.py:125
  73.1 5.3 %collective-permute-start.5 = (f32[8,96]{1,0:T(8,128)S(1)}, f32[8,96]{1,0:T(8,128)S(1)}, u32[]{:S(2)}, u32[]{:S(2)}) collective-permute-start(f32[8,96]{1,0:T(8,128)S(1)} %reduce_sum.9), channel_id=1, source_target_pairs={{0,64},{32,96},{64,0},{96,32},{128,192},{160,224},{192,128},{224,1... | collective-permute-start | bytes 9224 | tf_op jit(solution)/shard_map/ppermute | solution.py:125
  75.0 4.4 %collective-permute-start.4 = (f32[8,96]{1,0:T(8,128)S(1)}, f32[8,96]{1,0:T(8,128)S(1)}, u32[]{:S(2)}, u32[]{:S(2)}) collective-permute-start(f32[8,96]{1,0:T(8,128)S(1)} %reduce_sum.9), channel_id=1, source_target_pairs={{0,32},{32,0},{64,96},{96,64},{128,160},{160,128},{192,224},{224,1... | collective-permute-start | bytes 9224 | tf_op jit(solution)/shard_map/ppermute | solution.py:125
  79.4 22.0 %collective-permute-start.9 = (f32[8,96]{1,0:T(8,128)S(1)}, f32[8,96]{1,0:T(8,128)S(1)}, u32[]{:S(2)}, u32[]{:S(2)}) collective-permute-start(f32[8,96]{1,0:T(8,128)S(1)} %add_add_fusion.1), channel_id=1, source_target_pairs={{0,384},{32,416},{64,448},{96,480},{128,256},{160,288},{192,320},{... | collective-permute-start | bytes 9224 | tf_op jit(solution)/shard_map/ppermute | solution.py:125
  92.4 13.1 %collective-permute-start.8 = (f32[8,96]{1,0:T(8,128)S(1)}, f32[8,96]{1,0:T(8,128)S(1)}, u32[]{:S(2)}, u32[]{:S(2)}) collective-permute-start(f32[8,96]{1,0:T(8,128)S(1)} %add_add_fusion.1), channel_id=1, source_target_pairs={{0,256},{32,288},{64,320},{96,352},{128,384},{160,416},{192,448},{... | collective-permute-start | bytes 9224 | tf_op jit(solution)/shard_map/ppermute | solution.py:125
  95.2 10.3 %collective-permute-start.7 = (f32[8,96]{1,0:T(8,128)S(1)}, f32[8,96]{1,0:T(8,128)S(1)}, u32[]{:S(2)}, u32[]{:S(2)}) collective-permute-start(f32[8,96]{1,0:T(8,128)S(1)} %add_add_fusion.1), channel_id=1, source_target_pairs={{0,128},{32,160},{64,192},{96,224},{128,0},{160,32},{192,64},{224,... | collective-permute-start | bytes 9224 | tf_op jit(solution)/shard_map/ppermute | solution.py:125
  138.8 10.6 %all-to-all-start.4 = ((bf16[8,12,8,128]{3,2,1,0:T(8,128)(2,1)}), bf16[8,12,8,128]{3,2,1,0:T(8,128)(2,1)S(1)}, u32[]{:S(2)}, u32[]{:S(2)}) async-start(bf16[8,12,8,128]{3,2,1,0:T(8,128)(2,1)} %bitcast.21), calls=%async_computation.4 | async-start | bytes 393216 | tf_op jit(solution)/shard_map/all_to_all | solution.py:190

commit v2 on v1

--- a/solution.py
+++ b/solution.py
@@ -11,6 +11,7 @@
 DEGREE = 4
 ROOTS = (0.0, 0.7745967, 1.0, 1.3416408)
 REACH = DEGREE + 1
+SUBLANES, LANES = 8, 128
 
 AXES = ("z", "xl", "core", "xh", "y")
 GROUP = ("xl", "core")
@@ -120,18 +121,9 @@
     return lax.ppermute(value, axis, pairs)
 
 
-def exchanged(value, axis, mask):
-    size = lax.axis_size(axis)
-    return lax.ppermute(value, axis, [(i, i ^ mask) for i in range(size)])
-
-
 def summed_over_z(value):
-    for base in (1, 4):
-        one = exchanged(value, "z", base)
-        two = exchanged(value, "z", 2 * base)
-        three = exchanged(value, "z", 3 * base)
-        value = (value + one) + (two + three)
-    return value
+    copies = jnp.broadcast_to(value, (lax.axis_size("z"),) + value.shape)
+    return jnp.sum(lax.all_to_all(copies, "z", 0, 0, tiled=True), axis=0)
 
 
 def total_over_all(partial):
@@ -145,17 +137,63 @@
     return whole.reshape(peers * chunk, columns)[:rows]
 
 
-def factor(gram, cross):
-    lower = jnp.linalg.cholesky(gram)
-    inverse = jax.scipy.linalg.solve_triangular(
-        lower, jnp.eye(gram.shape[0], dtype=jnp.float32), lower=True
-    )
-    projected = jnp.dot(
+def inverse_kernel(gram, out):
+    groups = gram.shape[0] // SUBLANES
+    tile = (SUBLANES, gram.shape[1])
+    sub = lax.broadcasted_iota(jnp.int32, tile, 0)
+    lane = lax.broadcasted_iota(jnp.int32, tile, 1)
+    left = [gram[SUBLANES * g : SUBLANES * (g + 1), :] for g in range(groups)]
+    right = [jnp.where(lane == sub + SUBLANES * g, 1.0, 0.0) for g in range(groups)]
+
+    def row_of(value, t):
+        return jnp.broadcast_to(value[t : t + 1, :], tile)
+
+    for b in range(groups):
+        first = SUBLANES * b
+        columns = [
+            [jnp.broadcast_to(left[g][:, first + t : first + t + 1], tile) for g in range(b, groups)]
+            for t in range(SUBLANES)
+        ]
+        diagonal = jnp.ones(tile, jnp.float32)
+        for t in range(SUBLANES):
+            pivot = row_of(columns[t][0], t)
+            diagonal = jnp.where(sub == t, pivot, diagonal)
+            part = 1.0 / pivot
+            row_left = row_of(left[b], t) * part
+            row_right = row_of(right[b], t) * part
+            rest = range(t + 1, SUBLANES)
+            row_columns = [row_of(columns[s][0], t) * part for s in rest]
+            for g in range(b, groups):
+                weight = columns[t][g - b]
+                if g == b:
+                    weight = jnp.where(sub > t, weight, 0.0)
+                left[g] = left[g] - weight * row_left
+                right[g] = right[g] - weight * row_right
+                for s, row_column in zip(rest, row_columns):
+                    columns[s][g - b] = columns[s][g - b] - weight * row_column
+        out[first : first + SUBLANES, :] = right[b] * lax.rsqrt(diagonal)
+
+
+def inverse_factor(gram):
+    size = gram.shape[0]
+    padded = jnp.pad(gram, ((0, 0), (0, LANES - size)))
+    vmem = pl.BlockSpec(memory_space=pltpu.VMEM)
+    inverse = pl.pallas_call(
+        inverse_kernel,
+        out_shape=jax.ShapeDtypeStruct(padded.shape, jnp.float32),
+        in_specs=[vmem],
+        out_specs=vmem,
+        name="inverse_factor",
+    )(padded)
+    return inverse[:, :size]
+
+
+def projection(inverse, cross):
+    return jnp.dot(
         jnp.dot(inverse, cross, precision=lax.Precision.HIGHEST),
         inverse.T,
         precision=lax.Precision.HIGHEST,
     )
-    return (projected, inverse.astype(jnp.bfloat16))
 
 
 def per_device(initial_block, labels, filter_low, filter_high):
@@ -184,8 +222,9 @@
     partial = jnp.einsum("mc,nc->mn", both, filtered, preferred_element_type=jnp.float32)
     total = total_over_all(partial)
     gram, cross = total[:modes], total[modes:].T
-    projected, rotation = factor(gram, cross)
-    turned = jnp.einsum("jm,mc->jc", rotation, filtered, preferred_element_type=jnp.float32)
+    inverse = inverse_factor(gram)
+    projected = projection(inverse, cross)
+    turned = jnp.einsum("jm,mc->jc", inverse.astype(jnp.bfloat16), filtered, preferred_element_type=jnp.float32)
     turned = (turned * scale).astype(jnp.bfloat16).reshape(blocks, share, rows, width)
     turned = lax.all_to_all(turned, MODE, 0, 0, tiled=True)
     modes_out = jnp.transpose(turned, (1, 0, 2, 3)).reshape(share, 1, height, width)

time: 151 us -> 125 us (0.83)
  starting transfers between devices: 58.6 us -> 25.2 us
  blocking collectives: 41.5 us -> 67.8 us
  other arithmetic: 20 us -> 2.56 us
  waiting for transfers between devices: 17.5 us -> 11.2 us
  Pallas kernels: 6.99 us -> 11.3 us
    ppermute x6 -> x0, starting transfers between devices: 33.5 us -> none  [exchanged(): return lax.ppermute(value, axis, [(i, i ^ mask) for i in range(size)])]
    all_to_all x0 -> x1, blocking collectives: none -> 27.9 us  [summed_over_z(): return jnp.sum(lax.all_to_all(copies, 'z', 0, 0, tiled=True), axis=0)]
    another operation x5 -> x0, other arithmetic: 17.5 us -> none  [the longest x3 9.45 us: factor(): lower = jnp.linalg.cholesky(gram)]
    ppermute x6 -> x0, waiting for transfers between devices: 6.27 us -> none  [exchanged(): return lax.ppermute(value, axis, [(i, i ^ mask) for i in range(size)])]
    pallas_call x0 -> x1, Pallas kernels: none -> 4.26 us  [inverse_factor(): pl.pallas_call(inverse_kernel, out_shape=jax.ShapeDtypeStruct(padded.shap...]
    all_to_all x1, blocking collectives: 14.6 us -> 13 us  [total_over_all(): lax.all_to_all(jnp.broadcast_to(mine, (peers, chunk, columns)), LAYER, 0,...]
  transfers between devices with their start and end apart: 12 -> 6, of which waited for: 7 -> 4; matrix products, arithmetic and copies ran while one was open for 1% -> 1% of each run, Pallas kernels for 0% -> 0%
where the time goes in v2:
time: 125 us
  blocking collectives  67.8 us (54%)
  starting transfers between devices  25.2 us (20%)
  Pallas kernels  11.3 us (9%)
  waiting for transfers between devices  11.2 us (9%)
  other arithmetic  2.56 us (2%)
  matrix products  2.32 us (2%)
  local copies, waits for them, and re-layouts  2.22 us (2%)
  between operations  2.05 us (2%)
    all_to_all x1, blocking collectives, summed_over_z(): return jnp.sum(lax.all_to_all(copies, 'z', 0, 0, tiled=True), axis=0)  27.9 us
    all_to_all x1, blocking collectives, per_device(): pair = lax.all_to_all(pair, LAYER, 0, 0, tiled=True)  15.2 us
    all_to_all x1, blocking collectives, total_over_all(): lax.all_to_all(jnp.broadcast_to(mine, (peers, chunk, columns)), LAYER, 0,...  13 us
    all_to_all x1, blocking collectives, total_over_all(): terms = lax.all_to_all(padded, LAYER, 0, 0, tiled=True)  11.8 us
    ppermute x4, starting transfers between devices, shifted(): return lax.ppermute(value, axis, pairs)  11.5 us
    all_to_all x1, starting transfers between devices, per_device(): lax.all_to_all(jnp.concatenate([fields, tags], axis=1), GROUP, 0, 0, tile...  10.2 us
    pallas_call x1, Pallas kernels, filtered_and_applied(): pl.pallas_call(filter_kernel, out_shape=jax.ShapeDtypeStruct((blocks, dep...  6.99 us
    all_to_all x1, waiting for transfers between devices, per_device(): turned = lax.all_to_all(turned, MODE, 0, 0, tiled=True)  6.14 us
  transfers between devices with their start and end apart: 6, of which 4 were waited for; matrix products, arithmetic and copies ran while one was open for 1% of the time, Pallas kernels for 0%

profile of v2, /device:TPU:1, one launch (start us, length us, event | category | flops | bytes accessed | tf_op | source)
XLA Modules:
  0.0 124.7 jit_solution(14403463034198672665)
XLA Ops:
  0.6 0.8 convert_bitcast_fusion
  1.4 1.7 %pad_maximum_fusion = bf16[4,4,64,128]{3,2,1,0:T(8,128)(2,1)} fusion(bf16[4,1,64,128]{3,2,1,0:T(8,128)(2,1)S(1)} %broadcast_in_dim.15, bf16[4,3,64,128]{3,2,1,0:T(8,128)(2,1)} %bitcast.39), kind=kLoop, calls=%fused_computation.7 | loop fusion | flops 131072 | bytes 524288 | tf_op jit(solution)/shard_map/concatenate | solution.py:209
  3.1 10.2 %all-to-all-start = ((bf16[4,4,64,128]{3,2,1,0:T(8,128)(2,1)}), bf16[4,4,64,128]{3,2,1,0:T(8,128)(2,1)S(1)}, u32[]{:S(2)}, u32[]{:S(2)}) async-start(bf16[4,4,64,128]{3,2,1,0:T(8,128)(2,1)} %pad_maximum_fusion), calls=%async_computation | async-start | bytes 524288 | tf_op jit(solution)/shard_map/all_to_all | solution.py:209
  14.6 3.9 %all-to-all-done.own = bf16[4,4,64,128]{3,2,1,0:T(8,128)(2,1)S(1)} async-done(((bf16[4,4,64,128]{3,2,1,0:T(8,128)(2,1)}), bf16[4,4,64,128]{3,2,1,0:T(8,128)(2,1)S(1)}, u32[]{:S(2)}, u32[]{:S(2)}) %all-to-all-start) | async-done | bytes 262176 | tf_op jit(solution)/shard_map/all_to_all | solution.py:209
  18.5 1.3 %collective-permute-start.2 = (bf16[4,4,64,128]{3,2,1,0:T(8,128)(2,1)S(1)}, bf16[4,4,64,128]{3,2,1,0:T(8,128)(2,1)S(1)}, u32[]{:S(2)}, u32[]{:S(2)}) collective-permute-start(bf16[4,4,64,128]{3,2,1,0:T(8,128)(2,1)S(1)} %all-to-all-done.own), channel_id=1, source_target_pairs={{32,0},{64,32},{96,64},{128,96},{160,128},{192,160},{224,192},{256... | collective-permute-start | bytes 786440 | tf_op jit(solution)/shard_map/ppermute | solution.py:121
  19.8 4.0 %collective-permute-start.1 = (bf16[4,4,64,128]{3,2,1,0:T(8,128)(2,1)S(1)}, bf16[4,4,64,128]{3,2,1,0:T(8,128)(2,1)S(1)}, u32[]{:S(2)}, u32[]{:S(2)}) collective-permute-start(bf16[4,4,64,128]{3,2,1,0:T(8,128)(2,1)S(1)} %all-to-all-done.own), channel_id=1, source_target_pairs={{0,32},{32,64},{64,96},{96,128},{128,160},{160,192},{192,224},{224... | collective-permute-start | bytes 786440 | tf_op jit(solution)/shard_map/ppermute | solution.py:121
  23.8 1.3 %collective-permute-start.3 = (bf16[1,4,64,128]{3,2,1,0:T(8,128)(2,1)S(1)}, bf16[1,4,64,128]{3,2,1,0:T(8,128)(2,1)S(1)}, u32[]{:S(2)}, u32[]{:S(2)}) collective-permute-start(bf16[1,4,64,128]{3,2,1,0:T(8,128)(2,1)S(1)} %get-tuple-element.4), channel_id=1, source_target_pairs={{64,0},{96,32},{128,64},{160,96},{192,128},{224,160},{256,192},{28... | collective-permute-start | bytes 196616 | tf_op jit(solution)/shard_map/ppermute | solution.py:121
  25.1 4.9 %collective-permute-start = (bf16[1,4,64,128]{3,2,1,0:T(8,128)(2,1)S(1)}, bf16[1,4,64,128]{3,2,1,0:T(8,128)(2,1)S(1)}, u32[]{:S(2)}, u32[]{:S(2)}) collective-permute-start(bf16[1,4,64,128]{3,2,1,0:T(8,128)(2,1)S(1)} %get-tuple-element.5), channel_id=1, source_target_pairs={{0,64},{32,96},{64,128},{96,160},{128,192},{160,224},{192,256},{22... | collective-permute-start | bytes 196616 | tf_op jit(solution)/shard_map/ppermute | solution.py:121
  30.0 0.1 pad_maximum_fusion.1.bounds
  30.1 0.3 collective-permute-done.3.far_hi
  30.4 0.9 collective-permute-done.far_lo
  31.3 0.0 collective-permute-done.2.hi
  31.3 0.0 collective-permute-done.1.lo
  31.3 7.0 %chebyshev_filter.1 = bf16[8,4,6,8,128]{4,3,2,1,0:T(8,128)(2,1)S(1)} custom-call(f32[2]{0:T(128)S(1)} %pad_maximum_fusion.1.bounds, bf16[1,4,64,128]{3,2,1,0:T(8,128)(2,1)S(1)} %collective-permute-done.far_lo, bf16[4,4,64,128]{3,2,1,0:T(8,128)(2,1)S(1)} %collective-permute-done.1.lo, bf16[4,4,64,128]{3,2,1,0:T(8,128)(2,1)S(1)} %all-to-all-done.own, ...), custom_call_target="tpu_custom_call" | custom-call | tf_op jit(solution)/shard_map/chebyshev_filter/pallas_call | solution.py:107
  38.3 15.2 %all_to_all.30 = bf16[32,6,8,128]{3,2,1,0:T(8,128)(2,1)S(1)} all-to-all(bf16[32,6,8,128]{3,2,1,0:T(8,128)(2,1)S(1)} %bitcast.35), channel_id=1, replica_groups=mesh['z'=16,'xl'=2,'core'=2,'xh'=2,'y'=4] {'xh','y','xl','core'}, dimensions={0} | all-to-all | bytes 786432 | tf_op jit(solution)/shard_map/all_to_all | solution.py:218
  53.5 0.1 copy_bitcast_fusion
  53.6 0.3 fusion.2
  53.9 11.8 %all_to_all.31 = f32[32,8,96]{2,1,0:T(8,128)S(1)} all-to-all(f32[32,8,96]{2,1,0:T(8,128)S(1)} %pad_bitcast_fusion), channel_id=1, replica_groups=mesh['z'=16,'xl'=2,'core'=2,'xh'=2,'y'=4] {'xh','y','xl','core'}, dimensions={0} | all-to-all | bytes 196608 | tf_op jit(solution)/shard_map/all_to_all | solution.py:134
  65.7 27.9 %all_to_all.32 = f32[16,8,96]{2,1,0:T(8,128)S(1)} all-to-all(f32[16,8,96]{2,1,0:T(8,128)S(1)} %broadcast_in_dim.16), channel_id=1, replica_groups=mesh['z'=16,'xl'=2,'core'=2,'xh'=2,'y'=4] {'z'}, dimensions={0} | all-to-all | bytes 98304 | tf_op jit(solution)/shard_map/all_to_all | solution.py:126
  93.6 13.0 %all_to_all.33 = f32[32,8,96]{2,1,0:T(8,128)S(1)} all-to-all(f32[32,8,96]{2,1,0:T(8,128)S(1)} %broadcast_in_dim.17), channel_id=1, replica_groups=mesh['z'=16,'xl'=2,'core'=2,'xh'=2,'y'=4] {'xh','y','xl','core'}, dimensions={0} | all-to-all | bytes 196608 | tf_op jit(solution)/shard_map/all_to_all | solution.py:136
  106.6 0.6 pad.9.gram
  107.2 4.3 %inverse_factor.1 = f32[96,128]{1,0:T(8,128)} custom-call(f32[96,128]{1,0:T(8,128)} %pad.9.gram), custom_call_target="tpu_custom_call" | custom-call | tf_op jit(solution)/shard_map/inverse_factor/pallas_call | solution.py:181
  111.5 1.0 fusion.1
  112.5 0.7 copy.14
  113.2 0.0 copy-start
  113.2 3.5 %all-to-all-start.5 = ((bf16[8,12,8,128]{3,2,1,0:T(8,128)(2,1)}), bf16[8,12,8,128]{3,2,1,0:T(8,128)(2,1)S(1)}, u32[]{:S(2)}, u32[]{:S(2)}) async-start(bf16[8,12,8,128]{3,2,1,0:T(8,128)(2,1)} %bitcast.18), calls=%async_computation.5 | async-start | bytes 393216 | tf_op jit(solution)/shard_map/all_to_all | solution.py:229
  116.7 0.0 copy-done
  116.8 0.2 fusion.6
  117.0 0.8 fusion.7
  117.8 6.1 %all-to-all-done.5 = bf16[8,12,8,128]{3,2,1,0:T(8,128)(2,1)S(1)} async-done(((bf16[8,12,8,128]{3,2,1,0:T(8,128)(2,1)}), bf16[8,12,8,128]{3,2,1,0:T(8,128)(2,1)S(1)}, u32[]{:S(2)}, u32[]{:S(2)}) %all-to-all-start.5) | async-done | bytes 196640 | tf_op jit(solution)/shard_map/all_to_all | solution.py:229
  124.0 0.7 copy_bitcast_fusion.2
  (9 shorter events, 0.2 us)
Async XLA Ops:
  3.1 15.4 %all-to-all-start = ((bf16[4,4,64,128]{3,2,1,0:T(8,128)(2,1)}), bf16[4,4,64,128]{3,2,1,0:T(8,128)(2,1)S(1)}, u32[]{:S(2)}, u32[]{:S(2)}) async-start(bf16[4,4,64,128]{3,2,1,0:T(8,128)(2,1)} %pad_maximum_fusion), calls=%async_computation | async-start | bytes 524288 | tf_op jit(solution)/shard_map/all_to_all | solution.py:209
  18.5 12.8 %collective-permute-start.2 = (bf16[4,4,64,128]{3,2,1,0:T(8,128)(2,1)S(1)}, bf16[4,4,64,128]{3,2,1,0:T(8,128)(2,1)S(1)}, u32[]{:S(2)}, u32[]{:S(2)}) collective-permute-start(bf16[4,4,64,128]{3,2,1,0:T(8,128)(2,1)S(1)} %all-to-all-done.own), channel_id=1, source_target_pairs={{32,0},{64,32},{96,64},{128,96},{160,128},{192,160},{224,192},{256... | collective-permute-start | bytes 786440 | tf_op jit(solution)/shard_map/ppermute | solution.py:121
  19.8 11.5 %collective-permute-start.1 = (bf16[4,4,64,128]{3,2,1,0:T(8,128)(2,1)S(1)}, bf16[4,4,64,128]{3,2,1,0:T(8,128)(2,1)S(1)}, u32[]{:S(2)}, u32[]{:S(2)}) collective-permute-start(bf16[4,4,64,128]{3,2,1,0:T(8,128)(2,1)S(1)} %all-to-all-done.own), channel_id=1, source_target_pairs={{0,32},{32,64},{64,96},{96,128},{128,160},{160,192},{192,224},{224... | collective-permute-start | bytes 786440 | tf_op jit(solution)/shard_map/ppermute | solution.py:121
  23.8 6.6 %collective-permute-start.3 = (bf16[1,4,64,128]{3,2,1,0:T(8,128)(2,1)S(1)}, bf16[1,4,64,128]{3,2,1,0:T(8,128)(2,1)S(1)}, u32[]{:S(2)}, u32[]{:S(2)}) collective-permute-start(bf16[1,4,64,128]{3,2,1,0:T(8,128)(2,1)S(1)} %get-tuple-element.4), channel_id=1, source_target_pairs={{64,0},{96,32},{128,64},{160,96},{192,128},{224,160},{256,192},{28... | collective-permute-start | bytes 196616 | tf_op jit(solution)/shard_map/ppermute | solution.py:121
  25.1 6.2 %collective-permute-start = (bf16[1,4,64,128]{3,2,1,0:T(8,128)(2,1)S(1)}, bf16[1,4,64,128]{3,2,1,0:T(8,128)(2,1)S(1)}, u32[]{:S(2)}, u32[]{:S(2)}) collective-permute-start(bf16[1,4,64,128]{3,2,1,0:T(8,128)(2,1)S(1)} %get-tuple-element.5), channel_id=1, source_target_pairs={{0,64},{32,96},{64,128},{96,160},{128,192},{160,224},{192,256},{22... | collective-permute-start | bytes 196616 | tf_op jit(solution)/shard_map/ppermute | solution.py:121
  113.2 3.5 %copy-start = (f32[96,128]{1,0:T(8,128)S(1)}, f32[96,128]{1,0:T(8,128)}, u32[]{:S(2)}) copy-start(f32[96,128]{1,0:T(8,128)} %inverse_factor.1) | copy-start | bytes 147460
  113.2 10.8 %all-to-all-start.5 = ((bf16[8,12,8,128]{3,2,1,0:T(8,128)(2,1)}), bf16[8,12,8,128]{3,2,1,0:T(8,128)(2,1)S(1)}, u32[]{:S(2)}, u32[]{:S(2)}) async-start(bf16[8,12,8,128]{3,2,1,0:T(8,128)(2,1)} %bitcast.18), calls=%async_computation.5 | async-start | bytes 393216 | tf_op jit(solution)/shard_map/all_to_all | solution.py:229

commit v3 on v2

v3 whole, which is shorter than its diff:
```python
import functools
import math

import jax
import jax.numpy as jnp
from jax import lax
from jax.experimental import pallas as pl
from jax.experimental.pallas import tpu as pltpu
from jax.sharding import Mesh, PartitionSpec as P

DEGREE = 4
ROOTS = (0.0, 0.7745967, 1.0, 1.3416408)
REACH = DEGREE + 1
SUBLANES = 8
UNROLL = 4

AXES = ("z", "xl", "core", "xh", "y")
GROUP = ("xl", "core")
MODE = ("xh", "y")
LAYER = ("xh", "y", "xl", "core")


def filter_kernel(bounds, far_lo, lo, own, hi, far_hi, out, even, odd, weak_even, weak_odd, strong, degree):
  planes, height, width = degree.shape
  local = even.shape[1]
  rows = out.shape[3]
  low, high = bounds[0], bounds[1]
  centre = 0.5 * (high + low)
  scale = 1.0 / (0.5 * (high - low))
  inner = pl.ds(SUBLANES, height)
  lane = lax.broadcasted_iota(jnp.int32, (height, width), 1)

  def beside(ref, *index):
      value = ref[(*index, inner)]
      up = ref[(*index, pl.ds(SUBLANES - 1, height))]
      down = ref[(*index, pl.ds(SUBLANES + 1, height))]
      left = jnp.where(lane == 0, 0.0, pltpu.roll(value, 1, 1))
      right = jnp.where(lane == width - 1, 0.0, pltpu.roll(value, width - 1, 1))
      return value, (up + down) + (left + right)

  edge = jnp.zeros((SUBLANES, width), jnp.float32)

  def clear(plane, carry):
      for first in (0, SUBLANES + height):
          strong[plane, pl.ds(first, SUBLANES)] = edge
          for mode in range(local):
              weak_even[plane, mode, pl.ds(first, SUBLANES)] = edge
              weak_odd[plane, mode, pl.ds(first, SUBLANES)] = edge
      return carry

  lax.fori_loop(0, planes, clear, 0)

  start = 0
  for source in (far_lo, lo, own, hi, far_hi):
      count = source.shape[0]

      def load(index, carry, source=source, start=start):
          label = source[index, local].astype(jnp.float32)
          root = jnp.where(label == 1.0, ROOTS[1], 0.0)
          root = jnp.where(label == 2.0, ROOTS[2], root)
          root = jnp.where(label == 3.0, ROOTS[3], root)
          strong[start + index, inner] = root
          for mode in range(local):
              value = jnp.where(label > 0.0, source[index, mode].astype(jnp.float32), 0.0)
              even[start + index, mode] = value
              weak_even[start + index, mode, inner] = root * value
          return carry

      lax.fori_loop(0, count, load, 0, unroll=min(count, UNROLL))
      start += count

  def weigh(plane, carry):
      root, around = beside(strong, plane)
      degree[plane] = root * (strong[plane - 1, inner] + strong[plane + 1, inner] + around)
      return carry

  lax.fori_loop(1, planes - 1, weigh, 0, unroll=UNROLL)

  cur, prev, weak, weak_next = even, odd, weak_even, weak_odd
  for step in range(DEGREE):
      factor = scale if step == 0 else 2.0 * scale

      def advance(plane, carry, cur=cur, prev=prev, weak=weak, weak_next=weak_next, factor=factor, step=step):
          root = strong[plane, inner]
          here = (degree[plane] - centre) * factor
          there = root * factor
          for mode in range(local):
              _, around = beside(weak, plane, mode)
              around = around + (weak[plane - 1, mode, inner] + weak[plane + 1, mode, inner])
              value = here * cur[plane, mode] - there * around
              if step > 0:
                  value = value - prev[plane, mode]
              prev[plane, mode] = value
              weak_next[plane, mode, inner] = root * value
          return carry

      lax.fori_loop(step + 1, planes - step - 1, advance, 0, unroll=UNROLL)
      cur, prev = prev, cur
      weak, weak_next = weak_next, weak

  def finish(index, carry):
      plane = REACH + index
      root, heavy = strong[plane, inner], degree[plane]
      for mode in range(local):
          value = cur[plane, mode]
          _, around = beside(weak, plane, mode)
          around = around + (weak[plane - 1, mode, inner] + weak[plane + 1, mode, inner])
          image = heavy * value - root * around
          out[:, index, mode] = value.reshape(-1, rows, width).astype(out.dtype)
          out[:, index, local + mode] = image.reshape(-1, rows, width).astype(out.dtype)
      return carry

  lax.fori_loop(0, own.shape[0], finish, 0, unroll=2)

def filtered_and_applied(bounds, far_lo, lo, own, hi, far_hi, blocks):
    depth, fields, height, width = own.shape
    local = fields - 1
    planes = depth + 2 * REACH
    field = pltpu.VMEM((planes, local, height, width), jnp.float32)
    rimmed = pltpu.VMEM((planes, local, height + 2 * SUBLANES, width), jnp.float32)
    root = pltpu.VMEM((planes, height + 2 * SUBLANES, width), jnp.float32)
    degree = pltpu.VMEM((planes, height, width), jnp.float32)
    vmem = pl.BlockSpec(memory_space=pltpu.VMEM)
    return pl.pallas_call(
        filter_kernel,
        out_shape=jax.ShapeDtypeStruct((blocks, depth, 2 * local, height // blocks, width), jnp.bfloat16),
        in_specs=[pl.BlockSpec(memory_space=pltpu.SMEM)] + [vmem] * 5,
        out_specs=vmem,
        scratch_shapes=[field, field, rimmed, rimmed, root, degree],
        compiler_params=pltpu.CompilerParams(vmem_limit_bytes=40 * 1024 * 1024),
        name="chebyshev_filter",
    )(bounds, far_lo, lo, own, hi, far_hi)


def pack_kernel(block, labels, out):
    group, fields = out.shape[:2]
    local = fields - 1
    tags = labels[0].astype(jnp.float32).astype(out.dtype)
    for peer in range(group):
        for mode in range(local):
            out[peer, mode] = block[peer * local + mode, 0]
        out[peer, local] = tags


def packed(block, labels, group):
    share, _, height, width = block.shape
    vmem = pl.BlockSpec(memory_space=pltpu.VMEM)
    return pl.pallas_call(
        pack_kernel,
        out_shape=jax.ShapeDtypeStruct((group, share // group + 1, height, width), block.dtype),
        in_specs=[vmem, vmem],
        out_specs=vmem,
        name="pack",
    )(block, labels)


def shifted(value, axis, step):
    size = lax.axis_size(axis)
    pairs = [(i, i + step) for i in range(size) if 0 <= i + step < size]
    return lax.ppermute(value, axis, pairs)


def summed_over_z(value):
    copies = jnp.broadcast_to(value, (lax.axis_size("z"),) + value.shape)
    return jnp.sum(lax.all_to_all(copies, "z", 0, 0, tiled=True), axis=0)


def total_over_all(partial):
    rows, columns = partial.shape
    peers = lax.axis_size(LAYER)
    chunk = 8
    padded = jnp.pad(partial, ((0, peers * chunk - rows), (0, 0))).reshape(peers, chunk, columns)
    terms = lax.all_to_all(padded, LAYER, 0, 0, tiled=True)
    mine = summed_over_z(jnp.sum(terms, axis=0))
    whole = lax.all_to_all(jnp.broadcast_to(mine, (peers, chunk, columns)), LAYER, 0, 0, tiled=True)
    return whole


def turn_kernel(scale, whole, filtered, inverse, turned, staged):
    size = inverse.shape[0]
    rows = turned.shape[2]
    groups = size // SUBLANES
    tile = (SUBLANES, size)
    sub = lax.broadcasted_iota(jnp.int32, tile, 0)
    lane = lax.broadcasted_iota(jnp.int32, tile, 1)
    left = [whole[g] for g in range(groups)]
    right = [jnp.where(lane == sub + SUBLANES * g, 1.0, 0.0) for g in range(groups)]

    def row_of(value, t):
        return jnp.broadcast_to(value[t : t + 1, :], tile)

    for b in range(groups):
        first = SUBLANES * b
        columns = [
            [jnp.broadcast_to(left[g][:, first + t : first + t + 1], tile) for g in range(b, groups)]
            for t in range(SUBLANES)
        ]
        diagonal = jnp.ones(tile, jnp.float32)
        for t in range(SUBLANES):
            pivot = row_of(columns[t][0], t)
            diagonal = jnp.where(sub == t, pivot, diagonal)
            part = 1.0 / pivot
            row_left = row_of(left[b], t) * part
            row_right = row_of(right[b], t) * part
            rest = range(t + 1, SUBLANES)
            row_columns = [row_of(columns[s][0], t) * part for s in rest]
            for g in range(b, groups):
                weight = columns[t][g - b]
                if g == b:
                    weight = jnp.where(sub > t, weight, 0.0)
                left[g] = left[g] - weight * row_left
                right[g] = right[g] - weight * row_right
                for s, row_column in zip(rest, row_columns):
                    columns[s][g - b] = columns[s][g - b] - weight * row_column
        inverse[first : first + SUBLANES, :] = right[b] * lax.rsqrt(diagonal)

    rotation = inverse[...].astype(jnp.bfloat16)
    product = jnp.dot(rotation, filtered[...], preferred_element_type=jnp.float32) * scale
    width = turned.shape[3]
    for row in range(rows):
        staged[pl.ds(row, size, stride=rows), :] = product[:, row * width : (row + 1) * width]
    turned[...] = staged[...].reshape(turned.shape).astype(turned.dtype)


def inverse_and_turned(whole, filtered, scale, peers, rows):
    size = whole.shape[2]
    width = filtered.shape[1] // rows
    vmem = pl.BlockSpec(memory_space=pltpu.VMEM)
    return pl.pallas_call(
        functools.partial(turn_kernel, scale),
        out_shape=(
            jax.ShapeDtypeStruct((size, size), jnp.float32),
            jax.ShapeDtypeStruct((peers, size // peers, rows, width), jnp.bfloat16),
        ),
        in_specs=[vmem, vmem],
        out_specs=(vmem, vmem),
        scratch_shapes=[pltpu.VMEM((size * rows, width), jnp.float32)],
        name="inverse_and_turned",
    )(whole, filtered)


def projection(inverse, cross):
    return jnp.dot(
        jnp.dot(inverse, cross, precision=lax.Precision.HIGHEST),
        inverse.T,
        precision=lax.Precision.HIGHEST,
    )


def per_device(initial_block, labels, filter_low, filter_high):
    share, _, height, width = initial_block.shape
    group, blocks = lax.axis_size(GROUP), lax.axis_size(MODE)
    local = share // group
    modes = share * blocks
    rows = height // blocks
    scale = math.sqrt(height * width * group * lax.axis_size("z"))

    own = lax.all_to_all(packed(initial_block, labels, group), GROUP, 0, 0, tiled=True)
    extra = REACH - group
    lo, hi = shifted(own, "z", 1), shifted(own, "z", -1)
    far_lo, far_hi = shifted(own[group - extra :], "z", 2), shifted(own[:extra], "z", -2)

    bounds = jnp.stack([filter_low, filter_high])
    pair = filtered_and_applied(bounds, far_lo, lo, own, hi, far_hi, blocks)
    pair = pair.reshape(blocks * group, 2 * local, rows, width)

    pair = lax.all_to_all(pair, LAYER, 0, 0, tiled=True)
    filtered = pair[:, :local].reshape(modes, rows * width)
    applied = pair[:, local:].reshape(modes, rows * width)
    both = jnp.concatenate([filtered, applied], axis=0)
    partial = jnp.einsum("mc,nc->mn", both, filtered, preferred_element_type=jnp.float32)
    total = total_over_all(partial)
    inverse, turned = inverse_and_turned(total, filtered, scale, blocks, rows)
    cross = total.reshape(-1, modes)[modes : 2 * modes].T
    projected = projection(inverse, cross)
    turned = lax.all_to_all(turned, MODE, 0, 0, tiled=True)
    modes_out = jnp.transpose(turned, (1, 0, 2, 3)).reshape(share, 1, height, width)
    return (modes_out, projected)


def solution(mesh):
    devices = mesh.devices
    slabs, modes = devices.shape
    fine = Mesh(devices.reshape(slabs // 4, 2, 2, 2, modes // 2), AXES)
    placed = (P(MODE, ("z",) + GROUP, None, None), P(("z",) + GROUP, None, None), P(), P())
    return jax.shard_map(
        per_device,
        mesh=fine,
        in_specs=placed,
        out_specs=(P(MODE, ("z",) + GROUP, None, None), P()),
        check_vma=False,
    )
```

time: 125 us -> 121 us (0.968)
  other arithmetic: 2.56 us -> 0.14 us
    pallas_call x1, Pallas kernels: 6.99 us -> 4.73 us  [filtered_and_applied(): pl.pallas_call(filter_kernel, out_shape=jax.ShapeDtypeStruct((blocks, dep...]
    pallas_call x1 -> x2, Pallas kernels: 4.26 us -> 6.35 us  [the longest x1 4.71 us: inverse_and_turned(): pl.pallas_call(functools.partial(turn_kernel, scale), out_shape=(jax.Shap...]
    concatenate x1 -> x0, other arithmetic: 1.66 us -> none  [per_device(): jnp.concatenate([fields, tags], axis=1)]
  transfers between devices with their start and end apart: 6 -> 6, of which waited for: 4 -> 4; matrix products, arithmetic and copies ran while one was open for 1% -> 2% of each run, Pallas kernels for 0% -> 0%
where the time goes in v3:
time: 121 us; the launch traced here: 120 us
  blocking collectives  68 us (56%)
  starting transfers between devices  25.2 us (21%)
  Pallas kernels  11.1 us (9%)
  waiting for transfers between devices  10.4 us (9%)
  matrix products  2.12 us (2%)
  between operations  2.04 us (2%)
  local copies, waits for them, and re-layouts  1.27 us (1%)
    all_to_all x1, blocking collectives, summed_over_z(): return jnp.sum(lax.all_to_all(copies, 'z', 0, 0, tiled=True), axis=0)  27.9 us
    all_to_all x1, blocking collectives, per_device(): pair = lax.all_to_all(pair, LAYER, 0, 0, tiled=True)  15.2 us
    all_to_all x1, blocking collectives, total_over_all(): lax.all_to_all(jnp.broadcast_to(mine, (peers, chunk, columns)), LAYER, 0,...  13.2 us
    all_to_all x1, blocking collectives, total_over_all(): terms = lax.all_to_all(padded, LAYER, 0, 0, tiled=True)  11.8 us
    ppermute x4, starting transfers between devices, shifted(): return lax.ppermute(value, axis, pairs)  11.5 us
    all_to_all x1, starting transfers between devices, per_device(): lax.all_to_all(packed(initial_block, labels, group), GROUP, 0, 0, tiled=T...  10.2 us
    all_to_all x1, waiting for transfers between devices, per_device(): turned = lax.all_to_all(turned, MODE, 0, 0, tiled=True)  5.34 us
    pallas_call x1, Pallas kernels, filtered_and_applied(): pl.pallas_call(filter_kernel, out_shape=jax.ShapeDtypeStruct((blocks, dep...  4.73 us
  transfers between devices with their start and end apart: 6, of which 4 were waited for; matrix products, arithmetic and copies ran while one was open for 2% of the time, Pallas kernels for 0%

profile of v3, /device:TPU:1, one launch (start us, length us, event | category | flops | bytes accessed | tf_op | source)
XLA Modules:
  0.0 120.4 jit_solution(8800859565704886448)
XLA Ops:
  0.6 1.6 %pack.1 = bf16[4,4,64,128]{3,2,1,0:T(8,128)(2,1)} custom-call(bf16[12,1,64,128]{3,2,1,0:T(8,128)(2,1)} %block.1, s32[1,64,128]{2,1,0:T(8,128)} %labels.1), custom_call_target="tpu_custom_call" | custom-call | tf_op jit(solution)/shard_map/pack/pallas_call | solution.py:148
  2.3 10.2 %all-to-all-start = ((bf16[4,4,64,128]{3,2,1,0:T(8,128)(2,1)}), bf16[4,4,64,128]{3,2,1,0:T(8,128)(2,1)S(1)}, u32[]{:S(2)}, u32[]{:S(2)}) async-start(bf16[4,4,64,128]{3,2,1,0:T(8,128)(2,1)} %pack.1), calls=%async_computation | async-start | bytes 524288 | tf_op jit(solution)/shard_map/all_to_all | solution.py:258
  13.8 3.9 %all-to-all-done.own = bf16[4,4,64,128]{3,2,1,0:T(8,128)(2,1)S(1)} async-done(((bf16[4,4,64,128]{3,2,1,0:T(8,128)(2,1)}), bf16[4,4,64,128]{3,2,1,0:T(8,128)(2,1)S(1)}, u32[]{:S(2)}, u32[]{:S(2)}) %all-to-all-start) | async-done | bytes 262176 | tf_op jit(solution)/shard_map/all_to_all | solution.py:258
  17.7 1.3 %collective-permute-start.2 = (bf16[4,4,64,128]{3,2,1,0:T(8,128)(2,1)S(1)}, bf16[4,4,64,128]{3,2,1,0:T(8,128)(2,1)S(1)}, u32[]{:S(2)}, u32[]{:S(2)}) collective-permute-start(bf16[4,4,64,128]{3,2,1,0:T(8,128)(2,1)S(1)} %all-to-all-done.own), channel_id=1, source_target_pairs={{32,0},{64,32},{96,64},{128,96},{160,128},{192,160},{224,192},{256... | collective-permute-start | bytes 786440 | tf_op jit(solution)/shard_map/ppermute | solution.py:160
  19.0 4.0 %collective-permute-start.1 = (bf16[4,4,64,128]{3,2,1,0:T(8,128)(2,1)S(1)}, bf16[4,4,64,128]{3,2,1,0:T(8,128)(2,1)S(1)}, u32[]{:S(2)}, u32[]{:S(2)}) collective-permute-start(bf16[4,4,64,128]{3,2,1,0:T(8,128)(2,1)S(1)} %all-to-all-done.own), channel_id=1, source_target_pairs={{0,32},{32,64},{64,96},{96,128},{128,160},{160,192},{192,224},{224... | collective-permute-start | bytes 786440 | tf_op jit(solution)/shard_map/ppermute | solution.py:160
  23.0 1.3 %collective-permute-start.3 = (bf16[1,4,64,128]{3,2,1,0:T(8,128)(2,1)S(1)}, bf16[1,4,64,128]{3,2,1,0:T(8,128)(2,1)S(1)}, u32[]{:S(2)}, u32[]{:S(2)}) collective-permute-start(bf16[1,4,64,128]{3,2,1,0:T(8,128)(2,1)S(1)} %get-tuple-element.12), channel_id=1, source_target_pairs={{64,0},{96,32},{128,64},{160,96},{192,128},{224,160},{256,192},{28... | collective-permute-start | bytes 196616 | tf_op jit(solution)/shard_map/ppermute | solution.py:160
  24.3 4.9 %collective-permute-start = (bf16[1,4,64,128]{3,2,1,0:T(8,128)(2,1)S(1)}, bf16[1,4,64,128]{3,2,1,0:T(8,128)(2,1)S(1)}, u32[]{:S(2)}, u32[]{:S(2)}) collective-permute-start(bf16[1,4,64,128]{3,2,1,0:T(8,128)(2,1)S(1)} %get-tuple-element.13), channel_id=1, source_target_pairs={{0,64},{32,96},{64,128},{96,160},{128,192},{160,224},{192,256},{22... | collective-permute-start | bytes 196616 | tf_op jit(solution)/shard_map/ppermute | solution.py:160
  29.2 0.1 pad_maximum_fusion.bounds
  29.3 0.3 collective-permute-done.3.far_hi
  29.6 0.9 collective-permute-done.far_lo
  30.5 0.0 collective-permute-done.2.hi
  30.5 0.0 collective-permute-done.1.lo
  30.5 4.7 %chebyshev_filter.1 = bf16[8,4,6,8,128]{4,3,2,1,0:T(8,128)(2,1)S(1)} custom-call(f32[2]{0:T(128)S(1)} %pad_maximum_fusion.bounds, bf16[1,4,64,128]{3,2,1,0:T(8,128)(2,1)S(1)} %collective-permute-done.far_lo, bf16[4,4,64,128]{3,2,1,0:T(8,128)(2,1)S(1)} %collective-permute-done.1.lo, bf16[4,4,64,128]{3,2,1,0:T(8,128)(2,1)S(1)} %all-to-all-done.own, ...), custom_call_target="tpu_custom_call" | custom-call | tf_op jit(solution)/shard_map/chebyshev_filter/pallas_call | solution.py:124
  35.3 15.2 %all_to_all.30 = bf16[32,6,8,128]{3,2,1,0:T(8,128)(2,1)S(1)} all-to-all(bf16[32,6,8,128]{3,2,1,0:T(8,128)(2,1)S(1)} %bitcast.29), channel_id=1, replica_groups=mesh['z'=16,'xl'=2,'core'=2,'xh'=2,'y'=4] {'xh','y','xl','core'}, dimensions={0} | all-to-all | bytes 786432 | tf_op jit(solution)/shard_map/all_to_all | solution.py:267
  50.5 0.1 copy_bitcast_fusion
  50.5 0.0 copy-start
  50.5 0.3 fusion
  50.8 0.4 copy-done
  51.2 11.8 %all_to_all.31 = f32[32,8,96]{2,1,0:T(8,128)S(1)} all-to-all(f32[32,8,96]{2,1,0:T(8,128)S(1)} %pad_bitcast_fusion), channel_id=1, replica_groups=mesh['z'=16,'xl'=2,'core'=2,'xh'=2,'y'=4] {'xh','y','xl','core'}, dimensions={0} | all-to-all | bytes 196608 | tf_op jit(solution)/shard_map/all_to_all | solution.py:173
  63.0 27.9 %all_to_all.32 = f32[16,8,96]{2,1,0:T(8,128)S(1)} all-to-all(f32[16,8,96]{2,1,0:T(8,128)S(1)} %broadcast_in_dim.6), channel_id=1, replica_groups=mesh['z'=16,'xl'=2,'core'=2,'xh'=2,'y'=4] {'z'}, dimensions={0} | all-to-all | bytes 98304 | tf_op jit(solution)/shard_map/all_to_all | solution.py:165
  91.0 13.2 %all_to_all.33.whole = f32[32,8,96]{2,1,0:T(8,128)} all-to-all(f32[32,8,96]{2,1,0:T(8,128)S(1)} %broadcast_in_dim.7), channel_id=1, replica_groups=mesh['z'=16,'xl'=2,'core'=2,'xh'=2,'y'=4] {'xh','y','xl','core'}, dimensions={0} | all-to-all | bytes 196608 | tf_op jit(solution)/shard_map/all_to_all | solution.py:175
  104.2 4.7 %inverse_and_turned.1 = (f32[96,96]{1,0:T(8,128)}, bf16[8,12,8,128]{3,2,1,0:T(8,128)(2,1)}) custom-call(f32[32,8,96]{2,1,0:T(8,128)} %all_to_all.33.whole, bf16[96,1024]{1,0:T(8,128)(2,1)} %copy-done), custom_call_target="tpu_custom_call" | custom-call | tf_op jit(solution)/shard_map/inverse_and_turned/pallas_call | solution.py:229
  108.9 0.0 copy-start.1
  108.9 3.5 %all-to-all-start.5 = ((bf16[8,12,8,128]{3,2,1,0:T(8,128)(2,1)}), bf16[8,12,8,128]{3,2,1,0:T(8,128)(2,1)S(1)}, u32[]{:S(2)}, u32[]{:S(2)}) async-start(bf16[8,12,8,128]{3,2,1,0:T(8,128)(2,1)} %get-tuple-element.4), calls=%async_computation.5 | async-start | bytes 393216 | tf_op jit(solution)/shard_map/all_to_all | solution.py:276
  112.4 0.0 copy-done.1
  112.4 1.0 fusion.4
  113.5 0.8 fusion.8
  114.3 5.3 %all-to-all-done.5 = bf16[8,12,8,128]{3,2,1,0:T(8,128)(2,1)S(1)} async-done(((bf16[8,12,8,128]{3,2,1,0:T(8,128)(2,1)}), bf16[8,12,8,128]{3,2,1,0:T(8,128)(2,1)S(1)}, u32[]{:S(2)}, u32[]{:S(2)}) %all-to-all-start.5) | async-done | bytes 196640 | tf_op jit(solution)/shard_map/all_to_all | solution.py:276
  119.7 0.7 copy_bitcast_fusion.2
  (7 shorter events, 0.1 us)
Async XLA Ops:
  2.3 15.4 %all-to-all-start = ((bf16[4,4,64,128]{3,2,1,0:T(8,128)(2,1)}), bf16[4,4,64,128]{3,2,1,0:T(8,128)(2,1)S(1)}, u32[]{:S(2)}, u32[]{:S(2)}) async-start(bf16[4,4,64,128]{3,2,1,0:T(8,128)(2,1)} %pack.1), calls=%async_computation | async-start | bytes 524288 | tf_op jit(solution)/shard_map/all_to_all | solution.py:258
  17.7 12.8 %collective-permute-start.2 = (bf16[4,4,64,128]{3,2,1,0:T(8,128)(2,1)S(1)}, bf16[4,4,64,128]{3,2,1,0:T(8,128)(2,1)S(1)}, u32[]{:S(2)}, u32[]{:S(2)}) collective-permute-start(bf16[4,4,64,128]{3,2,1,0:T(8,128)(2,1)S(1)} %all-to-all-done.own), channel_id=1, source_target_pairs={{32,0},{64,32},{96,64},{128,96},{160,128},{192,160},{224,192},{256... | collective-permute-start | bytes 786440 | tf_op jit(solution)/shard_map/ppermute | solution.py:160
  19.0 11.5 %collective-permute-start.1 = (bf16[4,4,64,128]{3,2,1,0:T(8,128)(2,1)S(1)}, bf16[4,4,64,128]{3,2,1,0:T(8,128)(2,1)S(1)}, u32[]{:S(2)}, u32[]{:S(2)}) collective-permute-start(bf16[4,4,64,128]{3,2,1,0:T(8,128)(2,1)S(1)} %all-to-all-done.own), channel_id=1, source_target_pairs={{0,32},{32,64},{64,96},{96,128},{128,160},{160,192},{192,224},{224... | collective-permute-start | bytes 786440 | tf_op jit(solution)/shard_map/ppermute | solution.py:160
  23.0 6.6 %collective-permute-start.3 = (bf16[1,4,64,128]{3,2,1,0:T(8,128)(2,1)S(1)}, bf16[1,4,64,128]{3,2,1,0:T(8,128)(2,1)S(1)}, u32[]{:S(2)}, u32[]{:S(2)}) collective-permute-start(bf16[1,4,64,128]{3,2,1,0:T(8,128)(2,1)S(1)} %get-tuple-element.12), channel_id=1, source_target_pairs={{64,0},{96,32},{128,64},{160,96},{192,128},{224,160},{256,192},{28... | collective-permute-start | bytes 196616 | tf_op jit(solution)/shard_map/ppermute | solution.py:160
  24.3 6.2 %collective-permute-start = (bf16[1,4,64,128]{3,2,1,0:T(8,128)(2,1)S(1)}, bf16[1,4,64,128]{3,2,1,0:T(8,128)(2,1)S(1)}, u32[]{:S(2)}, u32[]{:S(2)}) collective-permute-start(bf16[1,4,64,128]{3,2,1,0:T(8,128)(2,1)S(1)} %get-tuple-element.13), channel_id=1, source_target_pairs={{0,64},{32,96},{64,128},{96,160},{128,192},{160,224},{192,256},{22... | collective-permute-start | bytes 196616 | tf_op jit(solution)/shard_map/ppermute | solution.py:160
  50.5 0.7 copy-start
  108.9 3.5 %copy-start.1 = (f32[96,96]{1,0:T(8,128)S(1)}, f32[96,96]{1,0:T(8,128)}, u32[]{:S(2)}) copy-start(f32[96,96]{1,0:T(8,128)} %get-tuple-element.5) | copy-start | bytes 110596
  108.9 10.8 %all-to-all-start.5 = ((bf16[8,12,8,128]{3,2,1,0:T(8,128)(2,1)}), bf16[8,12,8,128]{3,2,1,0:T(8,128)(2,1)S(1)}, u32[]{:S(2)}, u32[]{:S(2)}) async-start(bf16[8,12,8,128]{3,2,1,0:T(8,128)(2,1)} %get-tuple-element.4), calls=%async_computation.5 | async-start | bytes 393216 | tf_op jit(solution)/shard_map/all_to_all | solution.py:276

commit v4 on v2

v4 whole, which is shorter than its diff:
```python
import functools
import math

import jax
import jax.numpy as jnp
from jax import lax
from jax.experimental import pallas as pl
from jax.experimental.pallas import tpu as pltpu
from jax.sharding import Mesh, PartitionSpec as P

DEGREE = 4
ROOTS = (0.0, 0.7745967, 1.0, 1.3416408)
REACH = DEGREE + 1
SUBLANES = 8
UNROLL = 4

AXES = ("z", "xl", "core", "xh", "y")
GROUP = ("xl", "core")
MODE = ("xh", "y")
LAYER = ("xh", "y", "xl", "core")


def filter_kernel(bounds, odd_z, own, pair, other, far_pair, far_other, out, even, odd, weak_even, weak_odd, strong, degree):
    planes, height, width = degree.shape
    local = even.shape[1]
    rows = out.shape[3]
    low, high = bounds[0], bounds[1]
    centre = 0.5 * (high + low)
    scale = 1.0 / (0.5 * (high - low))
    inner = pl.ds(SUBLANES, height)
    lane = lax.broadcasted_iota(jnp.int32, (height, width), 1)

    def beside(ref, *index):
        value = ref[(*index, inner)]
        up = ref[(*index, pl.ds(SUBLANES - 1, height))]
        down = ref[(*index, pl.ds(SUBLANES + 1, height))]
        left = jnp.where(lane == 0, 0.0, pltpu.roll(value, 1, 1))
        right = jnp.where(lane == width - 1, 0.0, pltpu.roll(value, width - 1, 1))
        return value, (up + down) + (left + right)

    edge = jnp.zeros((SUBLANES, width), jnp.float32)

    def clear(plane, carry):
        for first in (0, SUBLANES + height):
            strong[plane, pl.ds(first, SUBLANES)] = edge
            for mode in range(local):
                weak_even[plane, mode, pl.ds(first, SUBLANES)] = edge
                weak_odd[plane, mode, pl.ds(first, SUBLANES)] = edge
        return carry

    lax.fori_loop(0, planes, clear, 0)

    depth, extra = own.shape[0], far_pair.shape[0]
    side = odd_z[0]
    below, above, farthest = extra, REACH + depth, planes - extra
    for source, start in (
        (own, REACH),
        (pair, jnp.where(side == 0, above, below)),
        (other, jnp.where(side == 0, below, above)),
        (far_pair, jnp.where(side == 0, farthest, 0)),
        (far_other, jnp.where(side == 0, 0, farthest)),
    ):
        count = source.shape[0]

        def load(index, carry, source=source, start=start):
            label = source[index, local].astype(jnp.float32)
            root = jnp.where(label == 1.0, ROOTS[1], 0.0)
            root = jnp.where(label == 2.0, ROOTS[2], root)
            root = jnp.where(label == 3.0, ROOTS[3], root)
            strong[start + index, inner] = root
            for mode in range(local):
                value = jnp.where(label > 0.0, source[index, mode].astype(jnp.float32), 0.0)
                even[start + index, mode] = value
                weak_even[start + index, mode, inner] = root * value
            return carry

        lax.fori_loop(0, count, load, 0, unroll=min(count, UNROLL))

    def weigh(plane, carry):
        root, around = beside(strong, plane)
        degree[plane] = root * (strong[plane - 1, inner] + strong[plane + 1, inner] + around)
        return carry

    lax.fori_loop(1, planes - 1, weigh, 0, unroll=UNROLL)

    cur, prev, weak, weak_next = even, odd, weak_even, weak_odd
    for step in range(DEGREE):
        factor = scale if step == 0 else 2.0 * scale

        def advance(plane, carry, cur=cur, prev=prev, weak=weak, weak_next=weak_next, factor=factor, step=step):
            root = strong[plane, inner]
            here = (degree[plane] - centre) * factor
            there = root * factor
            for mode in range(local):
                _, around = beside(weak, plane, mode)
                around = around + (weak[plane - 1, mode, inner] + weak[plane + 1, mode, inner])
                value = here * cur[plane, mode] - there * around
                if step > 0:
                    value = value - prev[plane, mode]
                prev[plane, mode] = value
                weak_next[plane, mode, inner] = root * value
            return carry

        lax.fori_loop(step + 1, planes - step - 1, advance, 0, unroll=UNROLL)
        cur, prev = prev, cur
        weak, weak_next = weak_next, weak

    def finish(index, carry):
        plane = REACH + index
        root, heavy = strong[plane, inner], degree[plane]
        for mode in range(local):
            value = cur[plane, mode]
            _, around = beside(weak, plane, mode)
            around = around + (weak[plane - 1, mode, inner] + weak[plane + 1, mode, inner])
            image = heavy * value - root * around
            out[:, index, mode] = value.reshape(-1, rows, width).astype(out.dtype)
            out[:, index, local + mode] = image.reshape(-1, rows, width).astype(out.dtype)
        return carry

    lax.fori_loop(0, own.shape[0], finish, 0, unroll=2)

def filtered_and_applied(bounds, odd_z, own, pair, other, far_pair, far_other, blocks):
    depth, fields, height, width = own.shape
    local = fields - 1
    planes = depth + 2 * REACH
    field = pltpu.VMEM((planes, local, height, width), jnp.float32)
    rimmed = pltpu.VMEM((planes, local, height + 2 * SUBLANES, width), jnp.float32)
    root = pltpu.VMEM((planes, height + 2 * SUBLANES, width), jnp.float32)
    degree = pltpu.VMEM((planes, height, width), jnp.float32)
    vmem = pl.BlockSpec(memory_space=pltpu.VMEM)
    return pl.pallas_call(
        filter_kernel,
        out_shape=jax.ShapeDtypeStruct((blocks, depth, 2 * local, height // blocks, width), jnp.bfloat16),
        in_specs=[pl.BlockSpec(memory_space=pltpu.SMEM)] * 2 + [vmem] * 5,
        out_specs=vmem,
        scratch_shapes=[field, field, rimmed, rimmed, root, degree],
        compiler_params=pltpu.CompilerParams(vmem_limit_bytes=40 * 1024 * 1024),
        name="chebyshev_filter",
    )(bounds, odd_z, own, pair, other, far_pair, far_other)


def pack_kernel(block, labels, out):
    group, fields = out.shape[:2]
    local = fields - 1
    tags = labels[0].astype(jnp.float32).astype(out.dtype)
    for peer in range(group):
        for mode in range(local):
            out[peer, mode] = block[peer * local + mode, 0]
        out[peer, local] = tags


def packed(block, labels, group):
    share, _, height, width = block.shape
    vmem = pl.BlockSpec(memory_space=pltpu.VMEM)
    return pl.pallas_call(
        pack_kernel,
        out_shape=jax.ShapeDtypeStruct((group, share // group + 1, height, width), block.dtype),
        in_specs=[vmem, vmem],
        out_specs=vmem,
        name="pack",
    )(block, labels)


def traded(value, step):
    size = lax.axis_size("z")
    pairs = [(z, z + step(z)) for z in range(size) if 0 <= z + step(z) < size]
    return lax.ppermute(value, "z", pairs)


def summed_over_z(value):
    copies = jnp.broadcast_to(value, (lax.axis_size("z"),) + value.shape)
    return jnp.sum(lax.all_to_all(copies, "z", 0, 0, tiled=True), axis=0)


def total_over_all(partial):
    rows, columns = partial.shape
    peers = lax.axis_size(LAYER)
    chunk = 8
    padded = jnp.pad(partial, ((0, peers * chunk - rows), (0, 0))).reshape(peers, chunk, columns)
    terms = lax.all_to_all(padded, LAYER, 0, 0, tiled=True)
    mine = summed_over_z(jnp.sum(terms, axis=0))
    whole = lax.all_to_all(jnp.broadcast_to(mine, (peers, chunk, columns)), LAYER, 0, 0, tiled=True)
    return whole


def turn_kernel(scale, whole, filtered, inverse, turned, staged):
    size = inverse.shape[0]
    rows = turned.shape[2]
    groups = size // SUBLANES
    tile = (SUBLANES, size)
    sub = lax.broadcasted_iota(jnp.int32, tile, 0)
    lane = lax.broadcasted_iota(jnp.int32, tile, 1)
    left = [whole[g] for g in range(groups)]
    right = [jnp.where(lane == sub + SUBLANES * g, 1.0, 0.0) for g in range(groups)]

    def row_of(value, t):
        return jnp.broadcast_to(value[t : t + 1, :], tile)

    for b in range(groups):
        first = SUBLANES * b
        columns = [
            [jnp.broadcast_to(left[g][:, first + t : first + t + 1], tile) for g in range(b, groups)]
            for t in range(SUBLANES)
        ]
        diagonal = jnp.ones(tile, jnp.float32)
        for t in range(SUBLANES):
            pivot = row_of(columns[t][0], t)
            diagonal = jnp.where(sub == t, pivot, diagonal)
            part = 1.0 / pivot
            row_left = row_of(left[b], t) * part
            row_right = row_of(right[b], t) * part
            rest = range(t + 1, SUBLANES)
            row_columns = [row_of(columns[s][0], t) * part for s in rest]
            for g in range(b, groups):
                weight = columns[t][g - b]
                if g == b:
                    weight = jnp.where(sub > t, weight, 0.0)
                left[g] = left[g] - weight * row_left
                right[g] = right[g] - weight * row_right
                for s, row_column in zip(rest, row_columns):
                    columns[s][g - b] = columns[s][g - b] - weight * row_column
        inverse[first : first + SUBLANES, :] = right[b] * lax.rsqrt(diagonal)

    rotation = inverse[...].astype(jnp.bfloat16)
    product = jnp.dot(rotation, filtered[...], preferred_element_type=jnp.float32) * scale
    width = turned.shape[3]
    for row in range(rows):
        staged[pl.ds(row, size, stride=rows), :] = product[:, row * width : (row + 1) * width]
    turned[...] = staged[...].reshape(turned.shape).astype(turned.dtype)


def inverse_and_turned(whole, filtered, scale, peers, rows):
    size = whole.shape[2]
    width = filtered.shape[1] // rows
    vmem = pl.BlockSpec(memory_space=pltpu.VMEM)
    return pl.pallas_call(
        functools.partial(turn_kernel, scale),
        out_shape=(
            jax.ShapeDtypeStruct((size, size), jnp.float32),
            jax.ShapeDtypeStruct((peers, size // peers, rows, width), jnp.bfloat16),
        ),
        in_specs=[vmem, vmem],
        out_specs=(vmem, vmem),
        scratch_shapes=[pltpu.VMEM((size * rows, width), jnp.float32)],
        name="inverse_and_turned",
    )(whole, filtered)


def projection(inverse, cross):
    return jnp.dot(
        jnp.dot(inverse, cross, precision=lax.Precision.HIGHEST),
        inverse.T,
        precision=lax.Precision.HIGHEST,
    )


def per_device(initial_block, labels, filter_low, filter_high):
    share, _, height, width = initial_block.shape
    group, blocks = lax.axis_size(GROUP), lax.axis_size(MODE)
    local = share // group
    modes = share * blocks
    rows = height // blocks
    scale = math.sqrt(height * width * group * lax.axis_size("z"))

    own = lax.all_to_all(packed(initial_block, labels, group), GROUP, 0, 0, tiled=True)
    extra = REACH - group
    odd_z = lax.axis_index("z") % 2
    pair = traded(own, lambda z: 1 - 2 * (z % 2))
    other = traded(own, lambda z: 2 * (z % 2) - 1)
    far_pair = traded(lax.dynamic_slice_in_dim(own, odd_z * (group - extra), extra), lambda z: 4 * (z % 2) - 2)
    far_other = traded(lax.dynamic_slice_in_dim(own, (1 - odd_z) * (group - extra), extra), lambda z: 2 - 4 * (z % 2))

    bounds = jnp.stack([filter_low, filter_high])
    side = jnp.reshape(odd_z, (1,)).astype(jnp.int32)
    both = filtered_and_applied(bounds, side, own, pair, other, far_pair, far_other, blocks)
    both = both.reshape(blocks * group, 2 * local, rows, width)

    both = lax.all_to_all(both, LAYER, 0, 0, tiled=True)
    filtered = both[:, :local].reshape(modes, rows * width)
    applied = both[:, local:].reshape(modes, rows * width)
    both = jnp.concatenate([filtered, applied], axis=0)
    partial = jnp.einsum("mc,nc->mn", both, filtered, preferred_element_type=jnp.float32)
    total = total_over_all(partial)
    inverse, turned = inverse_and_turned(total, filtered, scale, blocks, rows)
    cross = total.reshape(-1, modes)[modes : 2 * modes].T
    projected = projection(inverse, cross)
    turned = lax.all_to_all(turned, MODE, 0, 0, tiled=True)
    modes_out = jnp.transpose(turned, (1, 0, 2, 3)).reshape(share, 1, height, width)
    return (modes_out, projected)


def solution(mesh):
    devices = mesh.devices
    slabs, modes = devices.shape
    fine = Mesh(devices.reshape(slabs // 4, 2, 2, 2, modes // 2), AXES)
    placed = (P(MODE, ("z",) + GROUP, None, None), P(("z",) + GROUP, None, None), P(), P())
    return jax.shard_map(
        per_device,
        mesh=fine,
        in_specs=placed,
        out_specs=(P(MODE, ("z",) + GROUP, None, None), P()),
        check_vma=False,
    )
```

time: 125 us -> 122 us (0.976)
  blocking collectives: 67.8 us -> 81.8 us
  starting transfers between devices: 25.2 us -> 12.6 us
  other arithmetic: 2.56 us -> 0.14 us
    all_to_all x1 -> x2, blocking collectives: 15.2 us -> 34.7 us  [the longest x1 19.5 us: per_device(): both = lax.all_to_all(both, LAYER, 0, 0, tiled=True)]
    all_to_all x1 -> x0, starting transfers between devices: 10.2 us -> none  [per_device(): lax.all_to_all(jnp.concatenate([fields, tags], axis=1), GROUP, 0, 0, tile...]
    all_to_all x1, blocking collectives: 27.9 us -> 22.1 us  [summed_over_z(): return jnp.sum(lax.all_to_all(copies, 'z', 0, 0, tiled=True), axis=0)]
    ppermute x4, waiting for transfers between devices: 1.24 us -> 5.18 us  [traded(): return lax.ppermute(value, 'z', pairs)]
    all_to_all x1 -> x0, waiting for transfers between devices: 3.87 us -> none  [per_device(): lax.all_to_all(jnp.concatenate([fields, tags], axis=1), GROUP, 0, 0, tile...]
    ppermute x4, starting transfers between devices: 11.5 us -> 9.11 us  [traded(): return lax.ppermute(value, 'z', pairs)]
    pallas_call x1, Pallas kernels: 6.99 us -> 4.73 us  [filtered_and_applied(): pl.pallas_call(filter_kernel, out_shape=jax.ShapeDtypeStruct((blocks, dep...]
    pallas_call x1 -> x2, Pallas kernels: 4.26 us -> 6.36 us  [the longest x1 4.71 us: inverse_and_turned(): pl.pallas_call(functools.partial(turn_kernel, scale), out_shape=(jax.Shap...]
  transfers between devices with their start and end apart: 6 -> 5, of which waited for: 4 -> 2; matrix products, arithmetic and copies ran while one was open for 1% -> 2% of each run, Pallas kernels for 0% -> 0%
where the time goes in v4:
time: 122 us
  blocking collectives  81.8 us (67%)
  starting transfers between devices  12.6 us (10%)
  Pallas kernels  11.1 us (9%)
  waiting for transfers between devices  10.5 us (9%)
  matrix products  2.12 us (2%)
  between operations  2.06 us (2%)
  local copies, waits for them, and re-layouts  1.27 us (1%)
    all_to_all x1, blocking collectives, summed_over_z(): return jnp.sum(lax.all_to_all(copies, 'z', 0, 0, tiled=True), axis=0)  22.1 us
    all_to_all x1, blocking collectives, per_device(): both = lax.all_to_all(both, LAYER, 0, 0, tiled=True)  19.5 us
    all_to_all x1, blocking collectives, per_device(): lax.all_to_all(packed(initial_block, labels, group), GROUP, 0, 0, tiled=T...  15.2 us
    all_to_all x1, blocking collectives, total_over_all(): lax.all_to_all(jnp.broadcast_to(mine, (peers, chunk, columns)), LAYER, 0,...  13.2 us
    all_to_all x1, blocking collectives, total_over_all(): terms = lax.all_to_all(padded, LAYER, 0, 0, tiled=True)  11.8 us
    ppermute x4, starting transfers between devices, traded(): return lax.ppermute(value, 'z', pairs)  9.11 us
    all_to_all x1, waiting for transfers between devices, per_device(): turned = lax.all_to_all(turned, MODE, 0, 0, tiled=True)  5.34 us
    ppermute x4, waiting for transfers between devices, traded(): return lax.ppermute(value, 'z', pairs)  5.18 us
  transfers between devices with their start and end apart: 5, of which 2 were waited for; matrix products, arithmetic and copies ran while one was open for 2% of the time, Pallas kernels for 0%

profile of v4, /device:TPU:1, one launch (start us, length us, event | category | flops | bytes accessed | tf_op | source)
XLA Modules:
  0.0 121.6 jit_solution(5269095093807140371)
XLA Ops:
  0.6 1.7 %pack.1 = bf16[4,4,64,128]{3,2,1,0:T(8,128)(2,1)} custom-call(bf16[12,1,64,128]{3,2,1,0:T(8,128)(2,1)} %block.1, s32[1,64,128]{2,1,0:T(8,128)} %labels.1), custom_call_target="tpu_custom_call" | custom-call | tf_op jit(solution)/shard_map/pack/pallas_call | solution.py:155
  2.3 15.2 %all_to_all.30.own = bf16[4,4,64,128]{3,2,1,0:T(8,128)(2,1)S(1)} all-to-all(bf16[4,4,64,128]{3,2,1,0:T(8,128)(2,1)} %pack.1), channel_id=1, replica_groups=mesh['z'=16,'xl'=2,'core'=2,'xh'=2,'y'=4] {'xl','core'}, dimensions={0} | all-to-all | bytes 524288 | tf_op jit(solution)/shard_map/all_to_all | solution.py:265
  17.5 0.7 collective-permute-start.1
  18.2 1.9 %collective-permute-start = (bf16[4,4,64,128]{3,2,1,0:T(8,128)(2,1)S(1)}, bf16[4,4,64,128]{3,2,1,0:T(8,128)(2,1)S(1)}, u32[]{:S(2)}, u32[]{:S(2)}) collective-permute-start(bf16[4,4,64,128]{3,2,1,0:T(8,128)(2,1)S(1)} %all_to_all.30.own), channel_id=1, source_target_pairs={{0,32},{32,0},{64,96},{96,64},{128,160},{160,128},{192,224},{224,1... | collective-permute-start | bytes 786440 | tf_op jit(solution)/shard_map/ppermute | solution.py:167
  21.5 5.2 %collective-permute-start.3 = (bf16[1,4,64,128]{3,2,1,0:T(8,128)(2,1)S(1)}, bf16[1,4,64,128]{3,2,1,0:T(8,128)(2,1)S(1)}, u32[]{:S(2)}, u32[]{:S(2)}) collective-permute-start(bf16[1,4,64,128]{3,2,1,0:T(8,128)(2,1)S(1)} %get-tuple-element.12), channel_id=1, source_target_pairs={{0,64},{64,128},{96,32},{128,192},{160,96},{192,256},{224,160},{25... | collective-permute-start | bytes 196616 | tf_op jit(solution)/shard_map/ppermute | solution.py:167
  26.7 1.3 %collective-permute-start.2 = (bf16[1,4,64,128]{3,2,1,0:T(8,128)(2,1)S(1)}, bf16[1,4,64,128]{3,2,1,0:T(8,128)(2,1)S(1)}, u32[]{:S(2)}, u32[]{:S(2)}) collective-permute-start(bf16[1,4,64,128]{3,2,1,0:T(8,128)(2,1)S(1)} %get-tuple-element.13), channel_id=1, source_target_pairs={{32,96},{64,0},{96,160},{128,64},{160,224},{192,128},{224,288},{25... | collective-permute-start | bytes 196616 | tf_op jit(solution)/shard_map/ppermute | solution.py:167
  28.0 0.1 pad_maximum_fusion.bounds
  28.1 0.0 collective-permute-done.3.far_other
  28.1 5.2 %collective-permute-done.2.far_pair = bf16[1,4,64,128]{3,2,1,0:T(8,128)(2,1)S(1)} collective-permute-done((bf16[1,4,64,128]{3,2,1,0:T(8,128)(2,1)S(1)}, bf16[1,4,64,128]{3,2,1,0:T(8,128)(2,1)S(1)}, u32[]{:S(2)}, u32[]{:S(2)}) %collective-permute-start.2) | collective-permute-done | bytes 65568 | tf_op jit(solution)/shard_map/ppermute | solution.py:167
  33.3 0.0 collective-permute-done.1.other
  33.3 0.0 collective-permute-done.pair
  33.3 4.7 %chebyshev_filter.1 = bf16[8,4,6,8,128]{4,3,2,1,0:T(8,128)(2,1)S(1)} custom-call(f32[2]{0:T(128)S(1)} %pad_maximum_fusion.bounds, s32[1]{0:T(128)} %bitcast.2.odd_z, bf16[4,4,64,128]{3,2,1,0:T(8,128)(2,1)S(1)} %all_to_all.30.own, bf16[4,4,64,128]{3,2,1,0:T(8,128)(2,1)S(1)} %collective-permute-done.pair, ...), custom_call_target="tpu_custom_call" | custom-call | tf_op jit(solution)/shard_map/chebyshev_filter/pallas_call | solution.py:131
  38.0 19.5 %all_to_all.31 = bf16[32,6,8,128]{3,2,1,0:T(8,128)(2,1)S(1)} all-to-all(bf16[32,6,8,128]{3,2,1,0:T(8,128)(2,1)S(1)} %bitcast.30), channel_id=1, replica_groups=mesh['z'=16,'xl'=2,'core'=2,'xh'=2,'y'=4] {'xh','y','xl','core'}, dimensions={0} | all-to-all | bytes 786432 | tf_op jit(solution)/shard_map/all_to_all | solution.py:278
  57.5 0.1 copy_bitcast_fusion
  57.6 0.0 copy-start
  57.6 0.3 fusion
  57.9 0.4 copy-done
  58.3 11.8 %all_to_all.32 = f32[32,8,96]{2,1,0:T(8,128)S(1)} all-to-all(f32[32,8,96]{2,1,0:T(8,128)S(1)} %pad_bitcast_fusion), channel_id=1, replica_groups=mesh['z'=16,'xl'=2,'core'=2,'xh'=2,'y'=4] {'xh','y','xl','core'}, dimensions={0} | all-to-all | bytes 196608 | tf_op jit(solution)/shard_map/all_to_all | solution.py:180
  70.1 22.1 %all_to_all.33 = f32[16,8,96]{2,1,0:T(8,128)S(1)} all-to-all(f32[16,8,96]{2,1,0:T(8,128)S(1)} %broadcast_in_dim.6), channel_id=1, replica_groups=mesh['z'=16,'xl'=2,'core'=2,'xh'=2,'y'=4] {'z'}, dimensions={0} | all-to-all | bytes 98304 | tf_op jit(solution)/shard_map/all_to_all | solution.py:172
  92.2 13.2 %all_to_all.34.whole = f32[32,8,96]{2,1,0:T(8,128)} all-to-all(f32[32,8,96]{2,1,0:T(8,128)S(1)} %broadcast_in_dim.7), channel_id=1, replica_groups=mesh['z'=16,'xl'=2,'core'=2,'xh'=2,'y'=4] {'xh','y','xl','core'}, dimensions={0} | all-to-all | bytes 196608 | tf_op jit(solution)/shard_map/all_to_all | solution.py:182
  105.4 4.7 %inverse_and_turned.1 = (f32[96,96]{1,0:T(8,128)}, bf16[8,12,8,128]{3,2,1,0:T(8,128)(2,1)}) custom-call(f32[32,8,96]{2,1,0:T(8,128)} %all_to_all.34.whole, bf16[96,1024]{1,0:T(8,128)(2,1)} %copy-done), custom_call_target="tpu_custom_call" | custom-call | tf_op jit(solution)/shard_map/inverse_and_turned/pallas_call | solution.py:236
  110.1 0.0 copy-start.1
  110.1 3.5 %all-to-all-start.5 = ((bf16[8,12,8,128]{3,2,1,0:T(8,128)(2,1)}), bf16[8,12,8,128]{3,2,1,0:T(8,128)(2,1)S(1)}, u32[]{:S(2)}, u32[]{:S(2)}) async-start(bf16[8,12,8,128]{3,2,1,0:T(8,128)(2,1)} %get-tuple-element.4), calls=%async_computation.5 | async-start | bytes 393216 | tf_op jit(solution)/shard_map/all_to_all | solution.py:287
  113.7 0.0 copy-done.1
  113.7 1.0 fusion.4
  114.7 0.8 fusion.7
  115.5 5.3 %all-to-all-done.5 = bf16[8,12,8,128]{3,2,1,0:T(8,128)(2,1)S(1)} async-done(((bf16[8,12,8,128]{3,2,1,0:T(8,128)(2,1)}), bf16[8,12,8,128]{3,2,1,0:T(8,128)(2,1)S(1)}, u32[]{:S(2)}, u32[]{:S(2)}) %all-to-all-start.5) | async-done | bytes 196640 | tf_op jit(solution)/shard_map/all_to_all | solution.py:287
  120.9 0.7 copy_bitcast_fusion.2
  (7 shorter events, 0.1 us)
Async XLA Ops:
  17.5 15.7 %collective-permute-start.1 = (bf16[4,4,64,128]{3,2,1,0:T(8,128)(2,1)S(1)}, bf16[4,4,64,128]{3,2,1,0:T(8,128)(2,1)S(1)}, u32[]{:S(2)}, u32[]{:S(2)}) collective-permute-start(bf16[4,4,64,128]{3,2,1,0:T(8,128)(2,1)S(1)} %all_to_all.30.own), channel_id=1, source_target_pairs={{32,64},{64,32},{96,128},{128,96},{160,192},{192,160},{224,256},{2... | collective-permute-start | bytes 786440 | tf_op jit(solution)/shard_map/ppermute | solution.py:167
  18.2 15.1 %collective-permute-start = (bf16[4,4,64,128]{3,2,1,0:T(8,128)(2,1)S(1)}, bf16[4,4,64,128]{3,2,1,0:T(8,128)(2,1)S(1)}, u32[]{:S(2)}, u32[]{:S(2)}) collective-permute-start(bf16[4,4,64,128]{3,2,1,0:T(8,128)(2,1)S(1)} %all_to_all.30.own), channel_id=1, source_target_pairs={{0,32},{32,0},{64,96},{96,64},{128,160},{160,128},{192,224},{224,1... | collective-permute-start | bytes 786440 | tf_op jit(solution)/shard_map/ppermute | solution.py:167
  21.5 6.6 %collective-permute-start.3 = (bf16[1,4,64,128]{3,2,1,0:T(8,128)(2,1)S(1)}, bf16[1,4,64,128]{3,2,1,0:T(8,128)(2,1)S(1)}, u32[]{:S(2)}, u32[]{:S(2)}) collective-permute-start(bf16[1,4,64,128]{3,2,1,0:T(8,128)(2,1)S(1)} %get-tuple-element.12), channel_id=1, source_target_pairs={{0,64},{64,128},{96,32},{128,192},{160,96},{192,256},{224,160},{25... | collective-permute-start | bytes 196616 | tf_op jit(solution)/shard_map/ppermute | solution.py:167
  26.7 6.5 %collective-permute-start.2 = (bf16[1,4,64,128]{3,2,1,0:T(8,128)(2,1)S(1)}, bf16[1,4,64,128]{3,2,1,0:T(8,128)(2,1)S(1)}, u32[]{:S(2)}, u32[]{:S(2)}) collective-permute-start(bf16[1,4,64,128]{3,2,1,0:T(8,128)(2,1)S(1)} %get-tuple-element.13), channel_id=1, source_target_pairs={{32,96},{64,0},{96,160},{128,64},{160,224},{192,128},{224,288},{25... | collective-permute-start | bytes 196616 | tf_op jit(solution)/shard_map/ppermute | solution.py:167
  57.6 0.7 copy-start
  110.1 3.5 %copy-start.1 = (f32[96,96]{1,0:T(8,128)S(1)}, f32[96,96]{1,0:T(8,128)}, u32[]{:S(2)}) copy-start(f32[96,96]{1,0:T(8,128)} %get-tuple-element.5) | copy-start | bytes 110596
  110.1 10.8 %all-to-all-start.5 = ((bf16[8,12,8,128]{3,2,1,0:T(8,128)(2,1)}), bf16[8,12,8,128]{3,2,1,0:T(8,128)(2,1)S(1)}, u32[]{:S(2)}, u32[]{:S(2)}) async-start(bf16[8,12,8,128]{3,2,1,0:T(8,128)(2,1)} %get-tuple-element.4), calls=%async_computation.5 | async-start | bytes 393216 | tf_op jit(solution)/shard_map/all_to_all | solution.py:287

commit v5 on v4

--- a/solution.py
+++ b/solution.py
@@ -11,7 +11,7 @@
 DEGREE = 4
 ROOTS = (0.0, 0.7745967, 1.0, 1.3416408)
 REACH = DEGREE + 1
-SUBLANES = 8
+SUBLANES, LANES = 8, 128
 UNROLL = 4
 
 AXES = ("z", "xl", "core", "xh", "y")
@@ -20,7 +20,7 @@
 LAYER = ("xh", "y", "xl", "core")
 
 
-def filter_kernel(bounds, odd_z, own, pair, other, far_pair, far_other, out, even, odd, weak_even, weak_odd, strong, degree):
+def filter_kernel(bounds, far_lo, lo, own, hi, far_hi, out, even, odd, weak_even, weak_odd, strong, degree):
     planes, height, width = degree.shape
     local = even.shape[1]
     rows = out.shape[3]
@@ -50,16 +50,8 @@
 
     lax.fori_loop(0, planes, clear, 0)
 
-    depth, extra = own.shape[0], far_pair.shape[0]
-    side = odd_z[0]
-    below, above, farthest = extra, REACH + depth, planes - extra
-    for source, start in (
-        (own, REACH),
-        (pair, jnp.where(side == 0, above, below)),
-        (other, jnp.where(side == 0, below, above)),
-        (far_pair, jnp.where(side == 0, farthest, 0)),
-        (far_other, jnp.where(side == 0, 0, farthest)),
-    ):
+    start = 0
+    for source in (far_lo, lo, own, hi, far_hi):
         count = source.shape[0]
 
         def load(index, carry, source=source, start=start):
@@ -75,6 +67,7 @@
             return carry
 
         lax.fori_loop(0, count, load, 0, unroll=min(count, UNROLL))
+        start += count
 
     def weigh(plane, carry):
         root, around = beside(strong, plane)
@@ -119,7 +112,7 @@
 
     lax.fori_loop(0, own.shape[0], finish, 0, unroll=2)
 
-def filtered_and_applied(bounds, odd_z, own, pair, other, far_pair, far_other, blocks):
+def filtered_and_applied(bounds, far_lo, lo, own, hi, far_hi, blocks):
     depth, fields, height, width = own.shape
     local = fields - 1
     planes = depth + 2 * REACH
@@ -131,12 +124,12 @@
     return pl.pallas_call(
         filter_kernel,
         out_shape=jax.ShapeDtypeStruct((blocks, depth, 2 * local, height // blocks, width), jnp.bfloat16),
-        in_specs=[pl.BlockSpec(memory_space=pltpu.SMEM)] * 2 + [vmem] * 5,
+        in_specs=[pl.BlockSpec(memory_space=pltpu.SMEM)] + [vmem] * 5,
         out_specs=vmem,
         scratch_shapes=[field, field, rimmed, rimmed, root, degree],
         compiler_params=pltpu.CompilerParams(vmem_limit_bytes=40 * 1024 * 1024),
         name="chebyshev_filter",
-    )(bounds, odd_z, own, pair, other, far_pair, far_other)
+    )(bounds, far_lo, lo, own, hi, far_hi)
 
 
 def pack_kernel(block, labels, out):
@@ -161,10 +154,10 @@
     )(block, labels)
 
 
-def traded(value, step):
-    size = lax.axis_size("z")
-    pairs = [(z, z + step(z)) for z in range(size) if 0 <= z + step(z) < size]
-    return lax.ppermute(value, "z", pairs)
+def shifted(value, axis, step):
+    size = lax.axis_size(axis)
+    pairs = [(i, i + step) for i in range(size) if 0 <= i + step < size]
+    return lax.ppermute(value, axis, pairs)
 
 
 def summed_over_z(value):
@@ -172,25 +165,97 @@
     return jnp.sum(lax.all_to_all(copies, "z", 0, 0, tiled=True), axis=0)
 
 
+def lanes_of():
+    return lax.broadcasted_iota(jnp.int32, (SUBLANES, LANES), 1)
+
+
+def gram_kernel(filtered, applied, out, wide):
+    size = filtered.shape[0]
+    groups = size // SUBLANES
+    spare = LANES - size
+    full = groups - groups * spare // LANES
+    lane = lanes_of()
+    wide[...] = jnp.zeros(wide.shape, wide.dtype)
+    contract = (((1,), (1,)), ((), ()))
+    for half, source in enumerate((applied, filtered)):
+        product = lax.dot_general(source[...], filtered[...], contract, preferred_element_type=jnp.float32)
+        wide[half * size : (half + 1) * size, :size] = product
+
+    def group_of(half, g):
+        return wide[half * size + SUBLANES * g : half * size + SUBLANES * (g + 1), :]
+
+    pieces = size // spare
+    tiles = []
+    for t in range(full):
+        extra = group_of(0, full + t // pieces)
+        tiles.append(jnp.where(lane < size, group_of(0, t), pltpu.roll(extra, size - spare * (t % pieces), 1)))
+    for g in range(groups // 2):
+        ends = SUBLANES * (g + 1)
+        tiles.append(jnp.where(lane < ends, group_of(1, g), pltpu.roll(group_of(1, groups - 1 - g), ends, 1)))
+    half_rows = out.shape[1]
+    for t, tile in enumerate(tiles):
+        out[2 * t] = tile[:half_rows]
+        out[2 * t + 1] = tile[half_rows:]
+    for rest in range(2 * len(tiles), out.shape[0]):
+        out[rest] = jnp.zeros(out.shape[1:], out.dtype)
+
+
+def packed_terms(filtered, applied, peers):
+    size = filtered.shape[0]
+    vmem = pl.BlockSpec(memory_space=pltpu.VMEM)
+    return pl.pallas_call(
+        gram_kernel,
+        out_shape=jax.ShapeDtypeStruct((peers, SUBLANES // 2, LANES), jnp.float32),
+        in_specs=[vmem, vmem],
+        out_specs=vmem,
+        scratch_shapes=[pltpu.VMEM((2 * size, LANES), jnp.float32)],
+        compiler_params=pltpu.CompilerParams(vmem_limit_bytes=8 * 1024 * 1024),
+        name="packed_terms",
+    )(filtered, applied)
+
+
 def total_over_all(partial):
-    rows, columns = partial.shape
-    peers = lax.axis_size(LAYER)
-    chunk = 8
-    padded = jnp.pad(partial, ((0, peers * chunk - rows), (0, 0))).reshape(peers, chunk, columns)
-    terms = lax.all_to_all(padded, LAYER, 0, 0, tiled=True)
+    terms = lax.all_to_all(partial, LAYER, 0, 0, tiled=True)
     mine = summed_over_z(jnp.sum(terms, axis=0))
-    whole = lax.all_to_all(jnp.broadcast_to(mine, (peers, chunk, columns)), LAYER, 0, 0, tiled=True)
-    return whole
-
-
-def turn_kernel(scale, whole, filtered, inverse, turned, staged):
+    return lax.all_to_all(jnp.broadcast_to(mine, partial.shape), LAYER, 0, 0, tiled=True)
+
+
+def turn_kernel(scale, whole, filtered, inverse, crossed, turned, staged, square):
     size = inverse.shape[0]
     rows = turned.shape[2]
     groups = size // SUBLANES
-    tile = (SUBLANES, size)
+    spare = LANES - size
+    full = groups - groups * spare // LANES
+    pieces = size // spare
+    tile = (SUBLANES, LANES)
     sub = lax.broadcasted_iota(jnp.int32, tile, 0)
-    lane = lax.broadcasted_iota(jnp.int32, tile, 1)
-    left = [whole[g] for g in range(groups)]
+    lane = lanes_of()
+    tiles = [jnp.concatenate([whole[2 * t], whole[2 * t + 1]], axis=0) for t in range(full + groups // 2)]
+
+    for g in range(full):
+        crossed[SUBLANES * g : SUBLANES * (g + 1), :] = tiles[g][:, :size]
+    for g in range(full, groups):
+        first = pieces * (g - full)
+        value = pltpu.roll(tiles[first], spare, 1)
+        for p in range(1, pieces):
+            value = jnp.where(lane < spare * p, value, pltpu.roll(tiles[first + p], spare * (p + 1), 1))
+        crossed[SUBLANES * g : SUBLANES * (g + 1), :] = value[:, :size]
+
+    square[...] = jnp.zeros(square.shape, square.dtype)
+    for g in range(groups // 2):
+        ends = SUBLANES * (g + 1)
+        last = groups - 1 - g
+        square[SUBLANES * g : ends, :] = tiles[full + g]
+        square[SUBLANES * last : SUBLANES * (last + 1), :] = pltpu.roll(tiles[full + g], LANES - ends, 1)
+    mirrored = square[...].T
+    left = [
+        jnp.where(
+            lane < SUBLANES * (g + 1),
+            square[SUBLANES * g : SUBLANES * (g + 1), :],
+            mirrored[SUBLANES * g : SUBLANES * (g + 1), :],
+        )
+        for g in range(groups)
+    ]
     right = [jnp.where(lane == sub + SUBLANES * g, 1.0, 0.0) for g in range(groups)]
 
     def row_of(value, t):
@@ -219,7 +284,7 @@
                 right[g] = right[g] - weight * row_right
                 for s, row_column in zip(rest, row_columns):
                     columns[s][g - b] = columns[s][g - b] - weight * row_column
-        inverse[first : first + SUBLANES, :] = right[b] * lax.rsqrt(diagonal)
+        inverse[first : first + SUBLANES, :] = (right[b] * lax.rsqrt(diagonal))[:, :size]
 
     rotation = inverse[...].astype(jnp.bfloat16)
     product = jnp.dot(rotation, filtered[...], preferred_element_type=jnp.float32) * scale
@@ -230,18 +295,17 @@
 
 
 def inverse_and_turned(whole, filtered, scale, peers, rows):
-    size = whole.shape[2]
+    size = filtered.shape[0]
     width = filtered.shape[1] // rows
     vmem = pl.BlockSpec(memory_space=pltpu.VMEM)
+    matrix = jax.ShapeDtypeStruct((size, size), jnp.float32)
     return pl.pallas_call(
         functools.partial(turn_kernel, scale),
-        out_shape=(
-            jax.ShapeDtypeStruct((size, size), jnp.float32),
-            jax.ShapeDtypeStruct((peers, size // peers, rows, width), jnp.bfloat16),
-        ),
+        out_shape=(matrix, matrix, jax.ShapeDtypeStruct((peers, size // peers, rows, width), jnp.bfloat16)),
         in_specs=[vmem, vmem],
-        out_specs=(vmem, vmem),
-        scratch_shapes=[pltpu.VMEM((size * rows, width), jnp.float32)],
+        out_specs=(vmem, vmem, vmem),
+        scratch_shapes=[pltpu.VMEM((size * rows, width), jnp.float32), pltpu.VMEM((LANES, LANES), jnp.float32)],
+        compiler_params=pltpu.CompilerParams(vmem_limit_bytes=8 * 1024 * 1024),
         name="inverse_and_turned",
     )(whole, filtered)
 
@@ -264,26 +328,19 @@
 
     own = lax.all_to_all(packed(initial_block, labels, group), GROUP, 0, 0, tiled=True)
     extra = REACH - group
-    odd_z = lax.axis_index("z") % 2
-    pair = traded(own, lambda z: 1 - 2 * (z % 2))
-    other = traded(own, lambda z: 2 * (z % 2) - 1)
-    far_pair = traded(lax.dynamic_slice_in_dim(own, odd_z * (group - extra), extra), lambda z: 4 * (z % 2) - 2)
-    far_other = traded(lax.dynamic_slice_in_dim(own, (1 - odd_z) * (group - extra), extra), lambda z: 2 - 4 * (z % 2))
+    lo, hi = shifted(own, "z", 1), shifted(own, "z", -1)
+    far_lo, far_hi = shifted(own[group - extra :], "z", 2), shifted(own[:extra], "z", -2)
 
     bounds = jnp.stack([filter_low, filter_high])
-    side = jnp.reshape(odd_z, (1,)).astype(jnp.int32)
-    both = filtered_and_applied(bounds, side, own, pair, other, far_pair, far_other, blocks)
-    both = both.reshape(blocks * group, 2 * local, rows, width)
-
-    both = lax.all_to_all(both, LAYER, 0, 0, tiled=True)
-    filtered = both[:, :local].reshape(modes, rows * width)
-    applied = both[:, local:].reshape(modes, rows * width)
-    both = jnp.concatenate([filtered, applied], axis=0)
-    partial = jnp.einsum("mc,nc->mn", both, filtered, preferred_element_type=jnp.float32)
-    total = total_over_all(partial)
-    inverse, turned = inverse_and_turned(total, filtered, scale, blocks, rows)
-    cross = total.reshape(-1, modes)[modes : 2 * modes].T
-    projected = projection(inverse, cross)
+    pair = filtered_and_applied(bounds, far_lo, lo, own, hi, far_hi, blocks)
+    pair = pair.reshape(blocks * group, 2 * local, rows, width)
+
+    pair = lax.all_to_all(pair, LAYER, 0, 0, tiled=True)
+    filtered = pair[:, :local].reshape(modes, rows * width)
+    applied = pair[:, local:].reshape(modes, rows * width)
+    total = total_over_all(packed_terms(filtered, applied, blocks * group))
+    inverse, crossed, turned = inverse_and_turned(total, filtered, scale, blocks, rows)
+    projected = projection(inverse, crossed.T)
     turned = lax.all_to_all(turned, MODE, 0, 0, tiled=True)
     modes_out = jnp.transpose(turned, (1, 0, 2, 3)).reshape(share, 1, height, width)
     return (modes_out, projected)

time: 122 us -> 118 us (0.967)
  blocking collectives: 81.8 us -> 66.7 us
  starting transfers between devices: 12.6 us -> 25.1 us
    all_to_all x4 -> x3, blocking collectives: 59.7 us -> 38.9 us  [the longest x1 15.2 us: per_device(): pair = lax.all_to_all(pair, LAYER, 0, 0, tiled=True)]
    all_to_all x0 -> x1, starting transfers between devices: none -> 10.2 us  [per_device(): lax.all_to_all(packed(initial_block, labels, group), GROUP, 0, 0, tiled=T...]
    all_to_all x1, blocking collectives: 22.1 us -> 27.8 us  [summed_over_z(): return jnp.sum(lax.all_to_all(copies, 'z', 0, 0, tiled=True), axis=0)]
    ppermute x4, waiting for transfers between devices: 5.18 us -> 1.24 us  [shifted(): return lax.ppermute(value, axis, pairs)]
    all_to_all x0 -> x1, waiting for transfers between devices: none -> 3.87 us  [per_device(): lax.all_to_all(packed(initial_block, labels, group), GROUP, 0, 0, tiled=T...]
    ppermute x4, starting transfers between devices: 9.11 us -> 11.5 us  [shifted(): return lax.ppermute(value, axis, pairs)]
    pallas_call x1 -> x2, Pallas kernels: 4.71 us -> 4.22 us  [the longest x1 3.86 us: inverse_and_turned(): pl.pallas_call(functools.partial(turn_kernel, scale), out_shape=(matrix,...]
  transfers between devices with their start and end apart: 5 -> 6, of which waited for: 2 -> 4; matrix products, arithmetic and copies ran while one was open for 2% -> 1% of each run, Pallas kernels for 0% -> 0%
where the time goes in v5:
time: 118 us
  blocking collectives  66.7 us (57%)
  starting transfers between devices  25.1 us (21%)
  waiting for transfers between devices  11.3 us (10%)
  Pallas kernels  10.6 us (9%)
  between operations  2.02 us (2%)
    all_to_all x1, blocking collectives, summed_over_z(): return jnp.sum(lax.all_to_all(copies, 'z', 0, 0, tiled=True), axis=0)  27.8 us
    all_to_all x1, blocking collectives, per_device(): pair = lax.all_to_all(pair, LAYER, 0, 0, tiled=True)  15.2 us
    all_to_all x1, blocking collectives, total_over_all(): lax.all_to_all(jnp.broadcast_to(mine, partial.shape), LAYER, 0, 0, tiled=...  12.4 us
    ppermute x4, starting transfers between devices, shifted(): return lax.ppermute(value, axis, pairs)  11.5 us
    all_to_all x1, blocking collectives, total_over_all(): terms = lax.all_to_all(partial, LAYER, 0, 0, tiled=True)  11.4 us
    all_to_all x1, starting transfers between devices, per_device(): lax.all_to_all(packed(initial_block, labels, group), GROUP, 0, 0, tiled=T...  10.2 us
    all_to_all x1, waiting for transfers between devices, per_device(): turned = lax.all_to_all(turned, MODE, 0, 0, tiled=True)  6.15 us
    pallas_call x1, Pallas kernels, filtered_and_applied(): pl.pallas_call(filter_kernel, out_shape=jax.ShapeDtypeStruct((blocks, dep...  4.73 us
  transfers between devices with their start and end apart: 6, of which 4 were waited for; matrix products, arithmetic and copies ran while one was open for 1% of the time, Pallas kernels for 0%

profile of v5, /device:TPU:1, one launch (start us, length us, event | category | flops | bytes accessed | tf_op | source)
XLA Modules:
  0.0 117.8 jit_solution(10827276437652195704)
XLA Ops:
  0.6 1.7 %pack.1 = bf16[4,4,64,128]{3,2,1,0:T(8,128)(2,1)} custom-call(bf16[12,1,64,128]{3,2,1,0:T(8,128)(2,1)} %block.1, s32[1,64,128]{2,1,0:T(8,128)} %labels.1), custom_call_target="tpu_custom_call" | custom-call | tf_op jit(solution)/shard_map/pack/pallas_call | solution.py:148
  2.3 10.2 %all-to-all-start = ((bf16[4,4,64,128]{3,2,1,0:T(8,128)(2,1)}), bf16[4,4,64,128]{3,2,1,0:T(8,128)(2,1)S(1)}, u32[]{:S(2)}, u32[]{:S(2)}) async-start(bf16[4,4,64,128]{3,2,1,0:T(8,128)(2,1)} %pack.1), calls=%async_computation | async-start | bytes 524288 | tf_op jit(solution)/shard_map/all_to_all | solution.py:329
  13.8 3.9 %all-to-all-done.own = bf16[4,4,64,128]{3,2,1,0:T(8,128)(2,1)S(1)} async-done(((bf16[4,4,64,128]{3,2,1,0:T(8,128)(2,1)}), bf16[4,4,64,128]{3,2,1,0:T(8,128)(2,1)S(1)}, u32[]{:S(2)}, u32[]{:S(2)}) %all-to-all-start) | async-done | bytes 262176 | tf_op jit(solution)/shard_map/all_to_all | solution.py:329
  17.7 1.3 %collective-permute-start.2 = (bf16[4,4,64,128]{3,2,1,0:T(8,128)(2,1)S(1)}, bf16[4,4,64,128]{3,2,1,0:T(8,128)(2,1)S(1)}, u32[]{:S(2)}, u32[]{:S(2)}) collective-permute-start(bf16[4,4,64,128]{3,2,1,0:T(8,128)(2,1)S(1)} %all-to-all-done.own), channel_id=1, source_target_pairs={{32,0},{64,32},{96,64},{128,96},{160,128},{192,160},{224,192},{256... | collective-permute-start | bytes 786440 | tf_op jit(solution)/shard_map/ppermute | solution.py:160
  19.0 4.0 %collective-permute-start.1 = (bf16[4,4,64,128]{3,2,1,0:T(8,128)(2,1)S(1)}, bf16[4,4,64,128]{3,2,1,0:T(8,128)(2,1)S(1)}, u32[]{:S(2)}, u32[]{:S(2)}) collective-permute-start(bf16[4,4,64,128]{3,2,1,0:T(8,128)(2,1)S(1)} %all-to-all-done.own), channel_id=1, source_target_pairs={{0,32},{32,64},{64,96},{96,128},{128,160},{160,192},{192,224},{224... | collective-permute-start | bytes 786440 | tf_op jit(solution)/shard_map/ppermute | solution.py:160
  23.0 1.3 %collective-permute-start.3 = (bf16[1,4,64,128]{3,2,1,0:T(8,128)(2,1)S(1)}, bf16[1,4,64,128]{3,2,1,0:T(8,128)(2,1)S(1)}, u32[]{:S(2)}, u32[]{:S(2)}) collective-permute-start(bf16[1,4,64,128]{3,2,1,0:T(8,128)(2,1)S(1)} %get-tuple-element.16), channel_id=1, source_target_pairs={{64,0},{96,32},{128,64},{160,96},{192,128},{224,160},{256,192},{28... | collective-permute-start | bytes 196616 | tf_op jit(solution)/shard_map/ppermute | solution.py:160
  24.3 4.9 %collective-permute-start = (bf16[1,4,64,128]{3,2,1,0:T(8,128)(2,1)S(1)}, bf16[1,4,64,128]{3,2,1,0:T(8,128)(2,1)S(1)}, u32[]{:S(2)}, u32[]{:S(2)}) collective-permute-start(bf16[1,4,64,128]{3,2,1,0:T(8,128)(2,1)S(1)} %get-tuple-element.17), channel_id=1, source_target_pairs={{0,64},{32,96},{64,128},{96,160},{128,192},{160,224},{192,256},{22... | collective-permute-start | bytes 196616 | tf_op jit(solution)/shard_map/ppermute | solution.py:160
  29.2 0.1 pad_maximum_fusion.bounds
  29.3 0.3 collective-permute-done.3.far_hi
  29.6 0.9 collective-permute-done.far_lo
  30.5 0.0 collective-permute-done.2.hi
  30.5 0.0 collective-permute-done.1.lo
  30.5 4.7 %chebyshev_filter.1 = bf16[8,4,6,8,128]{4,3,2,1,0:T(8,128)(2,1)S(1)} custom-call(f32[2]{0:T(128)S(1)} %pad_maximum_fusion.bounds, bf16[1,4,64,128]{3,2,1,0:T(8,128)(2,1)S(1)} %collective-permute-done.far_lo, bf16[4,4,64,128]{3,2,1,0:T(8,128)(2,1)S(1)} %collective-permute-done.1.lo, bf16[4,4,64,128]{3,2,1,0:T(8,128)(2,1)S(1)} %all-to-all-done.own, ...), custom_call_target="tpu_custom_call" | custom-call | tf_op jit(solution)/shard_map/chebyshev_filter/pallas_call | solution.py:124
  35.3 15.2 %all_to_all.30 = bf16[32,6,8,128]{3,2,1,0:T(8,128)(2,1)S(1)} all-to-all(bf16[32,6,8,128]{3,2,1,0:T(8,128)(2,1)S(1)} %bitcast.24), channel_id=1, replica_groups=mesh['z'=16,'xl'=2,'core'=2,'xh'=2,'y'=4] {'xh','y','xl','core'}, dimensions={0} | all-to-all | bytes 786432 | tf_op jit(solution)/shard_map/all_to_all | solution.py:338
  50.5 0.4 packed_terms.1
  50.9 11.4 %all_to_all.31 = f32[32,4,128]{2,1,0:T(4,128)S(1)} all-to-all(f32[32,4,128]{2,1,0:T(4,128)S(1)} %packed_terms.1), channel_id=1, replica_groups=mesh['z'=16,'xl'=2,'core'=2,'xh'=2,'y'=4] {'xh','y','xl','core'}, dimensions={0} | all-to-all | bytes 131072 | tf_op jit(solution)/shard_map/all_to_all | solution.py:218
  62.3 27.8 %all_to_all.32 = f32[16,4,128]{2,1,0:T(4,128)S(1)} all-to-all(f32[16,4,128]{2,1,0:T(4,128)S(1)} %broadcast_in_dim.6), channel_id=1, replica_groups=mesh['z'=16,'xl'=2,'core'=2,'xh'=2,'y'=4] {'z'}, dimensions={0} | all-to-all | bytes 65536 | tf_op jit(solution)/shard_map/all_to_all | solution.py:165
  90.2 12.4 %all_to_all.33.whole = f32[32,4,128]{2,1,0:T(4,128)S(1)} all-to-all(f32[32,4,128]{2,1,0:T(4,128)S(1)} %broadcast_in_dim.7), channel_id=1, replica_groups=mesh['z'=16,'xl'=2,'core'=2,'xh'=2,'y'=4] {'xh','y','xl','core'}, dimensions={0} | all-to-all | bytes 131072 | tf_op jit(solution)/shard_map/all_to_all | solution.py:220
  102.6 3.9 %inverse_and_turned.1 = (f32[96,96]{1,0:T(8,128)S(1)}, f32[96,96]{1,0:T(8,128)S(1)}, bf16[8,12,8,128]{3,2,1,0:T(8,128)(2,1)}) custom-call(f32[32,4,128]{2,1,0:T(4,128)S(1)} %all_to_all.33.whole, bf16[96,1024]{1,0:T(8,128)(2,1)S(1)} %get-tuple-element.19.filtered), custom_call_target="tpu_custom_call" | custom-call | tf_op jit(solution)/shard_map/inverse_and_turned/pallas_call | solution.py:302
  106.4 3.4 %all-to-all-start.5 = ((bf16[8,12,8,128]{3,2,1,0:T(8,128)(2,1)}), bf16[8,12,8,128]{3,2,1,0:T(8,128)(2,1)S(1)}, u32[]{:S(2)}, u32[]{:S(2)}) async-start(bf16[8,12,8,128]{3,2,1,0:T(8,128)(2,1)} %get-tuple-element.5), calls=%async_computation.5 | async-start | bytes 393216 | tf_op jit(solution)/shard_map/all_to_all | solution.py:344
  109.8 0.2 fusion.2
  110.1 0.8 fusion.3
  110.9 6.1 %all-to-all-done.5 = bf16[8,12,8,128]{3,2,1,0:T(8,128)(2,1)S(1)} async-done(((bf16[8,12,8,128]{3,2,1,0:T(8,128)(2,1)}), bf16[8,12,8,128]{3,2,1,0:T(8,128)(2,1)S(1)}, u32[]{:S(2)}, u32[]{:S(2)}) %all-to-all-start.5) | async-done | bytes 196640 | tf_op jit(solution)/shard_map/all_to_all | solution.py:344
  117.0 0.7 copy_bitcast_fusion.2
  (7 shorter events, 0.2 us)
Async XLA Ops:
  2.3 15.4 %all-to-all-start = ((bf16[4,4,64,128]{3,2,1,0:T(8,128)(2,1)}), bf16[4,4,64,128]{3,2,1,0:T(8,128)(2,1)S(1)}, u32[]{:S(2)}, u32[]{:S(2)}) async-start(bf16[4,4,64,128]{3,2,1,0:T(8,128)(2,1)} %pack.1), calls=%async_computation | async-start | bytes 524288 | tf_op jit(solution)/shard_map/all_to_all | solution.py:329
  17.7 12.8 %collective-permute-start.2 = (bf16[4,4,64,128]{3,2,1,0:T(8,128)(2,1)S(1)}, bf16[4,4,64,128]{3,2,1,0:T(8,128)(2,1)S(1)}, u32[]{:S(2)}, u32[]{:S(2)}) collective-permute-start(bf16[4,4,64,128]{3,2,1,0:T(8,128)(2,1)S(1)} %all-to-all-done.own), channel_id=1, source_target_pairs={{32,0},{64,32},{96,64},{128,96},{160,128},{192,160},{224,192},{256... | collective-permute-start | bytes 786440 | tf_op jit(solution)/shard_map/ppermute | solution.py:160
  19.0 11.5 %collective-permute-start.1 = (bf16[4,4,64,128]{3,2,1,0:T(8,128)(2,1)S(1)}, bf16[4,4,64,128]{3,2,1,0:T(8,128)(2,1)S(1)}, u32[]{:S(2)}, u32[]{:S(2)}) collective-permute-start(bf16[4,4,64,128]{3,2,1,0:T(8,128)(2,1)S(1)} %all-to-all-done.own), channel_id=1, source_target_pairs={{0,32},{32,64},{64,96},{96,128},{128,160},{160,192},{192,224},{224... | collective-permute-start | bytes 786440 | tf_op jit(solution)/shard_map/ppermute | solution.py:160
  23.0 6.6 %collective-permute-start.3 = (bf16[1,4,64,128]{3,2,1,0:T(8,128)(2,1)S(1)}, bf16[1,4,64,128]{3,2,1,0:T(8,128)(2,1)S(1)}, u32[]{:S(2)}, u32[]{:S(2)}) collective-permute-start(bf16[1,4,64,128]{3,2,1,0:T(8,128)(2,1)S(1)} %get-tuple-element.16), channel_id=1, source_target_pairs={{64,0},{96,32},{128,64},{160,96},{192,128},{224,160},{256,192},{28... | collective-permute-start | bytes 196616 | tf_op jit(solution)/shard_map/ppermute | solution.py:160
  24.3 6.2 %collective-permute-start = (bf16[1,4,64,128]{3,2,1,0:T(8,128)(2,1)S(1)}, bf16[1,4,64,128]{3,2,1,0:T(8,128)(2,1)S(1)}, u32[]{:S(2)}, u32[]{:S(2)}) collective-permute-start(bf16[1,4,64,128]{3,2,1,0:T(8,128)(2,1)S(1)} %get-tuple-element.17), channel_id=1, source_target_pairs={{0,64},{32,96},{64,128},{96,160},{128,192},{160,224},{192,256},{22... | collective-permute-start | bytes 196616 | tf_op jit(solution)/shard_map/ppermute | solution.py:160
  106.4 10.6 %all-to-all-start.5 = ((bf16[8,12,8,128]{3,2,1,0:T(8,128)(2,1)}), bf16[8,12,8,128]{3,2,1,0:T(8,128)(2,1)S(1)}, u32[]{:S(2)}, u32[]{:S(2)}) async-start(bf16[8,12,8,128]{3,2,1,0:T(8,128)(2,1)} %get-tuple-element.5), calls=%async_computation.5 | async-start | bytes 393216 | tf_op jit(solution)/shard_map/all_to_all | solution.py:344

commit v6 on v5

--- a/solution.py
+++ b/solution.py
@@ -20,7 +20,13 @@
 LAYER = ("xh", "y", "xl", "core")
 
 
-def filter_kernel(bounds, far_lo, lo, own, hi, far_hi, out, even, odd, weak_even, weak_odd, strong, degree):
+def root_of(label):
+    root = jnp.where(label == 1.0, ROOTS[1], 0.0)
+    root = jnp.where(label == 2.0, ROOTS[2], root)
+    return jnp.where(label == 3.0, ROOTS[3], root)
+
+
+def filter_kernel(bounds, lo, own, hi, out, short, share, even, odd, weak_even, weak_odd, strong, degree):
     planes, height, width = degree.shape
     local = even.shape[1]
     rows = out.shape[3]
@@ -50,15 +56,19 @@
 
     lax.fori_loop(0, planes, clear, 0)
 
-    start = 0
-    for source in (far_lo, lo, own, hi, far_hi):
+    depth = own.shape[0]
+    for plane in (0, planes - 1):
+        strong[plane, inner] = jnp.zeros((height, width), jnp.float32)
+        even[plane] = jnp.zeros(even.shape[1:], jnp.float32)
+        for mode in range(local):
+            weak_even[plane, mode, inner] = jnp.zeros((height, width), jnp.float32)
+
+    for source, start in ((lo, REACH - depth), (own, REACH), (hi, REACH + depth)):
         count = source.shape[0]
 
         def load(index, carry, source=source, start=start):
             label = source[index, local].astype(jnp.float32)
-            root = jnp.where(label == 1.0, ROOTS[1], 0.0)
-            root = jnp.where(label == 2.0, ROOTS[2], root)
-            root = jnp.where(label == 3.0, ROOTS[3], root)
+            root = root_of(label)
             strong[start + index, inner] = root
             for mode in range(local):
                 value = jnp.where(label > 0.0, source[index, mode].astype(jnp.float32), 0.0)
@@ -67,7 +77,6 @@
             return carry
 
         lax.fori_loop(0, count, load, 0, unroll=min(count, UNROLL))
-        start += count
 
     def weigh(plane, carry):
         root, around = beside(strong, plane)
@@ -98,7 +107,7 @@
         cur, prev = prev, cur
         weak, weak_next = weak_next, weak
 
-    def finish(index, carry):
+    for index in range(depth):
         plane = REACH + index
         root, heavy = strong[plane, inner], degree[plane]
         for mode in range(local):
@@ -107,10 +116,32 @@
             around = around + (weak[plane - 1, mode, inner] + weak[plane + 1, mode, inner])
             image = heavy * value - root * around
             out[:, index, mode] = value.reshape(-1, rows, width).astype(out.dtype)
+            if index == 0:
+                short[0, mode] = image
+            elif index == depth - 1:
+                short[1, mode] = image
+            else:
+                out[:, index, local + mode] = image.reshape(-1, rows, width).astype(out.dtype)
+
+    for side, (outer, step) in enumerate(((REACH - depth, 1), (planes - 1 - REACH + depth, -1))):
+        between = strong[outer + step * (DEGREE - 1), inner]
+        for index in range(DEGREE - 1):
+            between = between * strong[outer + step * index, inner]
+        share[side] = (8.0 * scale * scale * scale * scale) * (between * between) * strong[outer + step * DEGREE, inner]
+
+
+def finish_kernel(lo, hi, far_lo, far_hi, short, share, done, out):
+    out[...] = done[...]
+    local = short.shape[1]
+    depth, rows, width = out.shape[1], out.shape[3], out.shape[4]
+    sides = ((lo, 0, far_lo, 0, 0), (hi, depth - 1, far_hi, 0, depth - 1))
+    for side, (near, near_plane, far, far_plane, index) in enumerate(sides):
+        weight = share[side] * root_of(far[far_plane, local].astype(jnp.float32))
+        for mode in range(local):
+            jump = near[near_plane, mode].astype(jnp.float32) - far[far_plane, mode].astype(jnp.float32)
+            image = short[side, mode] + weight * jump
             out[:, index, local + mode] = image.reshape(-1, rows, width).astype(out.dtype)
-        return carry
-
-    lax.fori_loop(0, own.shape[0], finish, 0, unroll=2)
+
 
 def filtered_and_applied(bounds, far_lo, lo, own, hi, far_hi, blocks):
     depth, fields, height, width = own.shape
@@ -121,15 +152,30 @@
     root = pltpu.VMEM((planes, height + 2 * SUBLANES, width), jnp.float32)
     degree = pltpu.VMEM((planes, height, width), jnp.float32)
     vmem = pl.BlockSpec(memory_space=pltpu.VMEM)
-    return pl.pallas_call(
+    whole = jax.ShapeDtypeStruct((blocks, depth, 2 * local, height // blocks, width), jnp.bfloat16)
+    steps = planes * local * height * width
+    whole_part, short, share = pl.pallas_call(
         filter_kernel,
-        out_shape=jax.ShapeDtypeStruct((blocks, depth, 2 * local, height // blocks, width), jnp.bfloat16),
-        in_specs=[pl.BlockSpec(memory_space=pltpu.SMEM)] + [vmem] * 5,
-        out_specs=vmem,
+        out_shape=(
+            whole,
+            jax.ShapeDtypeStruct((2, local, height, width), jnp.float32),
+            jax.ShapeDtypeStruct((2, height, width), jnp.float32),
+        ),
+        in_specs=[pl.BlockSpec(memory_space=pltpu.SMEM)] + [vmem] * 3,
+        out_specs=(vmem,) * 3,
         scratch_shapes=[field, field, rimmed, rimmed, root, degree],
         compiler_params=pltpu.CompilerParams(vmem_limit_bytes=40 * 1024 * 1024),
+        cost_estimate=pl.CostEstimate(flops=100 * steps, bytes_accessed=8 * steps, transcendentals=0),
         name="chebyshev_filter",
-    )(bounds, far_lo, lo, own, hi, far_hi)
+    )(bounds, lo, own, hi)
+    return pl.pallas_call(
+        finish_kernel,
+        out_shape=whole,
+        in_specs=[vmem] * 7,
+        out_specs=vmem,
+        compiler_params=pltpu.CompilerParams(vmem_limit_bytes=8 * 1024 * 1024),
+        name="outermost_planes",
+    )(lo, hi, far_lo, far_hi, short, share, whole_part)
 
 
 def pack_kernel(block, labels, out):

time: 118 us -> 115 us (0.975)
  blocking collectives: 66.7 us -> 64.4 us
  waiting for transfers between devices: 11.3 us -> 10 us
    all_to_all x1, blocking collectives: 27.8 us -> 26 us  [summed_over_z(): return jnp.sum(lax.all_to_all(copies, 'z', 0, 0, tiled=True), axis=0)]
    ppermute x4, waiting for transfers between devices: 1.24 us -> 0.01 us  [shifted(): return lax.ppermute(value, axis, pairs)]
    pallas_call x1 -> x2, Pallas kernels: 4.73 us -> 4.72 us  [the longest x1 4.63 us: filtered_and_applied(): pl.pallas_call(filter_kernel, out_shape=(whole, jax.ShapeDtypeStruct((2,...]
  transfers between devices with their start and end apart: 6 -> 6, of which waited for: 4 -> 2; matrix products, arithmetic and copies ran while one was open for 1% -> 1% of each run, Pallas kernels for 0% -> 4%
where the time goes in v6:
time: 115 us; the launch traced here: 114 us
  blocking collectives  64.4 us (56%)
  starting transfers between devices  25.1 us (22%)
  Pallas kernels  10.6 us (9%)
  waiting for transfers between devices  10 us (9%)
  between operations  2.04 us (2%)
    all_to_all x1, blocking collectives, summed_over_z(): return jnp.sum(lax.all_to_all(copies, 'z', 0, 0, tiled=True), axis=0)  26 us
    all_to_all x1, blocking collectives, per_device(): pair = lax.all_to_all(pair, LAYER, 0, 0, tiled=True)  14.6 us
    all_to_all x1, blocking collectives, total_over_all(): lax.all_to_all(jnp.broadcast_to(mine, partial.shape), LAYER, 0, 0, tiled=...  12.4 us
    ppermute x4, starting transfers between devices, shifted(): return lax.ppermute(value, axis, pairs)  11.5 us
    all_to_all x1, blocking collectives, total_over_all(): terms = lax.all_to_all(partial, LAYER, 0, 0, tiled=True)  11.4 us
    all_to_all x1, starting transfers between devices, per_device(): lax.all_to_all(packed(initial_block, labels, group), GROUP, 0, 0, tiled=T...  10.2 us
    all_to_all x1, waiting for transfers between devices, per_device(): turned = lax.all_to_all(turned, MODE, 0, 0, tiled=True)  6.15 us
    pallas_call x1, Pallas kernels, filtered_and_applied(): pl.pallas_call(filter_kernel, out_shape=(whole, jax.ShapeDtypeStruct((2,...  4.63 us
  transfers between devices with their start and end apart: 6, of which 2 were waited for; matrix products, arithmetic and copies ran while one was open for 1% of the time, Pallas kernels for 4%

profile of v6, /device:TPU:1, one launch (start us, length us, event | category | flops | bytes accessed | tf_op | source)
XLA Modules:
  0.0 114.2 jit_solution(13149993951151684955)
XLA Ops:
  0.6 1.6 %pack.1 = bf16[4,4,64,128]{3,2,1,0:T(8,128)(2,1)} custom-call(bf16[12,1,64,128]{3,2,1,0:T(8,128)(2,1)} %block.1, s32[1,64,128]{2,1,0:T(8,128)} %labels.1), custom_call_target="tpu_custom_call" | custom-call | tf_op jit(solution)/shard_map/pack/pallas_call | solution.py:194
  2.3 10.2 %all-to-all-start = ((bf16[4,4,64,128]{3,2,1,0:T(8,128)(2,1)}), bf16[4,4,64,128]{3,2,1,0:T(8,128)(2,1)S(1)}, u32[]{:S(2)}, u32[]{:S(2)}) async-start(bf16[4,4,64,128]{3,2,1,0:T(8,128)(2,1)} %pack.1), calls=%async_computation | async-start | bytes 524288 | tf_op jit(solution)/shard_map/all_to_all | solution.py:375
  13.8 3.9 %all-to-all-done.own = bf16[4,4,64,128]{3,2,1,0:T(8,128)(2,1)S(1)} async-done(((bf16[4,4,64,128]{3,2,1,0:T(8,128)(2,1)}), bf16[4,4,64,128]{3,2,1,0:T(8,128)(2,1)S(1)}, u32[]{:S(2)}, u32[]{:S(2)}) %all-to-all-start) | async-done | bytes 262176 | tf_op jit(solution)/shard_map/all_to_all | solution.py:375
  17.7 1.3 %collective-permute-start.1 = (bf16[4,4,64,128]{3,2,1,0:T(8,128)(2,1)S(1)}, bf16[4,4,64,128]{3,2,1,0:T(8,128)(2,1)S(1)}, u32[]{:S(2)}, u32[]{:S(2)}) collective-permute-start(bf16[4,4,64,128]{3,2,1,0:T(8,128)(2,1)S(1)} %all-to-all-done.own), channel_id=1, source_target_pairs={{32,0},{64,32},{96,64},{128,96},{160,128},{192,160},{224,192},{256... | collective-permute-start | bytes 786440 | tf_op jit(solution)/shard_map/ppermute | solution.py:206
  19.0 4.0 %collective-permute-start = (bf16[4,4,64,128]{3,2,1,0:T(8,128)(2,1)S(1)}, bf16[4,4,64,128]{3,2,1,0:T(8,128)(2,1)S(1)}, u32[]{:S(2)}, u32[]{:S(2)}) collective-permute-start(bf16[4,4,64,128]{3,2,1,0:T(8,128)(2,1)S(1)} %all-to-all-done.own), channel_id=1, source_target_pairs={{0,32},{32,64},{64,96},{96,128},{128,160},{160,192},{192,224},{224... | collective-permute-start | bytes 786440 | tf_op jit(solution)/shard_map/ppermute | solution.py:206
  23.0 1.3 %collective-permute-start.3 = (bf16[1,4,64,128]{3,2,1,0:T(8,128)(2,1)S(1)}, bf16[1,4,64,128]{3,2,1,0:T(8,128)(2,1)S(1)}, u32[]{:S(2)}, u32[]{:S(2)}) collective-permute-start(bf16[1,4,64,128]{3,2,1,0:T(8,128)(2,1)S(1)} %get-tuple-element.22), channel_id=1, source_target_pairs={{64,0},{96,32},{128,64},{160,96},{192,128},{224,160},{256,192},{28... | collective-permute-start | bytes 196616 | tf_op jit(solution)/shard_map/ppermute | solution.py:206
  24.3 4.9 %collective-permute-start.2 = (bf16[1,4,64,128]{3,2,1,0:T(8,128)(2,1)S(1)}, bf16[1,4,64,128]{3,2,1,0:T(8,128)(2,1)S(1)}, u32[]{:S(2)}, u32[]{:S(2)}) collective-permute-start(bf16[1,4,64,128]{3,2,1,0:T(8,128)(2,1)S(1)} %get-tuple-element.23), channel_id=1, source_target_pairs={{0,64},{32,96},{64,128},{96,160},{128,192},{160,224},{192,256},{22... | collective-permute-start | bytes 196616 | tf_op jit(solution)/shard_map/ppermute | solution.py:206
  29.2 0.1 pad_maximum_fusion.bounds
  29.3 0.0 collective-permute-done.1.hi
  29.3 0.0 collective-permute-done.lo
  29.3 4.6 %chebyshev_filter.1 = (bf16[8,4,6,8,128]{4,3,2,1,0:T(8,128)(2,1)S(1)}, f32[2,3,64,128]{3,2,1,0:T(8,128)S(1)}, f32[2,64,128]{2,1,0:T(8,128)S(1)}) custom-call(f32[2]{0:T(128)S(1)} %pad_maximum_fusion.bounds, bf16[4,4,64,128]{3,2,1,0:T(8,128)(2,1)S(1)} %collective-permute-done.lo, bf16[4,4,64,128]{3,2,1,0:T(8,128)(2,1)S(1)} %all-to-all-done.own, ...), custom_call_target="tpu_custom_call" | custom-call | flops 34406400 | bytes 2752512 | tf_op jit(solution)/shard_map/chebyshev_filter/pallas_call | solution.py:157
  33.9 0.0 collective-permute-done.3.far_hi
  33.9 0.0 collective-permute-done.2.far_lo
  34.0 0.1 outermost_planes.1
  34.1 14.6 %all_to_all.30 = bf16[32,6,8,128]{3,2,1,0:T(8,128)(2,1)S(1)} all-to-all(bf16[32,6,8,128]{3,2,1,0:T(8,128)(2,1)S(1)} %bitcast.24), channel_id=1, replica_groups=mesh['z'=16,'xl'=2,'core'=2,'xh'=2,'y'=4] {'xh','y','xl','core'}, dimensions={0} | all-to-all | bytes 786432 | tf_op jit(solution)/shard_map/all_to_all | solution.py:384
  48.7 0.4 packed_terms.1
  49.1 11.4 %all_to_all.31 = f32[32,4,128]{2,1,0:T(4,128)S(1)} all-to-all(f32[32,4,128]{2,1,0:T(4,128)S(1)} %packed_terms.1), channel_id=1, replica_groups=mesh['z'=16,'xl'=2,'core'=2,'xh'=2,'y'=4] {'xh','y','xl','core'}, dimensions={0} | all-to-all | bytes 131072 | tf_op jit(solution)/shard_map/all_to_all | solution.py:264
  60.5 26.0 %all_to_all.32 = f32[16,4,128]{2,1,0:T(4,128)S(1)} all-to-all(f32[16,4,128]{2,1,0:T(4,128)S(1)} %broadcast_in_dim.6), channel_id=1, replica_groups=mesh['z'=16,'xl'=2,'core'=2,'xh'=2,'y'=4] {'z'}, dimensions={0} | all-to-all | bytes 65536 | tf_op jit(solution)/shard_map/all_to_all | solution.py:211
  86.6 12.4 %all_to_all.33.whole = f32[32,4,128]{2,1,0:T(4,128)S(1)} all-to-all(f32[32,4,128]{2,1,0:T(4,128)S(1)} %broadcast_in_dim.7), channel_id=1, replica_groups=mesh['z'=16,'xl'=2,'core'=2,'xh'=2,'y'=4] {'xh','y','xl','core'}, dimensions={0} | all-to-all | bytes 131072 | tf_op jit(solution)/shard_map/all_to_all | solution.py:266
  99.0 3.9 %inverse_and_turned.1 = (f32[96,96]{1,0:T(8,128)S(1)}, f32[96,96]{1,0:T(8,128)S(1)}, bf16[8,12,8,128]{3,2,1,0:T(8,128)(2,1)}) custom-call(f32[32,4,128]{2,1,0:T(4,128)S(1)} %all_to_all.33.whole, bf16[96,1024]{1,0:T(8,128)(2,1)S(1)} %get-tuple-element.25.filtered), custom_call_target="tpu_custom_call" | custom-call | tf_op jit(solution)/shard_map/inverse_and_turned/pallas_call | solution.py:348
  102.9 3.4 %all-to-all-start.5 = ((bf16[8,12,8,128]{3,2,1,0:T(8,128)(2,1)}), bf16[8,12,8,128]{3,2,1,0:T(8,128)(2,1)S(1)}, u32[]{:S(2)}, u32[]{:S(2)}) async-start(bf16[8,12,8,128]{3,2,1,0:T(8,128)(2,1)} %get-tuple-element.11), calls=%async_computation.5 | async-start | bytes 393216 | tf_op jit(solution)/shard_map/all_to_all | solution.py:390
  106.3 0.2 fusion.2
  106.5 0.8 fusion.3
  107.3 6.1 %all-to-all-done.5 = bf16[8,12,8,128]{3,2,1,0:T(8,128)(2,1)S(1)} async-done(((bf16[8,12,8,128]{3,2,1,0:T(8,128)(2,1)}), bf16[8,12,8,128]{3,2,1,0:T(8,128)(2,1)S(1)}, u32[]{:S(2)}, u32[]{:S(2)}) %all-to-all-start.5) | async-done | bytes 196640 | tf_op jit(solution)/shard_map/all_to_all | solution.py:390
  113.5 0.7 copy_bitcast_fusion.2
  (7 shorter events, 0.2 us)
Async XLA Ops:
  2.3 15.4 %all-to-all-start = ((bf16[4,4,64,128]{3,2,1,0:T(8,128)(2,1)}), bf16[4,4,64,128]{3,2,1,0:T(8,128)(2,1)S(1)}, u32[]{:S(2)}, u32[]{:S(2)}) async-start(bf16[4,4,64,128]{3,2,1,0:T(8,128)(2,1)} %pack.1), calls=%async_computation | async-start | bytes 524288 | tf_op jit(solution)/shard_map/all_to_all | solution.py:375
  17.7 11.6 %collective-permute-start.1 = (bf16[4,4,64,128]{3,2,1,0:T(8,128)(2,1)S(1)}, bf16[4,4,64,128]{3,2,1,0:T(8,128)(2,1)S(1)}, u32[]{:S(2)}, u32[]{:S(2)}) collective-permute-start(bf16[4,4,64,128]{3,2,1,0:T(8,128)(2,1)S(1)} %all-to-all-done.own), channel_id=1, source_target_pairs={{32,0},{64,32},{96,64},{128,96},{160,128},{192,160},{224,192},{256... | collective-permute-start | bytes 786440 | tf_op jit(solution)/shard_map/ppermute | solution.py:206
  19.0 10.3 %collective-permute-start = (bf16[4,4,64,128]{3,2,1,0:T(8,128)(2,1)S(1)}, bf16[4,4,64,128]{3,2,1,0:T(8,128)(2,1)S(1)}, u32[]{:S(2)}, u32[]{:S(2)}) collective-permute-start(bf16[4,4,64,128]{3,2,1,0:T(8,128)(2,1)S(1)} %all-to-all-done.own), channel_id=1, source_target_pairs={{0,32},{32,64},{64,96},{96,128},{128,160},{160,192},{192,224},{224... | collective-permute-start | bytes 786440 | tf_op jit(solution)/shard_map/ppermute | solution.py:206
  23.0 10.9 %collective-permute-start.3 = (bf16[1,4,64,128]{3,2,1,0:T(8,128)(2,1)S(1)}, bf16[1,4,64,128]{3,2,1,0:T(8,128)(2,1)S(1)}, u32[]{:S(2)}, u32[]{:S(2)}) collective-permute-start(bf16[1,4,64,128]{3,2,1,0:T(8,128)(2,1)S(1)} %get-tuple-element.22), channel_id=1, source_target_pairs={{64,0},{96,32},{128,64},{160,96},{192,128},{224,160},{256,192},{28... | collective-permute-start | bytes 196616 | tf_op jit(solution)/shard_map/ppermute | solution.py:206
  24.3 9.6 %collective-permute-start.2 = (bf16[1,4,64,128]{3,2,1,0:T(8,128)(2,1)S(1)}, bf16[1,4,64,128]{3,2,1,0:T(8,128)(2,1)S(1)}, u32[]{:S(2)}, u32[]{:S(2)}) collective-permute-start(bf16[1,4,64,128]{3,2,1,0:T(8,128)(2,1)S(1)} %get-tuple-element.23), channel_id=1, source_target_pairs={{0,64},{32,96},{64,128},{96,160},{128,192},{160,224},{192,256},{22... | collective-permute-start | bytes 196616 | tf_op jit(solution)/shard_map/ppermute | solution.py:206
  102.9 10.6 %all-to-all-start.5 = ((bf16[8,12,8,128]{3,2,1,0:T(8,128)(2,1)}), bf16[8,12,8,128]{3,2,1,0:T(8,128)(2,1)S(1)}, u32[]{:S(2)}, u32[]{:S(2)}) async-start(bf16[8,12,8,128]{3,2,1,0:T(8,128)(2,1)} %get-tuple-element.11), calls=%async_computation.5 | async-start | bytes 393216 | tf_op jit(solution)/shard_map/all_to_all | solution.py:390

commit v7 on v6

--- a/solution.py
+++ b/solution.py
@@ -12,7 +12,7 @@
 ROOTS = (0.0, 0.7745967, 1.0, 1.3416408)
 REACH = DEGREE + 1
 SUBLANES, LANES = 8, 128
-UNROLL = 4
+UNROLL = 6
 
 AXES = ("z", "xl", "core", "xh", "y")
 GROUP = ("xl", "core")
@@ -26,23 +26,31 @@
     return jnp.where(label == 3.0, ROOTS[3], root)
 
 
-def filter_kernel(bounds, lo, own, hi, out, short, share, even, odd, weak_even, weak_odd, strong, degree):
+def inverse_root_of(label):
+    value = jnp.where(label == 1.0, 1.0 / ROOTS[1], 0.0)
+    value = jnp.where(label == 2.0, 1.0 / ROOTS[2], value)
+    return jnp.where(label == 3.0, 1.0 / ROOTS[3], value)
+
+
+def filter_kernel(lowest, highest, lo, own, hi, out, short, share, even, odd, strong, square, degree):
     planes, height, width = degree.shape
     local = even.shape[1]
     rows = out.shape[3]
-    low, high = bounds[0], bounds[1]
+    depth = own.shape[0]
+    low, high = lowest[0], highest[0]
     centre = 0.5 * (high + low)
     scale = 1.0 / (0.5 * (high - low))
     inner = pl.ds(SUBLANES, height)
     lane = lax.broadcasted_iota(jnp.int32, (height, width), 1)
 
-    def beside(ref, *index):
-        value = ref[(*index, inner)]
-        up = ref[(*index, pl.ds(SUBLANES - 1, height))]
-        down = ref[(*index, pl.ds(SUBLANES + 1, height))]
+    def beside(ref, plane, *index):
+        value = ref[(plane, *index, inner)]
+        up = ref[(plane, *index, pl.ds(SUBLANES - 1, height))]
+        down = ref[(plane, *index, pl.ds(SUBLANES + 1, height))]
         left = jnp.where(lane == 0, 0.0, pltpu.roll(value, 1, 1))
         right = jnp.where(lane == width - 1, 0.0, pltpu.roll(value, width - 1, 1))
-        return value, (up + down) + (left + right)
+        before, after = ref[(plane - 1, *index, inner)], ref[(plane + 1, *index, inner)]
+        return value, (up + down) + (left + right) + (before + after)
 
     edge = jnp.zeros((SUBLANES, width), jnp.float32)
 
@@ -50,72 +58,62 @@
         for first in (0, SUBLANES + height):
             strong[plane, pl.ds(first, SUBLANES)] = edge
             for mode in range(local):
-                weak_even[plane, mode, pl.ds(first, SUBLANES)] = edge
-                weak_odd[plane, mode, pl.ds(first, SUBLANES)] = edge
+                even[plane, mode, pl.ds(first, SUBLANES)] = edge
+                odd[plane, mode, pl.ds(first, SUBLANES)] = edge
         return carry
 
     lax.fori_loop(0, planes, clear, 0)
 
-    depth = own.shape[0]
     for plane in (0, planes - 1):
         strong[plane, inner] = jnp.zeros((height, width), jnp.float32)
-        even[plane] = jnp.zeros(even.shape[1:], jnp.float32)
         for mode in range(local):
-            weak_even[plane, mode, inner] = jnp.zeros((height, width), jnp.float32)
+            even[plane, mode, inner] = jnp.zeros((height, width), jnp.float32)
 
     for source, start in ((lo, REACH - depth), (own, REACH), (hi, REACH + depth)):
-        count = source.shape[0]
 
         def load(index, carry, source=source, start=start):
-            label = source[index, local].astype(jnp.float32)
-            root = root_of(label)
+            root = root_of(source[index, local].astype(jnp.float32))
             strong[start + index, inner] = root
+            square[start + index] = root * root
             for mode in range(local):
-                value = jnp.where(label > 0.0, source[index, mode].astype(jnp.float32), 0.0)
-                even[start + index, mode] = value
-                weak_even[start + index, mode, inner] = root * value
+                even[start + index, mode, inner] = root * source[index, mode].astype(jnp.float32)
             return carry
 
-        lax.fori_loop(0, count, load, 0, unroll=min(count, UNROLL))
+        lax.fori_loop(0, depth, load, 0, unroll=min(depth, UNROLL))
 
     def weigh(plane, carry):
         root, around = beside(strong, plane)
-        degree[plane] = root * (strong[plane - 1, inner] + strong[plane + 1, inner] + around)
+        degree[plane] = root * around
         return carry
 
     lax.fori_loop(1, planes - 1, weigh, 0, unroll=UNROLL)
 
-    cur, prev, weak, weak_next = even, odd, weak_even, weak_odd
+    cur, prev = even, odd
     for step in range(DEGREE):
         factor = scale if step == 0 else 2.0 * scale
 
-        def advance(plane, carry, cur=cur, prev=prev, weak=weak, weak_next=weak_next, factor=factor, step=step):
-            root = strong[plane, inner]
+        def advance(plane, carry, cur=cur, prev=prev, factor=factor, step=step):
             here = (degree[plane] - centre) * factor
-            there = root * factor
+            there = square[plane] * factor
             for mode in range(local):
-                _, around = beside(weak, plane, mode)
-                around = around + (weak[plane - 1, mode, inner] + weak[plane + 1, mode, inner])
-                value = here * cur[plane, mode] - there * around
+                value, around = beside(cur, plane, mode)
+                value = here * value - there * around
                 if step > 0:
-                    value = value - prev[plane, mode]
-                prev[plane, mode] = value
-                weak_next[plane, mode, inner] = root * value
+                    value = value - prev[plane, mode, inner]
+                prev[plane, mode, inner] = value
             return carry
 
         lax.fori_loop(step + 1, planes - step - 1, advance, 0, unroll=UNROLL)
         cur, prev = prev, cur
-        weak, weak_next = weak_next, weak
 
     for index in range(depth):
         plane = REACH + index
-        root, heavy = strong[plane, inner], degree[plane]
+        heavy, weight = degree[plane], square[plane]
+        upright = inverse_root_of(own[index, local].astype(jnp.float32))
         for mode in range(local):
-            value = cur[plane, mode]
-            _, around = beside(weak, plane, mode)
-            around = around + (weak[plane - 1, mode, inner] + weak[plane + 1, mode, inner])
-            image = heavy * value - root * around
-            out[:, index, mode] = value.reshape(-1, rows, width).astype(out.dtype)
+            value, around = beside(cur, plane, mode)
+            image = upright * (heavy * value - weight * around)
+            out[:, index, mode] = (upright * value).reshape(-1, rows, width).astype(out.dtype)
             if index == 0:
                 short[0, mode] = image
             elif index == depth - 1:
@@ -124,10 +122,10 @@
                 out[:, index, local + mode] = image.reshape(-1, rows, width).astype(out.dtype)
 
     for side, (outer, step) in enumerate(((REACH - depth, 1), (planes - 1 - REACH + depth, -1))):
-        between = strong[outer + step * (DEGREE - 1), inner]
-        for index in range(DEGREE - 1):
-            between = between * strong[outer + step * index, inner]
-        share[side] = (8.0 * scale * scale * scale * scale) * (between * between) * strong[outer + step * DEGREE, inner]
+        between = square[outer]
+        for index in range(1, DEGREE):
+            between = between * square[outer + step * index]
+        share[side] = (8.0 * scale * scale * scale * scale) * between * strong[outer + step * DEGREE, inner]
 
 
 def finish_kernel(lo, hi, far_lo, far_hi, short, share, done, out):
@@ -143,14 +141,13 @@
             out[:, index, local + mode] = image.reshape(-1, rows, width).astype(out.dtype)
 
 
-def filtered_and_applied(bounds, far_lo, lo, own, hi, far_hi, blocks):
+def filtered_and_applied(lowest, highest, far_lo, lo, own, hi, far_hi, blocks):
     depth, fields, height, width = own.shape
     local = fields - 1
     planes = depth + 2 * REACH
-    field = pltpu.VMEM((planes, local, height, width), jnp.float32)
     rimmed = pltpu.VMEM((planes, local, height + 2 * SUBLANES, width), jnp.float32)
     root = pltpu.VMEM((planes, height + 2 * SUBLANES, width), jnp.float32)
-    degree = pltpu.VMEM((planes, height, width), jnp.float32)
+    flat = pltpu.VMEM((planes, height, width), jnp.float32)
     vmem = pl.BlockSpec(memory_space=pltpu.VMEM)
     whole = jax.ShapeDtypeStruct((blocks, depth, 2 * local, height // blocks, width), jnp.bfloat16)
     steps = planes * local * height * width
@@ -161,13 +158,13 @@
             jax.ShapeDtypeStruct((2, local, height, width), jnp.float32),
             jax.ShapeDtypeStruct((2, height, width), jnp.float32),
         ),
-        in_specs=[pl.BlockSpec(memory_space=pltpu.SMEM)] + [vmem] * 3,
+        in_specs=[pl.BlockSpec(memory_space=pltpu.SMEM)] * 2 + [vmem] * 3,
         out_specs=(vmem,) * 3,
-        scratch_shapes=[field, field, rimmed, rimmed, root, degree],
+        scratch_shapes=[rimmed, rimmed, root, flat, flat],
         compiler_params=pltpu.CompilerParams(vmem_limit_bytes=40 * 1024 * 1024),
         cost_estimate=pl.CostEstimate(flops=100 * steps, bytes_accessed=8 * steps, transcendentals=0),
         name="chebyshev_filter",
-    )(bounds, lo, own, hi)
+    )(lowest, highest, lo, own, hi)
     return pl.pallas_call(
         finish_kernel,
         out_shape=whole,
@@ -196,6 +193,7 @@
         out_shape=jax.ShapeDtypeStruct((group, share // group + 1, height, width), block.dtype),
         in_specs=[vmem, vmem],
         out_specs=vmem,
+        compiler_params=pltpu.CompilerParams(vmem_limit_bytes=8 * 1024 * 1024),
         name="pack",
     )(block, labels)
 
@@ -377,8 +375,8 @@
     lo, hi = shifted(own, "z", 1), shifted(own, "z", -1)
     far_lo, far_hi = shifted(own[group - extra :], "z", 2), shifted(own[:extra], "z", -2)
 
-    bounds = jnp.stack([filter_low, filter_high])
-    pair = filtered_and_applied(bounds, far_lo, lo, own, hi, far_hi, blocks)
+    lowest, highest = jnp.reshape(filter_low, (1,)), jnp.reshape(filter_high, (1,))
+    pair = filtered_and_applied(lowest, highest, far_lo, lo, own, hi, far_hi, blocks)
     pair = pair.reshape(blocks * group, 2 * local, rows, width)
 
     pair = lax.all_to_all(pair, LAYER, 0, 0, tiled=True)

time: 115 us -> 114 us (level)
  blocking collectives: 64.4 us -> 78.8 us
  starting transfers between devices: 25.1 us -> 14.9 us
  waiting for transfers between devices: 10 us -> 6.16 us
  Pallas kernels: 10.6 us -> 8.01 us
  local copies, waits for them, and re-layouts: 0.84 us -> 2.52 us
    all_to_all x0 -> x1, blocking collectives: none -> 14.3 us  [per_device(): lax.all_to_all(packed(initial_block, labels, group), GROUP, 0, 0, tiled=T...]
    all_to_all x1 -> x0, starting transfers between devices: 10.2 us -> none  [per_device(): lax.all_to_all(packed(initial_block, labels, group), GROUP, 0, 0, tiled=T...]
    all_to_all x1 -> x0, waiting for transfers between devices: 3.87 us -> none  [per_device(): lax.all_to_all(packed(initial_block, labels, group), GROUP, 0, 0, tiled=T...]
    unnamed x1 -> x5, local copies, waits for them, and re-layouts: 0.72 us -> 2.4 us
    pallas_call x1, Pallas kernels: 1.65 us -> 0.02 us  [packed(): pl.pallas_call(pack_kernel, out_shape=jax.ShapeDtypeStruct((group, share...]
  transfers between devices with their start and end apart: 6 -> 5, of which waited for: 2 -> 1; matrix products, arithmetic and copies ran while one was open for 1% -> 1% of each run, Pallas kernels for 4% -> 3%
where the time goes in v7:
time: 114 us
  blocking collectives  78.8 us (69%)
  starting transfers between devices  14.9 us (13%)
  Pallas kernels  8.01 us (7%)
  waiting for transfers between devices  6.16 us (5%)
  local copies, waits for them, and re-layouts  2.52 us (2%)
  between operations  2.06 us (2%)
    all_to_all x1, blocking collectives, summed_over_z(): return jnp.sum(lax.all_to_all(copies, 'z', 0, 0, tiled=True), axis=0)  26 us
    all_to_all x1, blocking collectives, per_device(): pair = lax.all_to_all(pair, LAYER, 0, 0, tiled=True)  14.8 us
    all_to_all x1, blocking collectives, per_device(): lax.all_to_all(packed(initial_block, labels, group), GROUP, 0, 0, tiled=T...  14.3 us
    all_to_all x1, blocking collectives, total_over_all(): lax.all_to_all(jnp.broadcast_to(mine, partial.shape), LAYER, 0, 0, tiled=...  12.4 us
    ppermute x4, starting transfers between devices, shifted(): return lax.ppermute(value, axis, pairs)  11.5 us
    all_to_all x1, blocking collectives, total_over_all(): terms = lax.all_to_all(partial, LAYER, 0, 0, tiled=True)  11.4 us
    all_to_all x1, waiting for transfers between devices, per_device(): turned = lax.all_to_all(turned, MODE, 0, 0, tiled=True)  6.15 us
    pallas_call x1, Pallas kernels, inverse_and_turned(): pl.pallas_call(functools.partial(turn_kernel, scale), out_shape=(matrix,...  3.86 us
  transfers between devices with their start and end apart: 5, of which 1 were waited for; matrix products, arithmetic and copies ran while one was open for 1% of the time, Pallas kernels for 3%

profile of v7, /device:TPU:1, one launch (start us, length us, event | category | flops | bytes accessed | tf_op | source)
XLA Modules:
  0.0 113.6 jit_solution(2996014489178105310)
XLA Ops:
  0.6 0.0 copy-start
  0.6 0.9 copy-done
  1.6 0.0 copy-start.1
  1.6 0.8 copy-done.1
  2.3 14.3 %all_to_all.30.own = bf16[4,4,64,128]{3,2,1,0:T(8,128)(2,1)S(1)} all-to-all(bf16[4,4,64,128]{3,2,1,0:T(8,128)(2,1)S(1)} %pack.1), channel_id=1, replica_groups=mesh['z'=16,'xl'=2,'core'=2,'xh'=2,'y'=4] {'xl','core'}, dimensions={0} | all-to-all | bytes 524288 | tf_op jit(solution)/shard_map/all_to_all | solution.py:373
  16.6 1.3 %collective-permute-start.1 = (bf16[4,4,64,128]{3,2,1,0:T(8,128)(2,1)S(1)}, bf16[4,4,64,128]{3,2,1,0:T(8,128)(2,1)S(1)}, u32[]{:S(2)}, u32[]{:S(2)}) collective-permute-start(bf16[4,4,64,128]{3,2,1,0:T(8,128)(2,1)S(1)} %all_to_all.30.own), channel_id=1, source_target_pairs={{32,0},{64,32},{96,64},{128,96},{160,128},{192,160},{224,192},{256... | collective-permute-start | bytes 786440 | tf_op jit(solution)/shard_map/ppermute | solution.py:204
  17.9 4.0 %collective-permute-start = (bf16[4,4,64,128]{3,2,1,0:T(8,128)(2,1)S(1)}, bf16[4,4,64,128]{3,2,1,0:T(8,128)(2,1)S(1)}, u32[]{:S(2)}, u32[]{:S(2)}) collective-permute-start(bf16[4,4,64,128]{3,2,1,0:T(8,128)(2,1)S(1)} %all_to_all.30.own), channel_id=1, source_target_pairs={{0,32},{32,64},{64,96},{96,128},{128,160},{160,192},{192,224},{224... | collective-permute-start | bytes 786440 | tf_op jit(solution)/shard_map/ppermute | solution.py:204
  21.9 1.3 %collective-permute-start.3 = (bf16[1,4,64,128]{3,2,1,0:T(8,128)(2,1)S(1)}, bf16[1,4,64,128]{3,2,1,0:T(8,128)(2,1)S(1)}, u32[]{:S(2)}, u32[]{:S(2)}) collective-permute-start(bf16[1,4,64,128]{3,2,1,0:T(8,128)(2,1)S(1)} %get-tuple-element.22), channel_id=1, source_target_pairs={{64,0},{96,32},{128,64},{160,96},{192,128},{224,160},{256,192},{28... | collective-permute-start | bytes 196616 | tf_op jit(solution)/shard_map/ppermute | solution.py:204
  23.2 4.9 %collective-permute-start.2 = (bf16[1,4,64,128]{3,2,1,0:T(8,128)(2,1)S(1)}, bf16[1,4,64,128]{3,2,1,0:T(8,128)(2,1)S(1)}, u32[]{:S(2)}, u32[]{:S(2)}) collective-permute-start(bf16[1,4,64,128]{3,2,1,0:T(8,128)(2,1)S(1)} %get-tuple-element.23), channel_id=1, source_target_pairs={{0,64},{32,96},{64,128},{96,160},{128,192},{160,224},{192,256},{22... | collective-permute-start | bytes 196616 | tf_op jit(solution)/shard_map/ppermute | solution.py:204
  29.4 0.0 collective-permute-done.1.hi
  29.4 0.0 collective-permute-done.lo
  29.4 3.7 %chebyshev_filter.1 = (bf16[8,4,6,8,128]{4,3,2,1,0:T(8,128)(2,1)S(1)}, f32[2,3,64,128]{3,2,1,0:T(8,128)S(1)}, f32[2,64,128]{2,1,0:T(8,128)S(1)}) custom-call(f32[1]{0:T(128)} %bitcast.22.lowest, f32[1]{0:T(128)} %bitcast.23.highest, bf16[4,4,64,128]{3,2,1,0:T(8,128)(2,1)S(1)} %collective-permute-done.lo, bf16[4,4,64,128]{3,2,1,0:T(8,128)(2,1)S(1)} %all_to_all.30.own, ...), custom_call_target="tpu_custom_call" | custom-call | flops 34406400 | bytes 2752512 | tf_op jit(solution)/shard_map/chebyshev_filter/pallas_call | solution.py:154
  33.1 0.0 collective-permute-done.3.far_hi
  33.1 0.0 collective-permute-done.2.far_lo
  33.1 0.1 outermost_planes.1
  33.2 14.8 %all_to_all.31 = bf16[32,6,8,128]{3,2,1,0:T(8,128)(2,1)S(1)} all-to-all(bf16[32,6,8,128]{3,2,1,0:T(8,128)(2,1)S(1)} %bitcast.24), channel_id=1, replica_groups=mesh['z'=16,'xl'=2,'core'=2,'xh'=2,'y'=4] {'xh','y','xl','core'}, dimensions={0} | all-to-all | bytes 786432 | tf_op jit(solution)/shard_map/all_to_all | solution.py:382
  48.1 0.4 packed_terms.1
  48.5 11.4 %all_to_all.32 = f32[32,4,128]{2,1,0:T(4,128)S(1)} all-to-all(f32[32,4,128]{2,1,0:T(4,128)S(1)} %packed_terms.1), channel_id=1, replica_groups=mesh['z'=16,'xl'=2,'core'=2,'xh'=2,'y'=4] {'xh','y','xl','core'}, dimensions={0} | all-to-all | bytes 131072 | tf_op jit(solution)/shard_map/all_to_all | solution.py:262
  59.9 26.0 %all_to_all.33 = f32[16,4,128]{2,1,0:T(4,128)S(1)} all-to-all(f32[16,4,128]{2,1,0:T(4,128)S(1)} %broadcast_in_dim.6), channel_id=1, replica_groups=mesh['z'=16,'xl'=2,'core'=2,'xh'=2,'y'=4] {'z'}, dimensions={0} | all-to-all | bytes 65536 | tf_op jit(solution)/shard_map/all_to_all | solution.py:209
  86.0 12.4 %all_to_all.34.whole = f32[32,4,128]{2,1,0:T(4,128)S(1)} all-to-all(f32[32,4,128]{2,1,0:T(4,128)S(1)} %broadcast_in_dim.7), channel_id=1, replica_groups=mesh['z'=16,'xl'=2,'core'=2,'xh'=2,'y'=4] {'xh','y','xl','core'}, dimensions={0} | all-to-all | bytes 131072 | tf_op jit(solution)/shard_map/all_to_all | solution.py:264
  98.3 3.9 %inverse_and_turned.1 = (f32[96,96]{1,0:T(8,128)S(1)}, f32[96,96]{1,0:T(8,128)S(1)}, bf16[8,12,8,128]{3,2,1,0:T(8,128)(2,1)}) custom-call(f32[32,4,128]{2,1,0:T(4,128)S(1)} %all_to_all.34.whole, bf16[96,1024]{1,0:T(8,128)(2,1)S(1)} %get-tuple-element.25.filtered), custom_call_target="tpu_custom_call" | custom-call | tf_op jit(solution)/shard_map/inverse_and_turned/pallas_call | solution.py:346
  102.2 3.4 %all-to-all-start.5 = ((bf16[8,12,8,128]{3,2,1,0:T(8,128)(2,1)}), bf16[8,12,8,128]{3,2,1,0:T(8,128)(2,1)S(1)}, u32[]{:S(2)}, u32[]{:S(2)}) async-start(bf16[8,12,8,128]{3,2,1,0:T(8,128)(2,1)} %get-tuple-element.11), calls=%async_computation.5 | async-start | bytes 393216 | tf_op jit(solution)/shard_map/all_to_all | solution.py:388
  105.6 0.2 fusion.2
  105.8 0.8 fusion.3
  106.7 6.1 %all-to-all-done.5 = bf16[8,12,8,128]{3,2,1,0:T(8,128)(2,1)S(1)} async-done(((bf16[8,12,8,128]{3,2,1,0:T(8,128)(2,1)}), bf16[8,12,8,128]{3,2,1,0:T(8,128)(2,1)S(1)}, u32[]{:S(2)}, u32[]{:S(2)}) %all-to-all-start.5) | async-done | bytes 196640 | tf_op jit(solution)/shard_map/all_to_all | solution.py:388
  112.8 0.7 copy_bitcast_fusion.2
  (8 shorter events, 0.2 us)
Async XLA Ops:
  0.6 0.9 copy-start
  1.6 0.8 copy-start.1
  16.6 12.8 %collective-permute-start.1 = (bf16[4,4,64,128]{3,2,1,0:T(8,128)(2,1)S(1)}, bf16[4,4,64,128]{3,2,1,0:T(8,128)(2,1)S(1)}, u32[]{:S(2)}, u32[]{:S(2)}) collective-permute-start(bf16[4,4,64,128]{3,2,1,0:T(8,128)(2,1)S(1)} %all_to_all.30.own), channel_id=1, source_target_pairs={{32,0},{64,32},{96,64},{128,96},{160,128},{192,160},{224,192},{256... | collective-permute-start | bytes 786440 | tf_op jit(solution)/shard_map/ppermute | solution.py:204
  17.9 11.5 %collective-permute-start = (bf16[4,4,64,128]{3,2,1,0:T(8,128)(2,1)S(1)}, bf16[4,4,64,128]{3,2,1,0:T(8,128)(2,1)S(1)}, u32[]{:S(2)}, u32[]{:S(2)}) collective-permute-start(bf16[4,4,64,128]{3,2,1,0:T(8,128)(2,1)S(1)} %all_to_all.30.own), channel_id=1, source_target_pairs={{0,32},{32,64},{64,96},{96,128},{128,160},{160,192},{192,224},{224... | collective-permute-start | bytes 786440 | tf_op jit(solution)/shard_map/ppermute | solution.py:204
  21.9 11.2 %collective-permute-start.3 = (bf16[1,4,64,128]{3,2,1,0:T(8,128)(2,1)S(1)}, bf16[1,4,64,128]{3,2,1,0:T(8,128)(2,1)S(1)}, u32[]{:S(2)}, u32[]{:S(2)}) collective-permute-start(bf16[1,4,64,128]{3,2,1,0:T(8,128)(2,1)S(1)} %get-tuple-element.22), channel_id=1, source_target_pairs={{64,0},{96,32},{128,64},{160,96},{192,128},{224,160},{256,192},{28... | collective-permute-start | bytes 196616 | tf_op jit(solution)/shard_map/ppermute | solution.py:204
  23.2 9.9 %collective-permute-start.2 = (bf16[1,4,64,128]{3,2,1,0:T(8,128)(2,1)S(1)}, bf16[1,4,64,128]{3,2,1,0:T(8,128)(2,1)S(1)}, u32[]{:S(2)}, u32[]{:S(2)}) collective-permute-start(bf16[1,4,64,128]{3,2,1,0:T(8,128)(2,1)S(1)} %get-tuple-element.23), channel_id=1, source_target_pairs={{0,64},{32,96},{64,128},{96,160},{128,192},{160,224},{192,256},{22... | collective-permute-start | bytes 196616 | tf_op jit(solution)/shard_map/ppermute | solution.py:204
  102.2 10.6 %all-to-all-start.5 = ((bf16[8,12,8,128]{3,2,1,0:T(8,128)(2,1)}), bf16[8,12,8,128]{3,2,1,0:T(8,128)(2,1)S(1)}, u32[]{:S(2)}, u32[]{:S(2)}) async-start(bf16[8,12,8,128]{3,2,1,0:T(8,128)(2,1)} %get-tuple-element.11), calls=%async_computation.5 | async-start | bytes 393216 | tf_op jit(solution)/shard_map/all_to_all | solution.py:388

commit v8 on v7

--- a/solution.py
+++ b/solution.py
@@ -32,12 +32,12 @@
     return jnp.where(label == 3.0, 1.0 / ROOTS[3], value)
 
 
-def filter_kernel(lowest, highest, lo, own, hi, out, short, share, even, odd, strong, square, degree):
+def filter_kernel(bounds, lo, own, hi, out, short, share, even, odd, strong, square, degree):
     planes, height, width = degree.shape
     local = even.shape[1]
     rows = out.shape[3]
     depth = own.shape[0]
-    low, high = lowest[0], highest[0]
+    low, high = bounds[0:1], bounds[1:2]
     centre = 0.5 * (high + low)
     scale = 1.0 / (0.5 * (high - low))
     inner = pl.ds(SUBLANES, height)
@@ -141,7 +141,7 @@
             out[:, index, local + mode] = image.reshape(-1, rows, width).astype(out.dtype)
 
 
-def filtered_and_applied(lowest, highest, far_lo, lo, own, hi, far_hi, blocks):
+def filtered_and_applied(bounds, far_lo, lo, own, hi, far_hi, blocks):
     depth, fields, height, width = own.shape
     local = fields - 1
     planes = depth + 2 * REACH
@@ -158,13 +158,13 @@
             jax.ShapeDtypeStruct((2, local, height, width), jnp.float32),
             jax.ShapeDtypeStruct((2, height, width), jnp.float32),
         ),
-        in_specs=[pl.BlockSpec(memory_space=pltpu.SMEM)] * 2 + [vmem] * 3,
+        in_specs=[vmem] * 4,
         out_specs=(vmem,) * 3,
         scratch_shapes=[rimmed, rimmed, root, flat, flat],
         compiler_params=pltpu.CompilerParams(vmem_limit_bytes=40 * 1024 * 1024),
         cost_estimate=pl.CostEstimate(flops=100 * steps, bytes_accessed=8 * steps, transcendentals=0),
         name="chebyshev_filter",
-    )(lowest, highest, lo, own, hi)
+    )(bounds, lo, own, hi)
     return pl.pallas_call(
         finish_kernel,
         out_shape=whole,
@@ -193,9 +193,29 @@
         out_shape=jax.ShapeDtypeStruct((group, share // group + 1, height, width), block.dtype),
         in_specs=[vmem, vmem],
         out_specs=vmem,
-        compiler_params=pltpu.CompilerParams(vmem_limit_bytes=8 * 1024 * 1024),
+        compiler_params=pltpu.CompilerParams(vmem_limit_bytes=8192 * 1024),
         name="pack",
     )(block, labels)
+
+
+def outer_kernel(low, high, own, first, last, bounds):
+    first[...] = own[: first.shape[0]]
+    last[...] = own[own.shape[0] - last.shape[0] :]
+    row = lax.broadcasted_iota(jnp.int32, bounds.shape, 0)
+    bounds[...] = jnp.where(row == 0, low[0], high[0])
+
+
+def outer_planes(filter_low, filter_high, own, extra):
+    vmem, smem = pl.BlockSpec(memory_space=pltpu.VMEM), pl.BlockSpec(memory_space=pltpu.SMEM)
+    plane = jax.ShapeDtypeStruct((extra,) + own.shape[1:], own.dtype)
+    return pl.pallas_call(
+        outer_kernel,
+        out_shape=(plane, plane, jax.ShapeDtypeStruct((SUBLANES, own.shape[-1]), jnp.float32)),
+        in_specs=[smem, smem, vmem],
+        out_specs=(vmem,) * 3,
+        compiler_params=pltpu.CompilerParams(vmem_limit_bytes=8 * 1024 * 1024),
+        name="outer_planes",
+    )(jnp.reshape(filter_low, (1,)), jnp.reshape(filter_high, (1,)), own)
 
 
 def shifted(value, axis, step):
@@ -373,10 +393,10 @@
     own = lax.all_to_all(packed(initial_block, labels, group), GROUP, 0, 0, tiled=True)
     extra = REACH - group
     lo, hi = shifted(own, "z", 1), shifted(own, "z", -1)
-    far_lo, far_hi = shifted(own[group - extra :], "z", 2), shifted(own[:extra], "z", -2)
-
-    lowest, highest = jnp.reshape(filter_low, (1,)), jnp.reshape(filter_high, (1,))
-    pair = filtered_and_applied(lowest, highest, far_lo, lo, own, hi, far_hi, blocks)
+    first, last, bounds = outer_planes(filter_low, filter_high, own, extra)
+    far_lo, far_hi = shifted(last, "z", 2), shifted(first, "z", -2)
+
+    pair = filtered_and_applied(bounds, far_lo, lo, own, hi, far_hi, blocks)
     pair = pair.reshape(blocks * group, 2 * local, rows, width)
 
     pair = lax.all_to_all(pair, LAYER, 0, 0, tiled=True)

time: 114 us -> 114 us (level)
  starting transfers between devices: 14.9 us -> 11.3 us
  blocking collectives: 78.8 us -> 81.2 us
  waiting for transfers between devices: 6.16 us -> 7.51 us
    all_to_all x1, blocking collectives: 14.8 us -> 19.3 us  [per_device(): pair = lax.all_to_all(pair, LAYER, 0, 0, tiled=True)]
    ppermute x4, starting transfers between devices: 11.5 us -> 7.87 us  [shifted(): return lax.ppermute(value, axis, pairs)]
    all_to_all x1, blocking collectives: 26 us -> 23.9 us  [summed_over_z(): return jnp.sum(lax.all_to_all(copies, 'z', 0, 0, tiled=True), axis=0)]
    ppermute x4, waiting for transfers between devices: 0.01 us -> 1.37 us  [shifted(): return lax.ppermute(value, axis, pairs)]
  transfers between devices with their start and end apart: 5 -> 5, of which waited for: 1 -> 3; matrix products, arithmetic and copies ran while one was open for 1% -> 1% of each run, Pallas kernels for 3% -> 3%
where the time goes in v8:
time: 114 us
  blocking collectives  81.2 us (71%)
  starting transfers between devices  11.3 us (10%)
  Pallas kernels  7.98 us (7%)
  waiting for transfers between devices  7.51 us (7%)
  local copies, waits for them, and re-layouts  2.51 us (2%)
  between operations  2.05 us (2%)
    all_to_all x1, blocking collectives, summed_over_z(): return jnp.sum(lax.all_to_all(copies, 'z', 0, 0, tiled=True), axis=0)  23.9 us
    all_to_all x1, blocking collectives, per_device(): pair = lax.all_to_all(pair, LAYER, 0, 0, tiled=True)  19.3 us
    all_to_all x1, blocking collectives, per_device(): lax.all_to_all(packed(initial_block, labels, group), GROUP, 0, 0, tiled=T...  14.3 us
    all_to_all x1, blocking collectives, total_over_all(): lax.all_to_all(jnp.broadcast_to(mine, partial.shape), LAYER, 0, 0, tiled=...  12.4 us
    all_to_all x1, blocking collectives, total_over_all(): terms = lax.all_to_all(partial, LAYER, 0, 0, tiled=True)  11.4 us
    ppermute x4, starting transfers between devices, shifted(): return lax.ppermute(value, axis, pairs)  7.87 us
    all_to_all x1, waiting for transfers between devices, per_device(): turned = lax.all_to_all(turned, MODE, 0, 0, tiled=True)  6.15 us
    pallas_call x1, Pallas kernels, inverse_and_turned(): pl.pallas_call(functools.partial(turn_kernel, scale), out_shape=(matrix,...  3.86 us
  transfers between devices with their start and end apart: 5, of which 3 were waited for; matrix products, arithmetic and copies ran while one was open for 1% of the time, Pallas kernels for 3%

profile of v8, /device:TPU:1, one launch (start us, length us, event | category | flops | bytes accessed | tf_op | source)
XLA Modules:
  0.0 113.6 jit_solution(6136294042473330594)
XLA Ops:
  0.6 0.0 copy-start
  0.6 0.9 copy-done
  1.6 0.0 copy-start.1
  1.6 0.8 copy-done.1
  2.3 14.3 %all_to_all.30.own = bf16[4,4,64,128]{3,2,1,0:T(8,128)(2,1)S(1)} all-to-all(bf16[4,4,64,128]{3,2,1,0:T(8,128)(2,1)S(1)} %pack.1), channel_id=1, replica_groups=mesh['z'=16,'xl'=2,'core'=2,'xh'=2,'y'=4] {'xl','core'}, dimensions={0} | all-to-all | bytes 524288 | tf_op jit(solution)/shard_map/all_to_all | solution.py:393
  16.6 1.3 %collective-permute-start.1 = (bf16[4,4,64,128]{3,2,1,0:T(8,128)(2,1)S(1)}, bf16[4,4,64,128]{3,2,1,0:T(8,128)(2,1)S(1)}, u32[]{:S(2)}, u32[]{:S(2)}) collective-permute-start(bf16[4,4,64,128]{3,2,1,0:T(8,128)(2,1)S(1)} %all_to_all.30.own), channel_id=1, source_target_pairs={{32,0},{64,32},{96,64},{128,96},{160,128},{192,160},{224,192},{256... | collective-permute-start | bytes 786440 | tf_op jit(solution)/shard_map/ppermute | solution.py:224
  17.9 4.0 %collective-permute-start = (bf16[4,4,64,128]{3,2,1,0:T(8,128)(2,1)S(1)}, bf16[4,4,64,128]{3,2,1,0:T(8,128)(2,1)S(1)}, u32[]{:S(2)}, u32[]{:S(2)}) collective-permute-start(bf16[4,4,64,128]{3,2,1,0:T(8,128)(2,1)S(1)} %all_to_all.30.own), channel_id=1, source_target_pairs={{0,32},{32,64},{64,96},{96,128},{128,160},{160,192},{192,224},{224... | collective-permute-start | bytes 786440 | tf_op jit(solution)/shard_map/ppermute | solution.py:224
  23.2 1.3 %collective-permute-start.2 = (bf16[1,4,64,128]{3,2,1,0:T(8,128)(2,1)S(1)}, bf16[1,4,64,128]{3,2,1,0:T(8,128)(2,1)S(1)}, u32[]{:S(2)}, u32[]{:S(2)}) collective-permute-start(bf16[1,4,64,128]{3,2,1,0:T(8,128)(2,1)S(1)} %get-tuple-element.11), channel_id=1, source_target_pairs={{0,64},{32,96},{64,128},{96,160},{128,192},{160,224},{192,256},{22... | collective-permute-start | bytes 196616 | tf_op jit(solution)/shard_map/ppermute | solution.py:224
  24.5 1.3 %collective-permute-start.3 = (bf16[1,4,64,128]{3,2,1,0:T(8,128)(2,1)S(1)}, bf16[1,4,64,128]{3,2,1,0:T(8,128)(2,1)S(1)}, u32[]{:S(2)}, u32[]{:S(2)}) collective-permute-start(bf16[1,4,64,128]{3,2,1,0:T(8,128)(2,1)S(1)} %get-tuple-element.12), channel_id=1, source_target_pairs={{64,0},{96,32},{128,64},{160,96},{192,128},{224,160},{256,192},{28... | collective-permute-start | bytes 196616 | tf_op jit(solution)/shard_map/ppermute | solution.py:224
  25.8 0.0 collective-permute-done.1.hi
  25.8 0.3 collective-permute-done.lo
  26.1 3.6 %chebyshev_filter.1 = (bf16[8,4,6,8,128]{4,3,2,1,0:T(8,128)(2,1)S(1)}, f32[2,3,64,128]{3,2,1,0:T(8,128)S(1)}, f32[2,64,128]{2,1,0:T(8,128)S(1)}) custom-call(f32[8,128]{1,0:T(8,128)S(1)} %get-tuple-element.13.bounds, bf16[4,4,64,128]{3,2,1,0:T(8,128)(2,1)S(1)} %collective-permute-done.lo, bf16[4,4,64,128]{3,2,1,0:T(8,128)(2,1)S(1)} %all_to_all.30.own, ...), custom_call_target="tpu_custom_call" | custom-call | flops 34406400 | bytes 2752512 | tf_op jit(solution)/shard_map/chebyshev_filter/pallas_call | solution.py:154
  29.8 0.0 collective-permute-done.2.far_lo
  29.8 1.0 collective-permute-done.3.far_hi
  30.9 0.1 outermost_planes.1
  30.9 19.3 %all_to_all.31 = bf16[32,6,8,128]{3,2,1,0:T(8,128)(2,1)S(1)} all-to-all(bf16[32,6,8,128]{3,2,1,0:T(8,128)(2,1)S(1)} %bitcast.24), channel_id=1, replica_groups=mesh['z'=16,'xl'=2,'core'=2,'xh'=2,'y'=4] {'xh','y','xl','core'}, dimensions={0} | all-to-all | bytes 786432 | tf_op jit(solution)/shard_map/all_to_all | solution.py:402
  50.3 0.3 packed_terms.1
  50.7 11.4 %all_to_all.32 = f32[32,4,128]{2,1,0:T(4,128)S(1)} all-to-all(f32[32,4,128]{2,1,0:T(4,128)S(1)} %packed_terms.1), channel_id=1, replica_groups=mesh['z'=16,'xl'=2,'core'=2,'xh'=2,'y'=4] {'xh','y','xl','core'}, dimensions={0} | all-to-all | bytes 131072 | tf_op jit(solution)/shard_map/all_to_all | solution.py:282
  62.1 23.9 %all_to_all.33 = f32[16,4,128]{2,1,0:T(4,128)S(1)} all-to-all(f32[16,4,128]{2,1,0:T(4,128)S(1)} %broadcast_in_dim.6), channel_id=1, replica_groups=mesh['z'=16,'xl'=2,'core'=2,'xh'=2,'y'=4] {'z'}, dimensions={0} | all-to-all | bytes 65536 | tf_op jit(solution)/shard_map/all_to_all | solution.py:229
  86.0 12.4 %all_to_all.34.whole = f32[32,4,128]{2,1,0:T(4,128)S(1)} all-to-all(f32[32,4,128]{2,1,0:T(4,128)S(1)} %broadcast_in_dim.7), channel_id=1, replica_groups=mesh['z'=16,'xl'=2,'core'=2,'xh'=2,'y'=4] {'xh','y','xl','core'}, dimensions={0} | all-to-all | bytes 131072 | tf_op jit(solution)/shard_map/all_to_all | solution.py:284
  98.4 3.9 %inverse_and_turned.1 = (f32[96,96]{1,0:T(8,128)S(1)}, f32[96,96]{1,0:T(8,128)S(1)}, bf16[8,12,8,128]{3,2,1,0:T(8,128)(2,1)}) custom-call(f32[32,4,128]{2,1,0:T(4,128)S(1)} %all_to_all.34.whole, bf16[96,1024]{1,0:T(8,128)(2,1)S(1)} %get-tuple-element.29.filtered), custom_call_target="tpu_custom_call" | custom-call | tf_op jit(solution)/shard_map/inverse_and_turned/pallas_call | solution.py:366
  102.3 3.4 %all-to-all-start.5 = ((bf16[8,12,8,128]{3,2,1,0:T(8,128)(2,1)}), bf16[8,12,8,128]{3,2,1,0:T(8,128)(2,1)S(1)}, u32[]{:S(2)}, u32[]{:S(2)}) async-start(bf16[8,12,8,128]{3,2,1,0:T(8,128)(2,1)} %get-tuple-element.17), calls=%async_computation.5 | async-start | bytes 393216 | tf_op jit(solution)/shard_map/all_to_all | solution.py:408
  105.7 0.2 fusion.1
  105.9 0.8 fusion.2
  106.8 6.1 %all-to-all-done.5 = bf16[8,12,8,128]{3,2,1,0:T(8,128)(2,1)S(1)} async-done(((bf16[8,12,8,128]{3,2,1,0:T(8,128)(2,1)}), bf16[8,12,8,128]{3,2,1,0:T(8,128)(2,1)S(1)}, u32[]{:S(2)}, u32[]{:S(2)}) %all-to-all-start.5) | async-done | bytes 196640 | tf_op jit(solution)/shard_map/all_to_all | solution.py:408
  112.9 0.7 copy_bitcast_fusion.2
  (8 shorter events, 0.2 us)
Async XLA Ops:
  0.6 0.9 copy-start
  1.6 0.8 copy-start.1
  16.6 9.2 %collective-permute-start.1 = (bf16[4,4,64,128]{3,2,1,0:T(8,128)(2,1)S(1)}, bf16[4,4,64,128]{3,2,1,0:T(8,128)(2,1)S(1)}, u32[]{:S(2)}, u32[]{:S(2)}) collective-permute-start(bf16[4,4,64,128]{3,2,1,0:T(8,128)(2,1)S(1)} %all_to_all.30.own), channel_id=1, source_target_pairs={{32,0},{64,32},{96,64},{128,96},{160,128},{192,160},{224,192},{256... | collective-permute-start | bytes 786440 | tf_op jit(solution)/shard_map/ppermute | solution.py:224
  17.9 8.3 %collective-permute-start = (bf16[4,4,64,128]{3,2,1,0:T(8,128)(2,1)S(1)}, bf16[4,4,64,128]{3,2,1,0:T(8,128)(2,1)S(1)}, u32[]{:S(2)}, u32[]{:S(2)}) collective-permute-start(bf16[4,4,64,128]{3,2,1,0:T(8,128)(2,1)S(1)} %all_to_all.30.own), channel_id=1, source_target_pairs={{0,32},{32,64},{64,96},{96,128},{128,160},{160,192},{192,224},{224... | collective-permute-start | bytes 786440 | tf_op jit(solution)/shard_map/ppermute | solution.py:224
  23.2 6.6 %collective-permute-start.2 = (bf16[1,4,64,128]{3,2,1,0:T(8,128)(2,1)S(1)}, bf16[1,4,64,128]{3,2,1,0:T(8,128)(2,1)S(1)}, u32[]{:S(2)}, u32[]{:S(2)}) collective-permute-start(bf16[1,4,64,128]{3,2,1,0:T(8,128)(2,1)S(1)} %get-tuple-element.11), channel_id=1, source_target_pairs={{0,64},{32,96},{64,128},{96,160},{128,192},{160,224},{192,256},{22... | collective-permute-start | bytes 196616 | tf_op jit(solution)/shard_map/ppermute | solution.py:224
  24.5 6.3 %collective-permute-start.3 = (bf16[1,4,64,128]{3,2,1,0:T(8,128)(2,1)S(1)}, bf16[1,4,64,128]{3,2,1,0:T(8,128)(2,1)S(1)}, u32[]{:S(2)}, u32[]{:S(2)}) collective-permute-start(bf16[1,4,64,128]{3,2,1,0:T(8,128)(2,1)S(1)} %get-tuple-element.12), channel_id=1, source_target_pairs={{64,0},{96,32},{128,64},{160,96},{192,128},{224,160},{256,192},{28... | collective-permute-start | bytes 196616 | tf_op jit(solution)/shard_map/ppermute | solution.py:224
  102.3 10.6 %all-to-all-start.5 = ((bf16[8,12,8,128]{3,2,1,0:T(8,128)(2,1)}), bf16[8,12,8,128]{3,2,1,0:T(8,128)(2,1)S(1)}, u32[]{:S(2)}, u32[]{:S(2)}) async-start(bf16[8,12,8,128]{3,2,1,0:T(8,128)(2,1)} %get-tuple-element.17), calls=%async_computation.5 | async-start | bytes 393216 | tf_op jit(solution)/shard_map/all_to_all | solution.py:408

commit v9 on v7

--- a/solution.py
+++ b/solution.py
@@ -264,7 +264,7 @@
     return lax.all_to_all(jnp.broadcast_to(mine, partial.shape), LAYER, 0, 0, tiled=True)
 
 
-def turn_kernel(scale, whole, filtered, inverse, crossed, turned, staged, square):
+def turn_kernel(scale, whole, filtered, projected, turned, inverse, crossed, result, staged, square, written):
     size = inverse.shape[0]
     rows = turned.shape[2]
     groups = size // SUBLANES
@@ -330,36 +330,46 @@
                     columns[s][g - b] = columns[s][g - b] - weight * row_column
         inverse[first : first + SUBLANES, :] = (right[b] * lax.rsqrt(diagonal))[:, :size]
 
+    contract = (((1,), (1,)), ((), ()))
+    exact = dict(precision=lax.Precision.HIGHEST, preferred_element_type=jnp.float32)
+    half = lax.dot_general(inverse[...], crossed[...], contract, **exact)
+    result[...] = lax.dot_general(half, inverse[...], contract, **exact)
+    write = pltpu.make_async_copy(result, projected, written)
+    write.start()
+
     rotation = inverse[...].astype(jnp.bfloat16)
     product = jnp.dot(rotation, filtered[...], preferred_element_type=jnp.float32) * scale
     width = turned.shape[3]
     for row in range(rows):
         staged[pl.ds(row, size, stride=rows), :] = product[:, row * width : (row + 1) * width]
     turned[...] = staged[...].reshape(turned.shape).astype(turned.dtype)
-
-
-def inverse_and_turned(whole, filtered, scale, peers, rows):
+    write.wait()
+
+
+def projected_and_turned(whole, filtered, scale, peers, rows):
     size = filtered.shape[0]
     width = filtered.shape[1] // rows
     vmem = pl.BlockSpec(memory_space=pltpu.VMEM)
-    matrix = jax.ShapeDtypeStruct((size, size), jnp.float32)
+    matrix = pltpu.VMEM((size, size), jnp.float32)
     return pl.pallas_call(
         functools.partial(turn_kernel, scale),
-        out_shape=(matrix, matrix, jax.ShapeDtypeStruct((peers, size // peers, rows, width), jnp.bfloat16)),
+        out_shape=(
+            jax.ShapeDtypeStruct((size, size), jnp.float32),
+            jax.ShapeDtypeStruct((peers, size // peers, rows, width), jnp.bfloat16),
+        ),
         in_specs=[vmem, vmem],
-        out_specs=(vmem, vmem, vmem),
-        scratch_shapes=[pltpu.VMEM((size * rows, width), jnp.float32), pltpu.VMEM((LANES, LANES), jnp.float32)],
+        out_specs=(pl.BlockSpec(memory_space=pl.ANY), vmem),
+        scratch_shapes=[
+            matrix,
+            matrix,
+            matrix,
+            pltpu.VMEM((size * rows, width), jnp.float32),
+            pltpu.VMEM((LANES, LANES), jnp.float32),
+            pltpu.SemaphoreType.DMA,
+        ],
         compiler_params=pltpu.CompilerParams(vmem_limit_bytes=8 * 1024 * 1024),
-        name="inverse_and_turned",
+        name="projected_and_turned",
     )(whole, filtered)
-
-
-def projection(inverse, cross):
-    return jnp.dot(
-        jnp.dot(inverse, cross, precision=lax.Precision.HIGHEST),
-        inverse.T,
-        precision=lax.Precision.HIGHEST,
-    )
 
 
 def per_device(initial_block, labels, filter_low, filter_high):
@@ -383,8 +393,7 @@
     filtered = pair[:, :local].reshape(modes, rows * width)
     applied = pair[:, local:].reshape(modes, rows * width)
     total = total_over_all(packed_terms(filtered, applied, blocks * group))
-    inverse, crossed, turned = inverse_and_turned(total, filtered, scale, blocks, rows)
-    projected = projection(inverse, crossed.T)
+    projected, turned = projected_and_turned(total, filtered, scale, blocks, rows)
     turned = lax.all_to_all(turned, MODE, 0, 0, tiled=True)
     modes_out = jnp.transpose(turned, (1, 0, 2, 3)).reshape(share, 1, height, width)
     return (modes_out, projected)

time: 114 us -> 114 us (level)
  blocking collectives: 78.8 us -> 88.7 us
  waiting for transfers between devices: 6.16 us -> 0.01 us
  starting transfers between devices: 14.9 us -> 11.5 us
    all_to_all x0 -> x1, blocking collectives: none -> 9.93 us  [per_device(): turned = lax.all_to_all(turned, MODE, 0, 0, tiled=True)]
    all_to_all x1 -> x0, waiting for transfers between devices: 6.15 us -> none  [per_device(): turned = lax.all_to_all(turned, MODE, 0, 0, tiled=True)]
    all_to_all x1 -> x0, starting transfers between devices: 3.39 us -> none  [per_device(): turned = lax.all_to_all(turned, MODE, 0, 0, tiled=True)]
  transfers between devices with their start and end apart: 5 -> 4, of which waited for: 1 -> 0; matrix products, arithmetic and copies ran while one was open for 1% -> 0% of each run, Pallas kernels for 3% -> 3%
where the time goes in v9:
time: 114 us; the launch traced here: 113 us
  blocking collectives  88.7 us (78%)
  starting transfers between devices  11.5 us (10%)
  Pallas kernels  8.25 us (7%)
  local copies, waits for them, and re-layouts  2.52 us (2%)
  between operations  2.05 us (2%)
    all_to_all x1, blocking collectives, summed_over_z(): return jnp.sum(lax.all_to_all(copies, 'z', 0, 0, tiled=True), axis=0)  26 us
    all_to_all x1, blocking collectives, per_device(): pair = lax.all_to_all(pair, LAYER, 0, 0, tiled=True)  14.8 us
    all_to_all x1, blocking collectives, per_device(): lax.all_to_all(packed(initial_block, labels, group), GROUP, 0, 0, tiled=T...  14.3 us
    all_to_all x1, blocking collectives, total_over_all(): lax.all_to_all(jnp.broadcast_to(mine, partial.shape), LAYER, 0, 0, tiled=...  12.4 us
    ppermute x4, starting transfers between devices, shifted(): return lax.ppermute(value, axis, pairs)  11.5 us
    all_to_all x1, blocking collectives, total_over_all(): terms = lax.all_to_all(partial, LAYER, 0, 0, tiled=True)  11.4 us
    all_to_all x1, blocking collectives, per_device(): turned = lax.all_to_all(turned, MODE, 0, 0, tiled=True)  9.93 us
    pallas_call x1, Pallas kernels, projected_and_turned(): pl.pallas_call(functools.partial(turn_kernel, scale), out_shape=(jax.Shap...  4.1 us
  transfers between devices with their start and end apart: 4, of which 0 were waited for; matrix products, arithmetic and copies ran while one was open for 0% of the time, Pallas kernels for 3%

profile of v9, /device:TPU:1, one launch (start us, length us, event | category | flops | bytes accessed | tf_op | source)
XLA Modules:
  0.0 113.1 jit_solution(9284112529631924654)
XLA Ops:
  0.6 0.0 copy-start
  0.6 0.9 copy-done
  1.6 0.0 copy-start.1
  1.6 0.8 copy-done.1
  2.3 14.3 %all_to_all.30.own = bf16[4,4,64,128]{3,2,1,0:T(8,128)(2,1)S(1)} all-to-all(bf16[4,4,64,128]{3,2,1,0:T(8,128)(2,1)S(1)} %pack.1), channel_id=1, replica_groups=mesh['z'=16,'xl'=2,'core'=2,'xh'=2,'y'=4] {'xl','core'}, dimensions={0} | all-to-all | bytes 524288 | tf_op jit(solution)/shard_map/all_to_all | solution.py:383
  16.6 1.3 %collective-permute-start.1 = (bf16[4,4,64,128]{3,2,1,0:T(8,128)(2,1)S(1)}, bf16[4,4,64,128]{3,2,1,0:T(8,128)(2,1)S(1)}, u32[]{:S(2)}, u32[]{:S(2)}) collective-permute-start(bf16[4,4,64,128]{3,2,1,0:T(8,128)(2,1)S(1)} %all_to_all.30.own), channel_id=1, source_target_pairs={{32,0},{64,32},{96,64},{128,96},{160,128},{192,160},{224,192},{256... | collective-permute-start | bytes 786440 | tf_op jit(solution)/shard_map/ppermute | solution.py:204
  17.9 4.0 %collective-permute-start = (bf16[4,4,64,128]{3,2,1,0:T(8,128)(2,1)S(1)}, bf16[4,4,64,128]{3,2,1,0:T(8,128)(2,1)S(1)}, u32[]{:S(2)}, u32[]{:S(2)}) collective-permute-start(bf16[4,4,64,128]{3,2,1,0:T(8,128)(2,1)S(1)} %all_to_all.30.own), channel_id=1, source_target_pairs={{0,32},{32,64},{64,96},{96,128},{128,160},{160,192},{192,224},{224... | collective-permute-start | bytes 786440 | tf_op jit(solution)/shard_map/ppermute | solution.py:204
  21.9 1.3 %collective-permute-start.3 = (bf16[1,4,64,128]{3,2,1,0:T(8,128)(2,1)S(1)}, bf16[1,4,64,128]{3,2,1,0:T(8,128)(2,1)S(1)}, u32[]{:S(2)}, u32[]{:S(2)}) collective-permute-start(bf16[1,4,64,128]{3,2,1,0:T(8,128)(2,1)S(1)} %get-tuple-element.20), channel_id=1, source_target_pairs={{64,0},{96,32},{128,64},{160,96},{192,128},{224,160},{256,192},{28... | collective-permute-start | bytes 196616 | tf_op jit(solution)/shard_map/ppermute | solution.py:204
  23.2 4.9 %collective-permute-start.2 = (bf16[1,4,64,128]{3,2,1,0:T(8,128)(2,1)S(1)}, bf16[1,4,64,128]{3,2,1,0:T(8,128)(2,1)S(1)}, u32[]{:S(2)}, u32[]{:S(2)}) collective-permute-start(bf16[1,4,64,128]{3,2,1,0:T(8,128)(2,1)S(1)} %get-tuple-element.21), channel_id=1, source_target_pairs={{0,64},{32,96},{64,128},{96,160},{128,192},{160,224},{192,256},{22... | collective-permute-start | bytes 196616 | tf_op jit(solution)/shard_map/ppermute | solution.py:204
  29.4 0.0 collective-permute-done.1.hi
  29.4 0.0 collective-permute-done.lo
  29.4 3.7 %chebyshev_filter.1 = (bf16[8,4,6,8,128]{4,3,2,1,0:T(8,128)(2,1)S(1)}, f32[2,3,64,128]{3,2,1,0:T(8,128)S(1)}, f32[2,64,128]{2,1,0:T(8,128)S(1)}) custom-call(f32[1]{0:T(128)} %bitcast.18.lowest, f32[1]{0:T(128)} %bitcast.19.highest, bf16[4,4,64,128]{3,2,1,0:T(8,128)(2,1)S(1)} %collective-permute-done.lo, bf16[4,4,64,128]{3,2,1,0:T(8,128)(2,1)S(1)} %all_to_all.30.own, ...), custom_call_target="tpu_custom_call" | custom-call | flops 34406400 | bytes 2752512 | tf_op jit(solution)/shard_map/chebyshev_filter/pallas_call | solution.py:154
  33.1 0.0 collective-permute-done.3.far_hi
  33.1 0.0 collective-permute-done.2.far_lo
  33.1 0.1 outermost_planes.1
  33.2 14.8 %all_to_all.31 = bf16[32,6,8,128]{3,2,1,0:T(8,128)(2,1)S(1)} all-to-all(bf16[32,6,8,128]{3,2,1,0:T(8,128)(2,1)S(1)} %bitcast.20), channel_id=1, replica_groups=mesh['z'=16,'xl'=2,'core'=2,'xh'=2,'y'=4] {'xh','y','xl','core'}, dimensions={0} | all-to-all | bytes 786432 | tf_op jit(solution)/shard_map/all_to_all | solution.py:392
  48.1 0.4 packed_terms.1
  48.5 11.4 %all_to_all.32 = f32[32,4,128]{2,1,0:T(4,128)S(1)} all-to-all(f32[32,4,128]{2,1,0:T(4,128)S(1)} %packed_terms.1), channel_id=1, replica_groups=mesh['z'=16,'xl'=2,'core'=2,'xh'=2,'y'=4] {'xh','y','xl','core'}, dimensions={0} | all-to-all | bytes 131072 | tf_op jit(solution)/shard_map/all_to_all | solution.py:262
  59.9 26.0 %all_to_all.33 = f32[16,4,128]{2,1,0:T(4,128)S(1)} all-to-all(f32[16,4,128]{2,1,0:T(4,128)S(1)} %broadcast_in_dim.6), channel_id=1, replica_groups=mesh['z'=16,'xl'=2,'core'=2,'xh'=2,'y'=4] {'z'}, dimensions={0} | all-to-all | bytes 65536 | tf_op jit(solution)/shard_map/all_to_all | solution.py:209
  86.0 12.4 %all_to_all.34.whole = f32[32,4,128]{2,1,0:T(4,128)S(1)} all-to-all(f32[32,4,128]{2,1,0:T(4,128)S(1)} %broadcast_in_dim.7), channel_id=1, replica_groups=mesh['z'=16,'xl'=2,'core'=2,'xh'=2,'y'=4] {'xh','y','xl','core'}, dimensions={0} | all-to-all | bytes 131072 | tf_op jit(solution)/shard_map/all_to_all | solution.py:264
  98.3 4.1 %projected_and_turned.1 = (f32[96,96]{1,0:T(8,128)}, bf16[8,12,8,128]{3,2,1,0:T(8,128)(2,1)S(1)}) custom-call(f32[32,4,128]{2,1,0:T(4,128)S(1)} %all_to_all.34.whole, bf16[96,1024]{1,0:T(8,128)(2,1)S(1)} %get-tuple-element.23.filtered), custom_call_target="tpu_custom_call" | custom-call | tf_op jit(solution)/shard_map/projected_and_turned/pallas_call | solution.py:354
  102.5 9.9 %all_to_all.35 = bf16[8,12,8,128]{3,2,1,0:T(8,128)(2,1)S(1)} all-to-all(bf16[8,12,8,128]{3,2,1,0:T(8,128)(2,1)S(1)} %get-tuple-element.10), channel_id=1, replica_groups=mesh['z'=16,'xl'=2,'core'=2,'xh'=2,'y'=4] {'xh','y'}, dimensions={0} | all-to-all | bytes 393216 | tf_op jit(solution)/shard_map/all_to_all | solution.py:397
  112.4 0.7 copy_bitcast_fusion.2
  (8 shorter events, 0.2 us)
Async XLA Ops:
  0.6 0.9 copy-start
  1.6 0.8 copy-start.1
  16.6 12.8 %collective-permute-start.1 = (bf16[4,4,64,128]{3,2,1,0:T(8,128)(2,1)S(1)}, bf16[4,4,64,128]{3,2,1,0:T(8,128)(2,1)S(1)}, u32[]{:S(2)}, u32[]{:S(2)}) collective-permute-start(bf16[4,4,64,128]{3,2,1,0:T(8,128)(2,1)S(1)} %all_to_all.30.own), channel_id=1, source_target_pairs={{32,0},{64,32},{96,64},{128,96},{160,128},{192,160},{224,192},{256... | collective-permute-start | bytes 786440 | tf_op jit(solution)/shard_map/ppermute | solution.py:204
  17.9 11.5 %collective-permute-start = (bf16[4,4,64,128]{3,2,1,0:T(8,128)(2,1)S(1)}, bf16[4,4,64,128]{3,2,1,0:T(8,128)(2,1)S(1)}, u32[]{:S(2)}, u32[]{:S(2)}) collective-permute-start(bf16[4,4,64,128]{3,2,1,0:T(8,128)(2,1)S(1)} %all_to_all.30.own), channel_id=1, source_target_pairs={{0,32},{32,64},{64,96},{96,128},{128,160},{160,192},{192,224},{224... | collective-permute-start | bytes 786440 | tf_op jit(solution)/shard_map/ppermute | solution.py:204
  21.9 11.2 %collective-permute-start.3 = (bf16[1,4,64,128]{3,2,1,0:T(8,128)(2,1)S(1)}, bf16[1,4,64,128]{3,2,1,0:T(8,128)(2,1)S(1)}, u32[]{:S(2)}, u32[]{:S(2)}) collective-permute-start(bf16[1,4,64,128]{3,2,1,0:T(8,128)(2,1)S(1)} %get-tuple-element.20), channel_id=1, source_target_pairs={{64,0},{96,32},{128,64},{160,96},{192,128},{224,160},{256,192},{28... | collective-permute-start | bytes 196616 | tf_op jit(solution)/shard_map/ppermute | solution.py:204
  23.2 9.9 %collective-permute-start.2 = (bf16[1,4,64,128]{3,2,1,0:T(8,128)(2,1)S(1)}, bf16[1,4,64,128]{3,2,1,0:T(8,128)(2,1)S(1)}, u32[]{:S(2)}, u32[]{:S(2)}) collective-permute-start(bf16[1,4,64,128]{3,2,1,0:T(8,128)(2,1)S(1)} %get-tuple-element.21), channel_id=1, source_target_pairs={{0,64},{32,96},{64,128},{96,160},{128,192},{160,224},{192,256},{22... | collective-permute-start | bytes 196616 | tf_op jit(solution)/shard_map/ppermute | solution.py:204

commit v10 on v9

--- a/solution.py
+++ b/solution.py
@@ -37,7 +37,7 @@
     local = even.shape[1]
     rows = out.shape[3]
     depth = own.shape[0]
-    low, high = lowest[0], highest[0]
+    low, high = lowest[...], highest[...]
     centre = 0.5 * (high + low)
     scale = 1.0 / (0.5 * (high - low))
     inner = pl.ds(SUBLANES, height)
@@ -385,7 +385,7 @@
     lo, hi = shifted(own, "z", 1), shifted(own, "z", -1)
     far_lo, far_hi = shifted(own[group - extra :], "z", 2), shifted(own[:extra], "z", -2)
 
-    lowest, highest = jnp.reshape(filter_low, (1,)), jnp.reshape(filter_high, (1,))
+    lowest, highest = filter_low, filter_high
     pair = filtered_and_applied(lowest, highest, far_lo, lo, own, hi, far_hi, blocks)
     pair = pair.reshape(blocks * group, 2 * local, rows, width)
 

time: 114 us -> 114 us (level)
  no operation moved by 1% of the time
where the time goes in v10:
time: 114 us; the launch traced here: 113 us
  blocking collectives  88.7 us (78%)
  starting transfers between devices  11.5 us (10%)
  Pallas kernels  8.25 us (7%)
  local copies, waits for them, and re-layouts  2.52 us (2%)
  between operations  2.05 us (2%)
    all_to_all x1, blocking collectives, summed_over_z(): return jnp.sum(lax.all_to_all(copies, 'z', 0, 0, tiled=True), axis=0)  26 us
    all_to_all x1, blocking collectives, per_device(): pair = lax.all_to_all(pair, LAYER, 0, 0, tiled=True)  14.8 us
    all_to_all x1, blocking collectives, per_device(): lax.all_to_all(packed(initial_block, labels, group), GROUP, 0, 0, tiled=T...  14.3 us
    all_to_all x1, blocking collectives, total_over_all(): lax.all_to_all(jnp.broadcast_to(mine, partial.shape), LAYER, 0, 0, tiled=...  12.4 us
    ppermute x4, starting transfers between devices, shifted(): return lax.ppermute(value, axis, pairs)  11.5 us
    all_to_all x1, blocking collectives, total_over_all(): terms = lax.all_to_all(partial, LAYER, 0, 0, tiled=True)  11.4 us
    all_to_all x1, blocking collectives, per_device(): turned = lax.all_to_all(turned, MODE, 0, 0, tiled=True)  9.93 us
    pallas_call x1, Pallas kernels, projected_and_turned(): pl.pallas_call(functools.partial(turn_kernel, scale), out_shape=(jax.Shap...  4.1 us
  transfers between devices with their start and end apart: 4, of which 0 were waited for; matrix products, arithmetic and copies ran while one was open for 0% of the time, Pallas kernels for 3%

profile of v10, /device:TPU:1, one launch (start us, length us, event | category | flops | bytes accessed | tf_op | source)
XLA Modules:
  0.0 113.1 jit_solution(9284112529631924654)
XLA Ops:
  0.6 0.0 copy-start
  0.6 0.9 copy-done
  1.6 0.0 copy-start.1
  1.6 0.8 copy-done.1
  2.3 14.3 %all_to_all.30.own = bf16[4,4,64,128]{3,2,1,0:T(8,128)(2,1)S(1)} all-to-all(bf16[4,4,64,128]{3,2,1,0:T(8,128)(2,1)S(1)} %pack.1), channel_id=1, replica_groups=mesh['z'=16,'xl'=2,'core'=2,'xh'=2,'y'=4] {'xl','core'}, dimensions={0} | all-to-all | bytes 524288 | tf_op jit(solution)/shard_map/all_to_all | solution.py:383
  16.6 1.3 %collective-permute-start.1 = (bf16[4,4,64,128]{3,2,1,0:T(8,128)(2,1)S(1)}, bf16[4,4,64,128]{3,2,1,0:T(8,128)(2,1)S(1)}, u32[]{:S(2)}, u32[]{:S(2)}) collective-permute-start(bf16[4,4,64,128]{3,2,1,0:T(8,128)(2,1)S(1)} %all_to_all.30.own), channel_id=1, source_target_pairs={{32,0},{64,32},{96,64},{128,96},{160,128},{192,160},{224,192},{256... | collective-permute-start | bytes 786440 | tf_op jit(solution)/shard_map/ppermute | solution.py:204
  17.9 4.0 %collective-permute-start = (bf16[4,4,64,128]{3,2,1,0:T(8,128)(2,1)S(1)}, bf16[4,4,64,128]{3,2,1,0:T(8,128)(2,1)S(1)}, u32[]{:S(2)}, u32[]{:S(2)}) collective-permute-start(bf16[4,4,64,128]{3,2,1,0:T(8,128)(2,1)S(1)} %all_to_all.30.own), channel_id=1, source_target_pairs={{0,32},{32,64},{64,96},{96,128},{128,160},{160,192},{192,224},{224... | collective-permute-start | bytes 786440 | tf_op jit(solution)/shard_map/ppermute | solution.py:204
  21.9 1.3 %collective-permute-start.3 = (bf16[1,4,64,128]{3,2,1,0:T(8,128)(2,1)S(1)}, bf16[1,4,64,128]{3,2,1,0:T(8,128)(2,1)S(1)}, u32[]{:S(2)}, u32[]{:S(2)}) collective-permute-start(bf16[1,4,64,128]{3,2,1,0:T(8,128)(2,1)S(1)} %get-tuple-element.20), channel_id=1, source_target_pairs={{64,0},{96,32},{128,64},{160,96},{192,128},{224,160},{256,192},{28... | collective-permute-start | bytes 196616 | tf_op jit(solution)/shard_map/ppermute | solution.py:204
  23.2 4.9 %collective-permute-start.2 = (bf16[1,4,64,128]{3,2,1,0:T(8,128)(2,1)S(1)}, bf16[1,4,64,128]{3,2,1,0:T(8,128)(2,1)S(1)}, u32[]{:S(2)}, u32[]{:S(2)}) collective-permute-start(bf16[1,4,64,128]{3,2,1,0:T(8,128)(2,1)S(1)} %get-tuple-element.21), channel_id=1, source_target_pairs={{0,64},{32,96},{64,128},{96,160},{128,192},{160,224},{192,256},{22... | collective-permute-start | bytes 196616 | tf_op jit(solution)/shard_map/ppermute | solution.py:204
  29.4 0.0 collective-permute-done.1.hi
  29.4 0.0 collective-permute-done.lo
  29.4 3.7 %chebyshev_filter.1 = (bf16[8,4,6,8,128]{4,3,2,1,0:T(8,128)(2,1)S(1)}, f32[2,3,64,128]{3,2,1,0:T(8,128)S(1)}, f32[2,64,128]{2,1,0:T(8,128)S(1)}) custom-call(f32[]{:T(128)S(6)} %copy.19.lowest, f32[]{:T(128)S(6)} %copy.20.highest, bf16[4,4,64,128]{3,2,1,0:T(8,128)(2,1)S(1)} %collective-permute-done.lo, bf16[4,4,64,128]{3,2,1,0:T(8,128)(2,1)S(1)} %all_to_all.30.own, ...), custom_call_target="tpu_custom_call" | custom-call | flops 34406400 | bytes 2752512 | tf_op jit(solution)/shard_map/chebyshev_filter/pallas_call | solution.py:154
  33.1 0.0 collective-permute-done.3.far_hi
  33.1 0.0 collective-permute-done.2.far_lo
  33.1 0.1 outermost_planes.1
  33.2 14.8 %all_to_all.31 = bf16[32,6,8,128]{3,2,1,0:T(8,128)(2,1)S(1)} all-to-all(bf16[32,6,8,128]{3,2,1,0:T(8,128)(2,1)S(1)} %bitcast.16), channel_id=1, replica_groups=mesh['z'=16,'xl'=2,'core'=2,'xh'=2,'y'=4] {'xh','y','xl','core'}, dimensions={0} | all-to-all | bytes 786432 | tf_op jit(solution)/shard_map/all_to_all | solution.py:392
  48.1 0.4 packed_terms.1
  48.5 11.4 %all_to_all.32 = f32[32,4,128]{2,1,0:T(4,128)S(1)} all-to-all(f32[32,4,128]{2,1,0:T(4,128)S(1)} %packed_terms.1), channel_id=1, replica_groups=mesh['z'=16,'xl'=2,'core'=2,'xh'=2,'y'=4] {'xh','y','xl','core'}, dimensions={0} | all-to-all | bytes 131072 | tf_op jit(solution)/shard_map/all_to_all | solution.py:262
  59.9 26.0 %all_to_all.33 = f32[16,4,128]{2,1,0:T(4,128)S(1)} all-to-all(f32[16,4,128]{2,1,0:T(4,128)S(1)} %broadcast_in_dim.6), channel_id=1, replica_groups=mesh['z'=16,'xl'=2,'core'=2,'xh'=2,'y'=4] {'z'}, dimensions={0} | all-to-all | bytes 65536 | tf_op jit(solution)/shard_map/all_to_all | solution.py:209
  86.0 12.4 %all_to_all.34.whole = f32[32,4,128]{2,1,0:T(4,128)S(1)} all-to-all(f32[32,4,128]{2,1,0:T(4,128)S(1)} %broadcast_in_dim.7), channel_id=1, replica_groups=mesh['z'=16,'xl'=2,'core'=2,'xh'=2,'y'=4] {'xh','y','xl','core'}, dimensions={0} | all-to-all | bytes 131072 | tf_op jit(solution)/shard_map/all_to_all | solution.py:264
  98.3 4.1 %projected_and_turned.1 = (f32[96,96]{1,0:T(8,128)}, bf16[8,12,8,128]{3,2,1,0:T(8,128)(2,1)S(1)}) custom-call(f32[32,4,128]{2,1,0:T(4,128)S(1)} %all_to_all.34.whole, bf16[96,1024]{1,0:T(8,128)(2,1)S(1)} %get-tuple-element.23.filtered), custom_call_target="tpu_custom_call" | custom-call | tf_op jit(solution)/shard_map/projected_and_turned/pallas_call | solution.py:354
  102.5 9.9 %all_to_all.35 = bf16[8,12,8,128]{3,2,1,0:T(8,128)(2,1)S(1)} all-to-all(bf16[8,12,8,128]{3,2,1,0:T(8,128)(2,1)S(1)} %get-tuple-element.10), channel_id=1, replica_groups=mesh['z'=16,'xl'=2,'core'=2,'xh'=2,'y'=4] {'xh','y'}, dimensions={0} | all-to-all | bytes 393216 | tf_op jit(solution)/shard_map/all_to_all | solution.py:397
  112.4 0.7 copy_bitcast_fusion.2
  (8 shorter events, 0.2 us)
Async XLA Ops:
  0.6 0.9 copy-start
  1.6 0.8 copy-start.1
  16.6 12.8 %collective-permute-start.1 = (bf16[4,4,64,128]{3,2,1,0:T(8,128)(2,1)S(1)}, bf16[4,4,64,128]{3,2,1,0:T(8,128)(2,1)S(1)}, u32[]{:S(2)}, u32[]{:S(2)}) collective-permute-start(bf16[4,4,64,128]{3,2,1,0:T(8,128)(2,1)S(1)} %all_to_all.30.own), channel_id=1, source_target_pairs={{32,0},{64,32},{96,64},{128,96},{160,128},{192,160},{224,192},{256... | collective-permute-start | bytes 786440 | tf_op jit(solution)/shard_map/ppermute | solution.py:204
  17.9 11.5 %collective-permute-start = (bf16[4,4,64,128]{3,2,1,0:T(8,128)(2,1)S(1)}, bf16[4,4,64,128]{3,2,1,0:T(8,128)(2,1)S(1)}, u32[]{:S(2)}, u32[]{:S(2)}) collective-permute-start(bf16[4,4,64,128]{3,2,1,0:T(8,128)(2,1)S(1)} %all_to_all.30.own), channel_id=1, source_target_pairs={{0,32},{32,64},{64,96},{96,128},{128,160},{160,192},{192,224},{224... | collective-permute-start | bytes 786440 | tf_op jit(solution)/shard_map/ppermute | solution.py:204
  21.9 11.2 %collective-permute-start.3 = (bf16[1,4,64,128]{3,2,1,0:T(8,128)(2,1)S(1)}, bf16[1,4,64,128]{3,2,1,0:T(8,128)(2,1)S(1)}, u32[]{:S(2)}, u32[]{:S(2)}) collective-permute-start(bf16[1,4,64,128]{3,2,1,0:T(8,128)(2,1)S(1)} %get-tuple-element.20), channel_id=1, source_target_pairs={{64,0},{96,32},{128,64},{160,96},{192,128},{224,160},{256,192},{28... | collective-permute-start | bytes 196616 | tf_op jit(solution)/shard_map/ppermute | solution.py:204
  23.2 9.9 %collective-permute-start.2 = (bf16[1,4,64,128]{3,2,1,0:T(8,128)(2,1)S(1)}, bf16[1,4,64,128]{3,2,1,0:T(8,128)(2,1)S(1)}, u32[]{:S(2)}, u32[]{:S(2)}) collective-permute-start(bf16[1,4,64,128]{3,2,1,0:T(8,128)(2,1)S(1)} %get-tuple-element.21), channel_id=1, source_target_pairs={{0,64},{32,96},{64,128},{96,160},{128,192},{160,224},{192,256},{22... | collective-permute-start | bytes 196616 | tf_op jit(solution)/shard_map/ppermute | solution.py:204

commit v11 on v10

--- a/solution.py
+++ b/solution.py
@@ -62,7 +62,7 @@
                 odd[plane, mode, pl.ds(first, SUBLANES)] = edge
         return carry
 
-    lax.fori_loop(0, planes, clear, 0)
+    lax.fori_loop(0, planes, clear, 0, unroll=planes // 2)
 
     for plane in (0, planes - 1):
         strong[plane, inner] = jnp.zeros((height, width), jnp.float32)

time: 114 us -> 114 us (level)
  no operation moved by 1% of the time
where the time goes in v11:
time: 114 us; the launch traced here: 113 us
  blocking collectives  88.8 us (78%)
  starting transfers between devices  11.5 us (10%)
  Pallas kernels  8.22 us (7%)
  local copies, waits for them, and re-layouts  2.52 us (2%)
  between operations  2.05 us (2%)
    all_to_all x1, blocking collectives, summed_over_z(): return jnp.sum(lax.all_to_all(copies, 'z', 0, 0, tiled=True), axis=0)  26 us
    all_to_all x1, blocking collectives, per_device(): pair = lax.all_to_all(pair, LAYER, 0, 0, tiled=True)  14.8 us
    all_to_all x1, blocking collectives, per_device(): lax.all_to_all(packed(initial_block, labels, group), GROUP, 0, 0, tiled=T...  14.3 us
    all_to_all x1, blocking collectives, total_over_all(): lax.all_to_all(jnp.broadcast_to(mine, partial.shape), LAYER, 0, 0, tiled=...  12.4 us
    ppermute x4, starting transfers between devices, shifted(): return lax.ppermute(value, axis, pairs)  11.5 us
    all_to_all x1, blocking collectives, total_over_all(): terms = lax.all_to_all(partial, LAYER, 0, 0, tiled=True)  11.4 us
    all_to_all x1, blocking collectives, per_device(): turned = lax.all_to_all(turned, MODE, 0, 0, tiled=True)  9.93 us
    pallas_call x1, Pallas kernels, projected_and_turned(): pl.pallas_call(functools.partial(turn_kernel, scale), out_shape=(jax.Shap...  4.1 us
  transfers between devices with their start and end apart: 4, of which 0 were waited for; matrix products, arithmetic and copies ran while one was open for 0% of the time, Pallas kernels for 3%

profile of v11, /device:TPU:1, one launch (start us, length us, event | category | flops | bytes accessed | tf_op | source)
XLA Modules:
  0.0 113.1 jit_solution(5256216992170111926)
XLA Ops:
  0.6 0.0 copy-start
  0.6 0.9 copy-done
  1.6 0.0 copy-start.1
  1.6 0.8 copy-done.1
  2.3 14.3 %all_to_all.30.own = bf16[4,4,64,128]{3,2,1,0:T(8,128)(2,1)S(1)} all-to-all(bf16[4,4,64,128]{3,2,1,0:T(8,128)(2,1)S(1)} %pack.1), channel_id=1, replica_groups=mesh['z'=16,'xl'=2,'core'=2,'xh'=2,'y'=4] {'xl','core'}, dimensions={0} | all-to-all | bytes 524288 | tf_op jit(solution)/shard_map/all_to_all | solution.py:383
  16.6 1.3 %collective-permute-start.1 = (bf16[4,4,64,128]{3,2,1,0:T(8,128)(2,1)S(1)}, bf16[4,4,64,128]{3,2,1,0:T(8,128)(2,1)S(1)}, u32[]{:S(2)}, u32[]{:S(2)}) collective-permute-start(bf16[4,4,64,128]{3,2,1,0:T(8,128)(2,1)S(1)} %all_to_all.30.own), channel_id=1, source_target_pairs={{32,0},{64,32},{96,64},{128,96},{160,128},{192,160},{224,192},{256... | collective-permute-start | bytes 786440 | tf_op jit(solution)/shard_map/ppermute | solution.py:204
  17.9 4.0 %collective-permute-start = (bf16[4,4,64,128]{3,2,1,0:T(8,128)(2,1)S(1)}, bf16[4,4,64,128]{3,2,1,0:T(8,128)(2,1)S(1)}, u32[]{:S(2)}, u32[]{:S(2)}) collective-permute-start(bf16[4,4,64,128]{3,2,1,0:T(8,128)(2,1)S(1)} %all_to_all.30.own), channel_id=1, source_target_pairs={{0,32},{32,64},{64,96},{96,128},{128,160},{160,192},{192,224},{224... | collective-permute-start | bytes 786440 | tf_op jit(solution)/shard_map/ppermute | solution.py:204
  21.9 1.3 %collective-permute-start.3 = (bf16[1,4,64,128]{3,2,1,0:T(8,128)(2,1)S(1)}, bf16[1,4,64,128]{3,2,1,0:T(8,128)(2,1)S(1)}, u32[]{:S(2)}, u32[]{:S(2)}) collective-permute-start(bf16[1,4,64,128]{3,2,1,0:T(8,128)(2,1)S(1)} %get-tuple-element.20), channel_id=1, source_target_pairs={{64,0},{96,32},{128,64},{160,96},{192,128},{224,160},{256,192},{28... | collective-permute-start | bytes 196616 | tf_op jit(solution)/shard_map/ppermute | solution.py:204
  23.2 4.9 %collective-permute-start.2 = (bf16[1,4,64,128]{3,2,1,0:T(8,128)(2,1)S(1)}, bf16[1,4,64,128]{3,2,1,0:T(8,128)(2,1)S(1)}, u32[]{:S(2)}, u32[]{:S(2)}) collective-permute-start(bf16[1,4,64,128]{3,2,1,0:T(8,128)(2,1)S(1)} %get-tuple-element.21), channel_id=1, source_target_pairs={{0,64},{32,96},{64,128},{96,160},{128,192},{160,224},{192,256},{22... | collective-permute-start | bytes 196616 | tf_op jit(solution)/shard_map/ppermute | solution.py:204
  29.4 0.0 collective-permute-done.1.hi
  29.4 0.0 collective-permute-done.lo
  29.4 3.7 %chebyshev_filter.1 = (bf16[8,4,6,8,128]{4,3,2,1,0:T(8,128)(2,1)S(1)}, f32[2,3,64,128]{3,2,1,0:T(8,128)S(1)}, f32[2,64,128]{2,1,0:T(8,128)S(1)}) custom-call(f32[]{:T(128)S(6)} %copy.19.lowest, f32[]{:T(128)S(6)} %copy.20.highest, bf16[4,4,64,128]{3,2,1,0:T(8,128)(2,1)S(1)} %collective-permute-done.lo, bf16[4,4,64,128]{3,2,1,0:T(8,128)(2,1)S(1)} %all_to_all.30.own, ...), custom_call_target="tpu_custom_call" | custom-call | flops 34406400 | bytes 2752512 | tf_op jit(solution)/shard_map/chebyshev_filter/pallas_call | solution.py:154
  33.1 0.0 collective-permute-done.3.far_hi
  33.1 0.0 collective-permute-done.2.far_lo
  33.1 0.1 outermost_planes.1
  33.2 14.8 %all_to_all.31 = bf16[32,6,8,128]{3,2,1,0:T(8,128)(2,1)S(1)} all-to-all(bf16[32,6,8,128]{3,2,1,0:T(8,128)(2,1)S(1)} %bitcast.16), channel_id=1, replica_groups=mesh['z'=16,'xl'=2,'core'=2,'xh'=2,'y'=4] {'xh','y','xl','core'}, dimensions={0} | all-to-all | bytes 786432 | tf_op jit(solution)/shard_map/all_to_all | solution.py:392
  48.1 0.3 packed_terms.1
  48.4 11.4 %all_to_all.32 = f32[32,4,128]{2,1,0:T(4,128)S(1)} all-to-all(f32[32,4,128]{2,1,0:T(4,128)S(1)} %packed_terms.1), channel_id=1, replica_groups=mesh['z'=16,'xl'=2,'core'=2,'xh'=2,'y'=4] {'xh','y','xl','core'}, dimensions={0} | all-to-all | bytes 131072 | tf_op jit(solution)/shard_map/all_to_all | solution.py:262
  59.9 26.0 %all_to_all.33 = f32[16,4,128]{2,1,0:T(4,128)S(1)} all-to-all(f32[16,4,128]{2,1,0:T(4,128)S(1)} %broadcast_in_dim.6), channel_id=1, replica_groups=mesh['z'=16,'xl'=2,'core'=2,'xh'=2,'y'=4] {'z'}, dimensions={0} | all-to-all | bytes 65536 | tf_op jit(solution)/shard_map/all_to_all | solution.py:209
  85.9 12.4 %all_to_all.34.whole = f32[32,4,128]{2,1,0:T(4,128)S(1)} all-to-all(f32[32,4,128]{2,1,0:T(4,128)S(1)} %broadcast_in_dim.7), channel_id=1, replica_groups=mesh['z'=16,'xl'=2,'core'=2,'xh'=2,'y'=4] {'xh','y','xl','core'}, dimensions={0} | all-to-all | bytes 131072 | tf_op jit(solution)/shard_map/all_to_all | solution.py:264
  98.3 4.1 %projected_and_turned.1 = (f32[96,96]{1,0:T(8,128)}, bf16[8,12,8,128]{3,2,1,0:T(8,128)(2,1)S(1)}) custom-call(f32[32,4,128]{2,1,0:T(4,128)S(1)} %all_to_all.34.whole, bf16[96,1024]{1,0:T(8,128)(2,1)S(1)} %get-tuple-element.23.filtered), custom_call_target="tpu_custom_call" | custom-call | tf_op jit(solution)/shard_map/projected_and_turned/pallas_call | solution.py:354
  102.4 9.9 %all_to_all.35 = bf16[8,12,8,128]{3,2,1,0:T(8,128)(2,1)S(1)} all-to-all(bf16[8,12,8,128]{3,2,1,0:T(8,128)(2,1)S(1)} %get-tuple-element.10), channel_id=1, replica_groups=mesh['z'=16,'xl'=2,'core'=2,'xh'=2,'y'=4] {'xh','y'}, dimensions={0} | all-to-all | bytes 393216 | tf_op jit(solution)/shard_map/all_to_all | solution.py:397
  112.4 0.7 copy_bitcast_fusion.2
  (8 shorter events, 0.2 us)
Async XLA Ops:
  0.6 0.9 copy-start
  1.6 0.8 copy-start.1
  16.6 12.8 %collective-permute-start.1 = (bf16[4,4,64,128]{3,2,1,0:T(8,128)(2,1)S(1)}, bf16[4,4,64,128]{3,2,1,0:T(8,128)(2,1)S(1)}, u32[]{:S(2)}, u32[]{:S(2)}) collective-permute-start(bf16[4,4,64,128]{3,2,1,0:T(8,128)(2,1)S(1)} %all_to_all.30.own), channel_id=1, source_target_pairs={{32,0},{64,32},{96,64},{128,96},{160,128},{192,160},{224,192},{256... | collective-permute-start | bytes 786440 | tf_op jit(solution)/shard_map/ppermute | solution.py:204
  17.9 11.5 %collective-permute-start = (bf16[4,4,64,128]{3,2,1,0:T(8,128)(2,1)S(1)}, bf16[4,4,64,128]{3,2,1,0:T(8,128)(2,1)S(1)}, u32[]{:S(2)}, u32[]{:S(2)}) collective-permute-start(bf16[4,4,64,128]{3,2,1,0:T(8,128)(2,1)S(1)} %all_to_all.30.own), channel_id=1, source_target_pairs={{0,32},{32,64},{64,96},{96,128},{128,160},{160,192},{192,224},{224... | collective-permute-start | bytes 786440 | tf_op jit(solution)/shard_map/ppermute | solution.py:204
  21.9 11.2 %collective-permute-start.3 = (bf16[1,4,64,128]{3,2,1,0:T(8,128)(2,1)S(1)}, bf16[1,4,64,128]{3,2,1,0:T(8,128)(2,1)S(1)}, u32[]{:S(2)}, u32[]{:S(2)}) collective-permute-start(bf16[1,4,64,128]{3,2,1,0:T(8,128)(2,1)S(1)} %get-tuple-element.20), channel_id=1, source_target_pairs={{64,0},{96,32},{128,64},{160,96},{192,128},{224,160},{256,192},{28... | collective-permute-start | bytes 196616 | tf_op jit(solution)/shard_map/ppermute | solution.py:204
  23.2 9.9 %collective-permute-start.2 = (bf16[1,4,64,128]{3,2,1,0:T(8,128)(2,1)S(1)}, bf16[1,4,64,128]{3,2,1,0:T(8,128)(2,1)S(1)}, u32[]{:S(2)}, u32[]{:S(2)}) collective-permute-start(bf16[1,4,64,128]{3,2,1,0:T(8,128)(2,1)S(1)} %get-tuple-element.21), channel_id=1, source_target_pairs={{0,64},{32,96},{64,128},{96,160},{128,192},{160,224},{192,256},{22... | collective-permute-start | bytes 196616 | tf_op jit(solution)/shard_map/ppermute | solution.py:204

commit v12 on v11

--- a/solution.py
+++ b/solution.py
@@ -387,9 +387,9 @@
 
     lowest, highest = filter_low, filter_high
     pair = filtered_and_applied(lowest, highest, far_lo, lo, own, hi, far_hi, blocks)
-    pair = pair.reshape(blocks * group, 2 * local, rows, width)
-
-    pair = lax.all_to_all(pair, LAYER, 0, 0, tiled=True)
+    pair = pair.reshape(blocks * group, 2 * local * rows, width)
+
+    pair = lax.all_to_all(pair, LAYER, 0, 0, tiled=True).reshape(blocks * group, 2 * local, rows, width)
     filtered = pair[:, :local].reshape(modes, rows * width)
     applied = pair[:, local:].reshape(modes, rows * width)
     total = total_over_all(packed_terms(filtered, applied, blocks * group))

time: 114 us -> 114 us (level)
  no operation moved by 1% of the time
where the time goes in v12:
time: 114 us; the launch traced here: 113 us
  blocking collectives  88.8 us (78%)
  starting transfers between devices  11.5 us (10%)
  Pallas kernels  8.22 us (7%)
  local copies, waits for them, and re-layouts  2.52 us (2%)
  between operations  2.05 us (2%)
    all_to_all x1, blocking collectives, summed_over_z(): return jnp.sum(lax.all_to_all(copies, 'z', 0, 0, tiled=True), axis=0)  26 us
    all_to_all x1, blocking collectives, per_device(): lax.all_to_all(pair, LAYER, 0, 0, tiled=True)  14.8 us
    all_to_all x1, blocking collectives, per_device(): lax.all_to_all(packed(initial_block, labels, group), GROUP, 0, 0, tiled=T...  14.3 us
    all_to_all x1, blocking collectives, total_over_all(): lax.all_to_all(jnp.broadcast_to(mine, partial.shape), LAYER, 0, 0, tiled=...  12.4 us
    ppermute x4, starting transfers between devices, shifted(): return lax.ppermute(value, axis, pairs)  11.5 us
    all_to_all x1, blocking collectives, total_over_all(): terms = lax.all_to_all(partial, LAYER, 0, 0, tiled=True)  11.4 us
    all_to_all x1, blocking collectives, per_device(): turned = lax.all_to_all(turned, MODE, 0, 0, tiled=True)  9.93 us
    pallas_call x1, Pallas kernels, projected_and_turned(): pl.pallas_call(functools.partial(turn_kernel, scale), out_shape=(jax.Shap...  4.1 us
  transfers between devices with their start and end apart: 4, of which 0 were waited for; matrix products, arithmetic and copies ran while one was open for 0% of the time, Pallas kernels for 3%

profile of v12, /device:TPU:1, one launch (start us, length us, event | category | flops | bytes accessed | tf_op | source)
XLA Modules:
  0.0 113.1 jit_solution(5256216992170111926)
XLA Ops:
  0.6 0.0 copy-start
  0.6 0.9 copy-done
  1.6 0.0 copy-start.1
  1.6 0.8 copy-done.1
  2.3 14.3 %all_to_all.30.own = bf16[4,4,64,128]{3,2,1,0:T(8,128)(2,1)S(1)} all-to-all(bf16[4,4,64,128]{3,2,1,0:T(8,128)(2,1)S(1)} %pack.1), channel_id=1, replica_groups=mesh['z'=16,'xl'=2,'core'=2,'xh'=2,'y'=4] {'xl','core'}, dimensions={0} | all-to-all | bytes 524288 | tf_op jit(solution)/shard_map/all_to_all | solution.py:383
  16.6 1.3 %collective-permute-start.1 = (bf16[4,4,64,128]{3,2,1,0:T(8,128)(2,1)S(1)}, bf16[4,4,64,128]{3,2,1,0:T(8,128)(2,1)S(1)}, u32[]{:S(2)}, u32[]{:S(2)}) collective-permute-start(bf16[4,4,64,128]{3,2,1,0:T(8,128)(2,1)S(1)} %all_to_all.30.own), channel_id=1, source_target_pairs={{32,0},{64,32},{96,64},{128,96},{160,128},{192,160},{224,192},{256... | collective-permute-start | bytes 786440 | tf_op jit(solution)/shard_map/ppermute | solution.py:204
  17.9 4.0 %collective-permute-start = (bf16[4,4,64,128]{3,2,1,0:T(8,128)(2,1)S(1)}, bf16[4,4,64,128]{3,2,1,0:T(8,128)(2,1)S(1)}, u32[]{:S(2)}, u32[]{:S(2)}) collective-permute-start(bf16[4,4,64,128]{3,2,1,0:T(8,128)(2,1)S(1)} %all_to_all.30.own), channel_id=1, source_target_pairs={{0,32},{32,64},{64,96},{96,128},{128,160},{160,192},{192,224},{224... | collective-permute-start | bytes 786440 | tf_op jit(solution)/shard_map/ppermute | solution.py:204
  21.9 1.3 %collective-permute-start.3 = (bf16[1,4,64,128]{3,2,1,0:T(8,128)(2,1)S(1)}, bf16[1,4,64,128]{3,2,1,0:T(8,128)(2,1)S(1)}, u32[]{:S(2)}, u32[]{:S(2)}) collective-permute-start(bf16[1,4,64,128]{3,2,1,0:T(8,128)(2,1)S(1)} %get-tuple-element.20), channel_id=1, source_target_pairs={{64,0},{96,32},{128,64},{160,96},{192,128},{224,160},{256,192},{28... | collective-permute-start | bytes 196616 | tf_op jit(solution)/shard_map/ppermute | solution.py:204
  23.2 4.9 %collective-permute-start.2 = (bf16[1,4,64,128]{3,2,1,0:T(8,128)(2,1)S(1)}, bf16[1,4,64,128]{3,2,1,0:T(8,128)(2,1)S(1)}, u32[]{:S(2)}, u32[]{:S(2)}) collective-permute-start(bf16[1,4,64,128]{3,2,1,0:T(8,128)(2,1)S(1)} %get-tuple-element.21), channel_id=1, source_target_pairs={{0,64},{32,96},{64,128},{96,160},{128,192},{160,224},{192,256},{22... | collective-permute-start | bytes 196616 | tf_op jit(solution)/shard_map/ppermute | solution.py:204
  29.4 0.0 collective-permute-done.1.hi
  29.4 0.0 collective-permute-done.lo
  29.4 3.7 %chebyshev_filter.1 = (bf16[8,4,6,8,128]{4,3,2,1,0:T(8,128)(2,1)S(1)}, f32[2,3,64,128]{3,2,1,0:T(8,128)S(1)}, f32[2,64,128]{2,1,0:T(8,128)S(1)}) custom-call(f32[]{:T(128)S(6)} %copy.19.lowest, f32[]{:T(128)S(6)} %copy.20.highest, bf16[4,4,64,128]{3,2,1,0:T(8,128)(2,1)S(1)} %collective-permute-done.lo, bf16[4,4,64,128]{3,2,1,0:T(8,128)(2,1)S(1)} %all_to_all.30.own, ...), custom_call_target="tpu_custom_call" | custom-call | flops 34406400 | bytes 2752512 | tf_op jit(solution)/shard_map/chebyshev_filter/pallas_call | solution.py:154
  33.1 0.0 collective-permute-done.3.far_hi
  33.1 0.0 collective-permute-done.2.far_lo
  33.1 0.1 outermost_planes.1
  33.2 14.8 %all_to_all.31 = bf16[32,48,128]{2,1,0:T(8,128)(2,1)S(1)} all-to-all(bf16[32,48,128]{2,1,0:T(8,128)(2,1)S(1)} %bitcast.17), channel_id=1, replica_groups=mesh['z'=16,'xl'=2,'core'=2,'xh'=2,'y'=4] {'xh','y','xl','core'}, dimensions={0} | all-to-all | bytes 786432 | tf_op jit(solution)/shard_map/all_to_all | solution.py:392
  48.1 0.3 packed_terms.1
  48.4 11.4 %all_to_all.32 = f32[32,4,128]{2,1,0:T(4,128)S(1)} all-to-all(f32[32,4,128]{2,1,0:T(4,128)S(1)} %packed_terms.1), channel_id=1, replica_groups=mesh['z'=16,'xl'=2,'core'=2,'xh'=2,'y'=4] {'xh','y','xl','core'}, dimensions={0} | all-to-all | bytes 131072 | tf_op jit(solution)/shard_map/all_to_all | solution.py:262
  59.9 26.0 %all_to_all.33 = f32[16,4,128]{2,1,0:T(4,128)S(1)} all-to-all(f32[16,4,128]{2,1,0:T(4,128)S(1)} %broadcast_in_dim.6), channel_id=1, replica_groups=mesh['z'=16,'xl'=2,'core'=2,'xh'=2,'y'=4] {'z'}, dimensions={0} | all-to-all | bytes 65536 | tf_op jit(solution)/shard_map/all_to_all | solution.py:209
  85.9 12.4 %all_to_all.34.whole = f32[32,4,128]{2,1,0:T(4,128)S(1)} all-to-all(f32[32,4,128]{2,1,0:T(4,128)S(1)} %broadcast_in_dim.7), channel_id=1, replica_groups=mesh['z'=16,'xl'=2,'core'=2,'xh'=2,'y'=4] {'xh','y','xl','core'}, dimensions={0} | all-to-all | bytes 131072 | tf_op jit(solution)/shard_map/all_to_all | solution.py:264
  98.3 4.1 %projected_and_turned.1 = (f32[96,96]{1,0:T(8,128)}, bf16[8,12,8,128]{3,2,1,0:T(8,128)(2,1)S(1)}) custom-call(f32[32,4,128]{2,1,0:T(4,128)S(1)} %all_to_all.34.whole, bf16[96,1024]{1,0:T(8,128)(2,1)S(1)} %get-tuple-element.23.filtered), custom_call_target="tpu_custom_call" | custom-call | tf_op jit(solution)/shard_map/projected_and_turned/pallas_call | solution.py:354
  102.4 9.9 %all_to_all.35 = bf16[8,12,8,128]{3,2,1,0:T(8,128)(2,1)S(1)} all-to-all(bf16[8,12,8,128]{3,2,1,0:T(8,128)(2,1)S(1)} %get-tuple-element.10), channel_id=1, replica_groups=mesh['z'=16,'xl'=2,'core'=2,'xh'=2,'y'=4] {'xh','y'}, dimensions={0} | all-to-all | bytes 393216 | tf_op jit(solution)/shard_map/all_to_all | solution.py:397
  112.4 0.7 copy_bitcast_fusion.2
  (8 shorter events, 0.2 us)
Async XLA Ops:
  0.6 0.9 copy-start
  1.6 0.8 copy-start.1
  16.6 12.8 %collective-permute-start.1 = (bf16[4,4,64,128]{3,2,1,0:T(8,128)(2,1)S(1)}, bf16[4,4,64,128]{3,2,1,0:T(8,128)(2,1)S(1)}, u32[]{:S(2)}, u32[]{:S(2)}) collective-permute-start(bf16[4,4,64,128]{3,2,1,0:T(8,128)(2,1)S(1)} %all_to_all.30.own), channel_id=1, source_target_pairs={{32,0},{64,32},{96,64},{128,96},{160,128},{192,160},{224,192},{256... | collective-permute-start | bytes 786440 | tf_op jit(solution)/shard_map/ppermute | solution.py:204
  17.9 11.5 %collective-permute-start = (bf16[4,4,64,128]{3,2,1,0:T(8,128)(2,1)S(1)}, bf16[4,4,64,128]{3,2,1,0:T(8,128)(2,1)S(1)}, u32[]{:S(2)}, u32[]{:S(2)}) collective-permute-start(bf16[4,4,64,128]{3,2,1,0:T(8,128)(2,1)S(1)} %all_to_all.30.own), channel_id=1, source_target_pairs={{0,32},{32,64},{64,96},{96,128},{128,160},{160,192},{192,224},{224... | collective-permute-start | bytes 786440 | tf_op jit(solution)/shard_map/ppermute | solution.py:204
  21.9 11.2 %collective-permute-start.3 = (bf16[1,4,64,128]{3,2,1,0:T(8,128)(2,1)S(1)}, bf16[1,4,64,128]{3,2,1,0:T(8,128)(2,1)S(1)}, u32[]{:S(2)}, u32[]{:S(2)}) collective-permute-start(bf16[1,4,64,128]{3,2,1,0:T(8,128)(2,1)S(1)} %get-tuple-element.20), channel_id=1, source_target_pairs={{64,0},{96,32},{128,64},{160,96},{192,128},{224,160},{256,192},{28... | collective-permute-start | bytes 196616 | tf_op jit(solution)/shard_map/ppermute | solution.py:204
  23.2 9.9 %collective-permute-start.2 = (bf16[1,4,64,128]{3,2,1,0:T(8,128)(2,1)S(1)}, bf16[1,4,64,128]{3,2,1,0:T(8,128)(2,1)S(1)}, u32[]{:S(2)}, u32[]{:S(2)}) collective-permute-start(bf16[1,4,64,128]{3,2,1,0:T(8,128)(2,1)S(1)} %get-tuple-element.21), channel_id=1, source_target_pairs={{0,64},{32,96},{64,128},{96,160},{128,192},{160,224},{192,256},{22... | collective-permute-start | bytes 196616 | tf_op jit(solution)/shard_map/ppermute | solution.py:204
